TPU v7x, 256 devices: a whole 4x4x8 slice. The times are simulated.
256 devices in a mesh: section: 4 (over x), dp: 8 (over y, z_lo), tensor: 8 (over z_hi, core).
Axes of the slice: x: 4, y: 4, z: 8 (z_hi: 4, z_lo: 2; z = z_hi * 2 + z_lo), core: 2. Of those that a mesh axis runs over, the one named last changes fastest.
Arguments:
- activations: bfloat16 [4, 256, 4096], P('section', ('dp', 'tensor')), may hold values from -6 to 6
- w_gate: bfloat16 [4, 4096, 16384], P('section', None, ('dp', 'tensor')), may hold values from -0.09375 to 0.09375
- w_up: bfloat16 [4, 4096, 16384], P('section', None, ('dp', 'tensor')), may hold values from -0.09375 to 0.09375
- w_down: bfloat16 [4, 16384, 4096], P('section', ('dp', 'tensor')), may hold values from -0.046875 to 0.046875
- out_grad: bfloat16 [4, 256, 4096], P('section', ('dp', 'tensor')), may hold values from -6 to 6
Outputs:
- output: bfloat16 [4, 256, 4096], P('section', ('dp', 'tensor'))
- input_grad: bfloat16 [4, 256, 4096], P('section', ('dp', 'tensor'))
- grad_gate: bfloat16 [4, 4096, 16384], P('section', None, ('dp', 'tensor'))
- grad_up: bfloat16 [4, 4096, 16384], P('section', None, ('dp', 'tensor'))
- grad_down: bfloat16 [4, 16384, 4096], P('section', ('dp', 'tensor'))
All inputs are finite; a program needn't handle non-finite values.
Results may differ from a plain program's by a relative error of at most 0.006.
Values may be sent and summed in bfloat16 or wider, within the bound.
No kernel may reach another device: no remote copies, remote signals or barrier semaphores. Data moves between devices by JAX's collectives and lax.ppermute only.
A program may use at most 128 MiB of HBM per device.

v0:
```python
import jax
import jax.numpy as jnp
from jax import lax
from jax.sharding import PartitionSpec as P


def from_behind(x, axis, by):
    length = lax.axis_size(axis)
    return lax.ppermute(x, axis, [(i, (i + by) % length) for i in range(length)])


def swish_parts(gate):
    sigma = jax.nn.sigmoid(gate)
    return (gate * sigma, sigma * (1.0 + gate * (1.0 - sigma)))


def collect(shard_rows):
    return lax.all_gather(shard_rows, ("dp", "tensor"), axis=0, tiled=True)


def reduce_rows(term_fn, shard_count):
    return lax.psum_scatter(
        term_fn(jnp.int32(0), shard_count * lax.axis_size(("dp", "tensor"))),
        ("dp", "tensor"),
        scatter_dimension=0,
        tiled=True,
    )


def contract_rows(left, right):
    return lax.dot_general(
        left, right, (((0,), (0,)), ((), ())), preferred_element_type=jnp.float32
    )


def contract_cols(left, right):
    return lax.dot_general(
        left, right, (((1,), (1,)), ((), ())), preferred_element_type=jnp.float32
    )


def on_device(activations, w_gate, w_up, w_down, out_grad):
    own_rows = activations[0]
    shard_count = own_rows.shape[0]
    gate_weight = w_gate[0]
    up_weight = w_up[0]
    down_weight = w_down[0]
    arrived = from_behind(own_rows, "section", 1)
    layer_in = collect(arrived)
    gate = jnp.dot(layer_in, gate_weight, preferred_element_type=jnp.float32)
    upper = jnp.dot(layer_in, up_weight, preferred_element_type=jnp.float32)
    swish, slope = swish_parts(gate)
    hidden = (swish * upper).astype(jnp.bfloat16)

    def forward_term(first_row, row_count):
        return jnp.dot(hidden, down_weight, preferred_element_type=jnp.float32)

    output_rows = reduce_rows(forward_term, shard_count).astype(jnp.bfloat16)
    cotangent = collect(out_grad[0])
    hidden_grad = contract_cols(cotangent, down_weight)
    grad_down = contract_rows(hidden, cotangent).astype(jnp.bfloat16)
    gate_grad = (hidden_grad * upper * slope).astype(jnp.bfloat16)
    up_grad = (hidden_grad * swish).astype(jnp.bfloat16)
    grad_gate = contract_rows(layer_in, gate_grad).astype(jnp.bfloat16)
    grad_up = contract_rows(layer_in, up_grad).astype(jnp.bfloat16)

    def backward_term(first_row, row_count):
        return contract_cols(gate_grad, gate_weight) + contract_cols(up_grad, up_weight)

    back_rows = reduce_rows(backward_term, shard_count).astype(jnp.bfloat16)
    returned = from_behind(back_rows, "section", -1)
    return (output_rows[None], returned[None], grad_gate[None], grad_up[None], grad_down[None])


def solution(mesh):
    return jax.shard_map(
        on_device,
        mesh=mesh,
        in_specs=(
            P("section", ("dp", "tensor"), None),
            P("section", None, ("dp", "tensor")),
            P("section", None, ("dp", "tensor")),
            P("section", ("dp", "tensor"), None),
            P("section", ("dp", "tensor"), None),
        ),
        out_specs=(
            P("section", ("dp", "tensor"), None),
            P("section", ("dp", "tensor"), None),
            P("section", None, ("dp", "tensor")),
            P("section", None, ("dp", "tensor")),
            P("section", ("dp", "tensor"), None),
        ),
        check_vma=False,
    )
```

profile of v0, /device:TPU:6, one launch (start us, length us, event | category | flops | bytes accessed | tf_op | source)
XLA Modules:
  0.0 616.8 jit_solution(5814710247110026739)
XLA Ops:
  7.2 1.6 copy.15
  8.9 2.3 collective-permute-start
  11.2 1.9 collective-permute-done
  13.1 0.6 copy-done.5
  13.7 1.3 dynamic-slice
  15.6 114.0 %all-gather.5.cloned.1.call-done = bf16[1,256,4096]{2,0,1:T(2,128)(2,1)} async-done(((bf16[1,4,4096]{2,0,1:T(2,128)(2,1)}), bf16[1,256,4096]{2,0,1:T(2,128)(2,1)}) %all-gather.5.cloned.1.call-update) | async-done | bytes 2097168 | tf_op jit(solution)/shard_map/all_gather | solution.py:18
  129.6 5.4 fusion.4
  135.0 109.2 %all-gather.7.cloned.1.call-done = bf16[64,4,4096]{2,1,0:T(4,128)(2,1)} async-done(((bf16[1,4,4096]{2,1,0:T(4,128)(2,1)}), bf16[64,4,4096]{2,1,0:T(4,128)(2,1)}) %all-gather.7.cloned.1.call-update) | async-done | bytes 2097168 | tf_op jit(solution)/shard_map/all_gather | solution.py:18
  244.2 3.9 reshape.12
  248.2 3.1 fusion.10
  251.3 0.8 multiply_convert_fusion
  252.1 2.1 fusion.1
  254.2 0.7 fusion.12
  254.9 0.8 copy-done.3
  255.8 2.7 convolution_add_fusion
  258.5 2.7 fusion.7
  261.2 329.0 %all-reduce.4 = (bf16[256,4096]{1,0:T(8,128)(2,1)}, bf16[256,4096]{1,0:T(8,128)(2,1)}) all-reduce(f32[256,4096]{1,0:T(8,128)} %fusion.7, f32[256,4096]{1,0:T(8,128)} %convolution_add_fusion), channel_id=3, replica_groups=mesh['section'=4,'dp'=8,'tensor'=8] {'dp','tensor'}, use_global_device_ids=true, to_apply=%region_0.0.clone | all-reduce | flops 2097152 | bytes 12582912
  590.2 1.5 fusion.19
  591.7 0.9 dynamic-slice_convert_fusion
  592.8 6.3 %fusion.2 = bf16[1,256,4096]{2,1,0:T(8,128)(2,1)} fusion(bf16[256,256]{1,0:T(8,128)(2,1)S(1)} %get-tuple-element.24, bf16[1,256,4096]{2,0,1:T(2,128)(2,1)} %all-gather.5.cloned.1.call-done), kind=kOutput, calls=%fused_computation.6 | convolution fusion | flops 537919488 | bytes 4325376 | tf_op jit(solution)/shard_map/dot_general | solution.py:31
  599.1 2.1 fusion
  601.2 4.1 copy.16
  605.2 4.1 copy.17
  609.3 0.6 copy.32
  (16 shorter events, 0.4 us)
Async XLA Ops:
  7.2 244.1 %copy-start = (bf16[1,4096,256]{2,1,0:T(8,128)(2,1)S(1)}, bf16[1,4096,256]{2,1,0:T(8,128)(2,1)}, u32[]{:S(2)}) copy-start(bf16[1,4096,256]{2,1,0:T(8,128)(2,1)} %param.6) | copy-start | bytes 6291460
  7.2 122.4 %all-gather.5.cloned.1.call-start = ((), (), s32[]{:S(2)}) async-start(), calls=%async_computation | async-start | bytes 4259840 | tf_op jit(solution)/shard_map/all_gather | solution.py:18
  8.8 235.4 %all-gather.7.cloned.1.call-start = ((), (), s32[]{:S(2)}) async-start(), calls=%async_computation.1 | async-start | bytes 2129920 | tf_op jit(solution)/shard_map/all_gather | solution.py:18
  8.9 4.2 collective-permute-start
  13.1 0.6 copy-start.5
  248.2 3.1 copy-start.1
  254.2 1.6 copy-start.3
  255.8 2.7 copy-start.4
  592.5 6.6 %copy-start.2 = (bf16[256,4096]{1,0:T(8,128)(2,1)S(1)}, bf16[256,4096]{1,0:T(8,128)(2,1)}, u32[]{:S(2)}) copy-start(bf16[256,4096]{1,0:T(8,128)(2,1)} %reshape.12) | copy-start | bytes 6291460
  592.5 16.8 %collective-permute-start.1 = (bf16[4,4096]{1,0:T(4,128)(2,1)S(1)}, bf16[4,4096]{1,0:T(4,128)(2,1)S(1)}, u32[]{:S(2)}, u32[]{:S(2)}) collective-permute-start(bf16[4,4096]{1,0:T(4,128)(2,1)S(1)} %dynamic-slice_convert_fusion), channel_id=1, source_target_pairs={{0,192},{64,0},{128,64},{192,128},{1,193},{65,1},{129,65},{193,129... | collective-permute-start | bytes 98312 | tf_op jit(solution)/shard_map/ppermute | solution.py:9
Sparse Core Ops, SparseCore 0:
  10.4 119.1 all-gather.4
  132.0 112.1 all-gather.6
where the time goes:
time: 618 us; the launch traced here: 617 us
  blocking collectives  329 us (53%)
  waiting for transfers between devices  225 us (36%)
  matrix products  25.9 us (4%)
  local copies, waits for them, and re-layouts  19.4 us (3%)
  between operations  14.8 us (2%)
    unnamed x1, blocking collectives  329 us
    all_gather x2, waiting for transfers between devices, collect(): return lax.all_gather(shard_rows, ('dp', 'tensor'), axis=0, tiled=True)  223 us
    unnamed x18, local copies, waits for them, and re-layouts  17 us
  transfers between devices with their start and end apart: 4, of which 3 were waited for; matrix products, arithmetic and copies ran while one was open for 4% of the time, Pallas kernels for 0%

commit v1 on v0

v1 whole, which is shorter than its diff:
```python
import jax
import jax.numpy as jnp
from jax import lax
from jax.sharding import PartitionSpec as P

PLANE = ("dp", "tensor")
NY, NZ = 4, 8
BF16 = jnp.bfloat16
F32 = jnp.float32


def place(y, z, core):
    y, z = y % NY, z % NZ
    return ((y * 2 + z % 2) * 4 + z // 2) * 2 + core


CHIPS = [(y, z) for y in range(NY) for z in range(NZ)]
CORE_SWAP = [(place(y, z, c), place(y, z, 1 - c)) for y, z in CHIPS for c in (0, 1)]
Y_STEP = [(place(y, z, c), place(y + 1 - 2 * c, z, c)) for y, z in CHIPS for c in (0, 1)]
Z_STEP = [(place(y, z, c), place(y, z + 1 - 2 * c, c)) for y, z in CHIPS for c in (0, 1)]
COLOURS = [[place(k - 2 * z, z, c) for z in range(NZ)] for k in range(NY) for c in (0, 1)]


def swap(x):
    return lax.ppermute(x, PLANE, CORE_SWAP)


def y_step(x):
    return lax.ppermute(x, PLANE, Y_STEP)


def z_step(x):
    return lax.ppermute(x, PLANE, Z_STEP)


def colour_all_to_all(x):
    return lax.all_to_all(x, PLANE, 0, 0, axis_index_groups=COLOURS)


def from_behind(x, axis, by):
    length = lax.axis_size(axis)
    return lax.ppermute(x, axis, [(i, (i + by) % length) for i in range(length)])


def swish_parts(gate):
    sigma = jax.nn.sigmoid(gate)
    return (gate * sigma, sigma * (1.0 + gate * (1.0 - sigma)))


def spread(own):
    other = swap(own)
    opposite = z_step(own)
    direct = y_step(jnp.concatenate([own, other], 0))
    return jnp.concatenate([own, other, direct, swap(direct), opposite, swap(opposite)], 0)


def fold(part):
    own, other, direct, crossed, opposite, opposite_other = (
        part[:32], part[32:64], part[64:128], part[128:192], part[192:224], part[224:])
    got = swap(jnp.concatenate([other, direct, opposite_other], 0).astype(BF16)).astype(F32)
    own = own + got[:32]
    crossed = y_step((crossed + got[32:96]).astype(BF16))
    opposite = z_step((opposite + got[96:]).astype(BF16))
    return own + crossed[32:].astype(F32) + swap(crossed[:32]).astype(F32) + opposite.astype(F32)


def contract_rows(left, right):
    return lax.dot_general(left, right, (((0,), (0,)), ((), ())), preferred_element_type=F32)


def contract_cols(left, right):
    return lax.dot_general(left, right, (((1,), (1,)), ((), ())), preferred_element_type=F32)


def on_device(activations, w_gate, w_up, w_down, out_grad):
    gate_weight, up_weight, down_weight = w_gate[0], w_up[0], w_down[0]
    arrived = from_behind(activations[0], "section", 1)
    rows, width = arrived.shape
    mine = jnp.stack([arrived, out_grad[0]])
    got = colour_all_to_all(jnp.broadcast_to(mine[None], (NZ,) + mine.shape))
    layer_in = spread(got[:, 0].reshape(NZ * rows, width))
    cotangent = spread(got[:, 1].reshape(NZ * rows, width))

    gate = jnp.dot(layer_in, gate_weight, preferred_element_type=F32)
    upper = jnp.dot(layer_in, up_weight, preferred_element_type=F32)
    swish, slope = swish_parts(gate)
    hidden = (swish * upper).astype(BF16)
    out_sums = fold(jnp.dot(hidden, down_weight, preferred_element_type=F32))

    hidden_grad = contract_cols(cotangent, down_weight)
    gate_grad = (hidden_grad * upper * slope).astype(BF16)
    up_grad = (hidden_grad * swish).astype(BF16)
    back_sums = fold(contract_cols(gate_grad, gate_weight) + contract_cols(up_grad, up_weight))

    grad_down = contract_rows(hidden, cotangent).astype(BF16)
    grad_gate = contract_rows(layer_in, gate_grad).astype(BF16)
    grad_up = contract_rows(layer_in, up_grad).astype(BF16)

    sums = jnp.stack([out_sums.reshape(NZ, rows, width), back_sums.reshape(NZ, rows, width)], 1)
    final = jnp.sum(colour_all_to_all(sums.astype(BF16)).astype(F32), 0).astype(BF16)
    returned = from_behind(final[1], "section", -1)
    return (final[0][None], returned[None], grad_gate[None], grad_up[None], grad_down[None])


def solution(mesh):
    return jax.shard_map(
        on_device,
        mesh=mesh,
        in_specs=(
            P("section", PLANE, None),
            P("section", None, PLANE),
            P("section", None, PLANE),
            P("section", PLANE, None),
            P("section", PLANE, None),
        ),
        out_specs=(
            P("section", PLANE, None),
            P("section", PLANE, None),
            P("section", None, PLANE),
            P("section", None, PLANE),
            P("section", PLANE, None),
        ),
        check_vma=False,
    )
```

time: 618 us -> 114 us (0.18)
  blocking collectives: 329 us -> 26.8 us
  waiting for transfers between devices: 225 us -> 46.5 us
  between operations: 14.8 us -> 1.14 us
  local copies, waits for them, and re-layouts: 19.4 us -> 6.14 us
  matrix products: 25.9 us -> 13.9 us
  starting transfers between devices: 2.63 us -> 13.6 us
    unnamed x1 -> x0, blocking collectives: 329 us -> none
    all_gather x2 -> x0, waiting for transfers between devices: 223 us -> none  [collect(): return lax.all_gather(shard_rows, ('dp', 'tensor'), axis=0, tiled=True)]
    ppermute x0 -> x18, waiting for transfers between devices: none -> 31.9 us  [the longest x4 21.6 us: y_step(): return lax.ppermute(x, PLANE, Y_STEP)]
    all_to_all x0 -> x1, blocking collectives: none -> 26.8 us  [colour_all_to_all(): return lax.all_to_all(x, PLANE, 0, 0, axis_index_groups=COLOURS)]
    unnamed x18 -> x37, local copies, waits for them, and re-layouts: 17 us -> 3.85 us
    all_to_all x0 -> x1, waiting for transfers between devices: none -> 12 us  [colour_all_to_all(): return lax.all_to_all(x, PLANE, 0, 0, axis_index_groups=COLOURS)]
    ppermute x0 -> x18, starting transfers between devices: none -> 7 us  [the longest x4 3.92 us: z_step(): return lax.ppermute(x, PLANE, Z_STEP)]
    dot_general x3, matrix products: 8.86 us -> 2.22 us  [contract_cols(): lax.dot_general(left, right, (((1,), (1,)), ((), ())), preferred_element_...]
  transfers between devices with their start and end apart: 4 -> 21, of which waited for: 3 -> 14; matrix products, arithmetic and copies ran while one was open for 4% -> 13% of each run, Pallas kernels for 0% -> 0%
where the time goes in v1:
time: 114 us; the launch traced here: 113 us
  waiting for transfers between devices  46.5 us (41%)
  blocking collectives  26.8 us (24%)
  matrix products  13.9 us (12%)
  starting transfers between devices  13.6 us (12%)
  local copies, waits for them, and re-layouts  6.14 us (5%)
  other arithmetic  4.72 us (4%)
    all_to_all x1, blocking collectives, colour_all_to_all(): return lax.all_to_all(x, PLANE, 0, 0, axis_index_groups=COLOURS)  26.8 us
    ppermute x4, waiting for transfers between devices, y_step(): return lax.ppermute(x, PLANE, Y_STEP)  21.6 us
    all_to_all x1, waiting for transfers between devices, colour_all_to_all(): return lax.all_to_all(x, PLANE, 0, 0, axis_index_groups=COLOURS)  12 us
    dot_general x3, matrix products, contract_rows(): lax.dot_general(left, right, (((0,), (0,)), ((), ())), preferred_element_...  9.56 us
    ppermute x4, waiting for transfers between devices, z_step(): return lax.ppermute(x, PLANE, Z_STEP)  7.1 us
    ppermute x4, starting transfers between devices, z_step(): return lax.ppermute(x, PLANE, Z_STEP)  3.92 us
    unnamed x37, local copies, waits for them, and re-layouts  3.85 us
    all_to_all x1, starting transfers between devices, colour_all_to_all(): return lax.all_to_all(x, PLANE, 0, 0, axis_index_groups=COLOURS)  3.49 us
  transfers between devices with their start and end apart: 21, of which 14 were waited for; matrix products, arithmetic and copies ran while one was open for 13% of the time, Pallas kernels for 0%

profile of v1, /device:TPU:6, one launch (start us, length us, event | category | flops | bytes accessed | tf_op | source)
XLA Modules:
  0.0 112.9 jit_solution(16598214877226834721)
XLA Ops:
  0.6 2.3 %collective-permute-start = (bf16[4,4096]{1,0:T(4,128)(2,1)}, bf16[4,4096]{1,0:T(4,128)(2,1)S(1)}, u32[]{:S(2)}, u32[]{:S(2)}) collective-permute-start(bf16[4,4096]{1,0:T(4,128)(2,1)} %bitcast.50), channel_id=1, source_target_pairs={{0,64},{64,128},{128,192},{192,0},{1,65},{65,129},{129,193},{193,1... | collective-permute-start | bytes 98312 | tf_op jit(solution)/shard_map/ppermute | solution.py:42
  2.9 1.9 %collective-permute-done = bf16[4,4096]{1,0:T(4,128)(2,1)S(1)} collective-permute-done((bf16[4,4096]{1,0:T(4,128)(2,1)}, bf16[4,4096]{1,0:T(4,128)(2,1)S(1)}, u32[]{:S(2)}, u32[]{:S(2)}) %collective-permute-start) | collective-permute-done | bytes 32800 | tf_op jit(solution)/shard_map/ppermute | solution.py:42
  4.9 0.8 pad_maximum_fusion.5
  5.9 26.8 %all_to_all.10 = bf16[8,2,4,4096]{3,2,1,0:T(4,128)(2,1)S(1)} all-to-all(bf16[8,2,4,4096]{3,2,1,0:T(4,128)(2,1)S(1)} %broadcast_in_dim.18), channel_id=1, replica_groups={{0,40,2,42,4,44,6,46},{1,41,3,43,5,45,7,47},{16,56,18,58,20,60,22,62},{..., dimensions={0} | all-to-all | bytes 1048576 | tf_op jit(solution)/shard_map/all_to_all | solution.py:37
  33.8 0.9 collective-permute-start.4
  34.9 1.6 %collective-permute-start.13 = (bf16[32,4096]{1,0:T(8,128)(2,1)S(1)}, bf16[32,4096]{1,0:T(8,128)(2,1)S(1)}, u32[]{:S(2)}, u32[]{:S(2)}) collective-permute-start(bf16[32,4096]{1,0:T(8,128)(2,1)S(1)} %reshape_squeeze.7), channel_id=1, source_target_pairs={{0,8},{1,15},{8,2},{9,1},{2,10},{3,9},{10,4},{11,3},{4,12},{5,11},... | collective-permute-start | bytes 786440 | tf_op jit(solution)/shard_map/ppermute | solution.py:33
  37.4 1.0 collective-permute-start.11
  38.4 3.0 %collective-permute-done.4 = bf16[32,4096]{1,0:T(8,128)(2,1)S(1)} collective-permute-done((bf16[32,4096]{1,0:T(8,128)(2,1)S(1)}, bf16[32,4096]{1,0:T(8,128)(2,1)S(1)}, u32[]{:S(2)}, u32[]{:S(2)}) %collective-permute-start.4) | collective-permute-done | bytes 262176 | tf_op jit(solution)/shard_map/ppermute | solution.py:33
  41.4 2.8 %collective-permute-done.13 = bf16[32,4096]{1,0:T(8,128)(2,1)S(1)} collective-permute-done((bf16[32,4096]{1,0:T(8,128)(2,1)S(1)}, bf16[32,4096]{1,0:T(8,128)(2,1)S(1)}, u32[]{:S(2)}, u32[]{:S(2)}) %collective-permute-start.13) | collective-permute-done | bytes 262176 | tf_op jit(solution)/shard_map/ppermute | solution.py:33
  44.1 2.9 %collective-permute-done.2 = bf16[64,4096]{1,0:T(8,128)(2,1)S(1)} collective-permute-done((bf16[64,4096]{1,0:T(8,128)(2,1)S(1)}, bf16[64,4096]{1,0:T(8,128)(2,1)S(1)}, u32[]{:S(2)}, u32[]{:S(2)}) %collective-permute-start.2) | collective-permute-done | bytes 524320 | tf_op jit(solution)/shard_map/ppermute | solution.py:29
  47.1 5.6 %collective-permute-done.11 = bf16[64,4096]{1,0:T(8,128)(2,1)S(1)} collective-permute-done((bf16[64,4096]{1,0:T(8,128)(2,1)S(1)}, bf16[64,4096]{1,0:T(8,128)(2,1)S(1)}, u32[]{:S(2)}, u32[]{:S(2)}) %collective-permute-start.11) | collective-permute-done | bytes 524320 | tf_op jit(solution)/shard_map/ppermute | solution.py:29
  52.8 1.8 %collective-permute-done.12 = bf16[64,4096]{1,0:T(8,128)(2,1)S(1)} collective-permute-done((bf16[64,4096]{1,0:T(8,128)(2,1)S(1)}, bf16[64,4096]{1,0:T(8,128)(2,1)S(1)}, u32[]{:S(2)}, u32[]{:S(2)}) %collective-permute-start.12) | collective-permute-done | bytes 524320 | tf_op jit(solution)/shard_map/ppermute | solution.py:25
  55.4 1.6 %copy-done.5 = bf16[1,256,4096]{2,1,0:T(8,128)(2,1)S(1)} copy-done((bf16[1,256,4096]{2,1,0:T(8,128)(2,1)S(1)}, bf16[1,256,4096]{2,1,0:T(8,128)(2,1)}, u32[]{:S(2)}) %copy-start.5) | copy-done | bytes 2097176
  65.3 8.5 %collective-permute-done.7 = bf16[64,4096]{1,0:T(8,128)(2,1)S(1)} collective-permute-done((bf16[64,4096]{1,0:T(8,128)(2,1)S(1)}, bf16[64,4096]{1,0:T(8,128)(2,1)S(1)}, u32[]{:S(2)}, u32[]{:S(2)}) %collective-permute-start.7) | collective-permute-done | bytes 524320 | tf_op jit(solution)/shard_map/ppermute | solution.py:29
  74.7 4.7 %collective-permute-done.16 = bf16[64,4096]{1,0:T(8,128)(2,1)S(1)} collective-permute-done((bf16[64,4096]{1,0:T(8,128)(2,1)S(1)}, bf16[64,4096]{1,0:T(8,128)(2,1)S(1)}, u32[]{:S(2)}, u32[]{:S(2)}) %collective-permute-start.16) | collective-permute-done | bytes 524320 | tf_op jit(solution)/shard_map/ppermute | solution.py:29
  80.4 1.4 %collective-permute-done.18 = bf16[32,4096]{1,0:T(8,128)(2,1)} collective-permute-done((bf16[32,4096]{1,0:T(8,128)(2,1)S(1)}, bf16[32,4096]{1,0:T(8,128)(2,1)}, u32[]{:S(2)}, u32[]{:S(2)}) %collective-permute-start.18) | collective-permute-done | bytes 262176 | tf_op jit(solution)/shard_map/ppermute | solution.py:33
  82.0 1.5 %fusion.20 = bf16[32,4096]{1,0:T(8,128)(2,1)S(1)} fusion(f32[128,4096]{1,0:T(8,128)} %copy-done.4, f32[256,4096]{1,0:T(8,128)} %copy-done.2, bf16[32,4096]{1,0:T(8,128)(2,1)} %collective-permute-done.18, bf16[32,4096]{1,0:T(8,128)(2,1)} %collective-permute-done.17, bf16[64,4096]{1,0:T(8,128)(2,1)S(1)} %collective-permute-done.16), kind=kLoop, calls=%fused_computation.30 | loop fusion | flops 1048576 | bytes 2097152 | tf_op jit(solution)/shard_map/convert.3
  83.6 1.1 %pad_maximum_fusion.4 = bf16[8,2,4,4096]{3,2,1,0:T(4,128)(2,1)} fusion(bf16[8,1,4,4096]{3,2,1,0:T(4,128)(2,1)S(1)} %bitcast.47, bf16[8,1,4,4096]{3,2,1,0:T(4,128)(2,1)S(1)} %bitcast.46), kind=kLoop, calls=%fused_computation.40 | loop fusion | flops 262144 | bytes 1048576 | tf_op jit(solution)/shard_map/stack | solution.py:99
  84.7 3.5 %all-to-all-start.1 = ((bf16[8,2,4,4096]{3,2,1,0:T(4,128)(2,1)}), bf16[8,2,4,4096]{3,2,1,0:T(4,128)(2,1)S(1)}, u32[]{:S(2)}, u32[]{:S(2)}) async-start(bf16[8,2,4,4096]{3,2,1,0:T(4,128)(2,1)} %pad_maximum_fusion.4), calls=%async_computation.1 | async-start | bytes 1048576 | tf_op jit(solution)/shard_map/all_to_all | solution.py:37
  88.3 3.8 %fusion = bf16[1,4096,256]{2,1,0:T(8,128)(2,1)} fusion(bf16[256,4096]{1,0:T(8,128)(2,1)} %copy-done.7, bf16[256,256]{1,0:T(8,128)(2,1)S(1)} %copy-done.12), kind=kOutput, calls=%fused_computation.4 | convolution fusion | flops 537919488 | bytes 4325376 | tf_op jit(solution)/shard_map/dot_general | solution.py:68
  92.1 2.1 %fusion.1 = bf16[1,4096,256]{2,1,0:T(8,128)(2,1)} fusion(bf16[256,4096]{1,0:T(8,128)(2,1)S(1)} %copy-done.8, bf16[256,256]{1,0:T(8,128)(2,1)S(1)} %copy-done.10), kind=kOutput, calls=%fused_computation.5 | convolution fusion | flops 537919488 | bytes 4325376 | tf_op jit(solution)/shard_map/dot_general | solution.py:68
  94.2 12.0 %all-to-all-done.1 = bf16[8,2,4,4096]{3,2,1,0:T(4,128)(2,1)S(1)} async-done(((bf16[8,2,4,4096]{3,2,1,0:T(4,128)(2,1)}), bf16[8,2,4,4096]{3,2,1,0:T(4,128)(2,1)S(1)}, u32[]{:S(2)}, u32[]{:S(2)}) %all-to-all-start.1) | async-done | bytes 524320 | tf_op jit(solution)/shard_map/all_to_all | solution.py:37
  107.1 0.8 collective-permute-start.19
  108.0 3.6 %fusion.2 = bf16[1,256,4096]{2,1,0:T(8,128)(2,1)} fusion(bf16[256,256]{1,0:T(8,128)(2,1)S(1)} %get-tuple-element.5, bf16[256,4096]{1,0:T(8,128)(2,1)} %copy-done.1), kind=kOutput, calls=%fused_computation.6 | convolution fusion | flops 537919488 | bytes 4325376 | tf_op jit(solution)/shard_map/dot_general | solution.py:68
  (95 shorter events, 15.7 us)
Async XLA Ops:
  0.6 57.8 %copy-start = (bf16[1,4096,256]{2,1,0:T(8,128)(2,1)S(1)}, bf16[1,4096,256]{2,1,0:T(8,128)(2,1)}, u32[]{:S(2)}) copy-start(bf16[1,4096,256]{2,1,0:T(8,128)(2,1)} %param.7) | copy-start | bytes 6291460
  0.6 4.2 %collective-permute-start = (bf16[4,4096]{1,0:T(4,128)(2,1)}, bf16[4,4096]{1,0:T(4,128)(2,1)S(1)}, u32[]{:S(2)}, u32[]{:S(2)}) collective-permute-start(bf16[4,4096]{1,0:T(4,128)(2,1)} %bitcast.50), channel_id=1, source_target_pairs={{0,64},{64,128},{128,192},{192,0},{1,65},{65,129},{129,193},{193,1... | collective-permute-start | bytes 98312 | tf_op jit(solution)/shard_map/ppermute | solution.py:42
  32.9 3.6 %collective-permute-start.1 = (bf16[32,4096]{1,0:T(8,128)(2,1)S(1)}, bf16[32,4096]{1,0:T(8,128)(2,1)S(1)}, u32[]{:S(2)}, u32[]{:S(2)}) collective-permute-start(bf16[32,4096]{1,0:T(8,128)(2,1)S(1)} %reshape_squeeze.6), channel_id=1, source_target_pairs={{0,1},{1,0},{8,9},{9,8},{2,3},{3,2},{10,11},{11,10},{4,5},{5,4},{1... | collective-permute-start | bytes 786440 | tf_op jit(solution)/shard_map/ppermute | solution.py:25
  33.8 7.6 %collective-permute-start.4 = (bf16[32,4096]{1,0:T(8,128)(2,1)S(1)}, bf16[32,4096]{1,0:T(8,128)(2,1)S(1)}, u32[]{:S(2)}, u32[]{:S(2)}) collective-permute-start(bf16[32,4096]{1,0:T(8,128)(2,1)S(1)} %reshape_squeeze.6), channel_id=1, source_target_pairs={{0,8},{1,15},{8,2},{9,1},{2,10},{3,9},{10,4},{11,3},{4,12},{5,11},... | collective-permute-start | bytes 786440 | tf_op jit(solution)/shard_map/ppermute | solution.py:33
  34.8 2.6 %collective-permute-start.10 = (bf16[32,4096]{1,0:T(8,128)(2,1)S(1)}, bf16[32,4096]{1,0:T(8,128)(2,1)S(1)}, u32[]{:S(2)}, u32[]{:S(2)}) collective-permute-start(bf16[32,4096]{1,0:T(8,128)(2,1)S(1)} %reshape_squeeze.7), channel_id=1, source_target_pairs={{0,1},{1,0},{8,9},{9,8},{2,3},{3,2},{10,11},{11,10},{4,5},{5,4},{1... | collective-permute-start | bytes 786440 | tf_op jit(solution)/shard_map/ppermute | solution.py:25
  34.9 9.3 %collective-permute-start.13 = (bf16[32,4096]{1,0:T(8,128)(2,1)S(1)}, bf16[32,4096]{1,0:T(8,128)(2,1)S(1)}, u32[]{:S(2)}, u32[]{:S(2)}) collective-permute-start(bf16[32,4096]{1,0:T(8,128)(2,1)S(1)} %reshape_squeeze.7), channel_id=1, source_target_pairs={{0,8},{1,15},{8,2},{9,1},{2,10},{3,9},{10,4},{11,3},{4,12},{5,11},... | collective-permute-start | bytes 786440 | tf_op jit(solution)/shard_map/ppermute | solution.py:33
  36.6 10.5 %collective-permute-start.2 = (bf16[64,4096]{1,0:T(8,128)(2,1)S(1)}, bf16[64,4096]{1,0:T(8,128)(2,1)S(1)}, u32[]{:S(2)}, u32[]{:S(2)}) collective-permute-start(bf16[64,4096]{1,0:T(8,128)(2,1)S(1)} %pad_maximum_fusion.2), channel_id=1, source_target_pairs={{0,16},{1,49},{8,24},{9,57},{2,18},{3,51},{10,26},{11,59},{4,20},{... | collective-permute-start | bytes 1572872 | tf_op jit(solution)/shard_map/ppermute | solution.py:29
  37.4 15.3 %collective-permute-start.11 = (bf16[64,4096]{1,0:T(8,128)(2,1)S(1)}, bf16[64,4096]{1,0:T(8,128)(2,1)S(1)}, u32[]{:S(2)}, u32[]{:S(2)}) collective-permute-start(bf16[64,4096]{1,0:T(8,128)(2,1)S(1)} %pad_maximum_fusion.3), channel_id=1, source_target_pairs={{0,16},{1,49},{8,24},{9,57},{2,18},{3,51},{10,26},{11,59},{4,20},{... | collective-permute-start | bytes 1572872 | tf_op jit(solution)/shard_map/ppermute | solution.py:29
  41.3 13.3 %collective-permute-start.5 = (bf16[32,4096]{1,0:T(8,128)(2,1)S(1)}, bf16[32,4096]{1,0:T(8,128)(2,1)S(1)}, u32[]{:S(2)}, u32[]{:S(2)}) collective-permute-start(bf16[32,4096]{1,0:T(8,128)(2,1)S(1)} %collective-permute-done.4), channel_id=1, source_target_pairs={{0,1},{1,0},{8,9},{9,8},{2,3},{3,2},{10,11},{11,10},{4,5},{5,4},{1... | collective-permute-start | bytes 786440 | tf_op jit(solution)/shard_map/ppermute | solution.py:25
  44.1 11.3 %collective-permute-start.14 = (bf16[32,4096]{1,0:T(8,128)(2,1)S(1)}, bf16[32,4096]{1,0:T(8,128)(2,1)S(1)}, u32[]{:S(2)}, u32[]{:S(2)}) collective-permute-start(bf16[32,4096]{1,0:T(8,128)(2,1)S(1)} %collective-permute-done.13), channel_id=1, source_target_pairs={{0,1},{1,0},{8,9},{9,8},{2,3},{3,2},{10,11},{11,10},{4,5},{5,4},{1... | collective-permute-start | bytes 786440 | tf_op jit(solution)/shard_map/ppermute | solution.py:25
  47.0 5.7 %collective-permute-start.3 = (bf16[64,4096]{1,0:T(8,128)(2,1)S(1)}, bf16[64,4096]{1,0:T(8,128)(2,1)S(1)}, u32[]{:S(2)}, u32[]{:S(2)}) collective-permute-start(bf16[64,4096]{1,0:T(8,128)(2,1)S(1)} %collective-permute-done.2), channel_id=1, source_target_pairs={{0,1},{1,0},{8,9},{9,8},{2,3},{3,2},{10,11},{11,10},{4,5},{5,4},{1... | collective-permute-start | bytes 1572872 | tf_op jit(solution)/shard_map/ppermute | solution.py:25
  52.6 1.9 %collective-permute-start.12 = (bf16[64,4096]{1,0:T(8,128)(2,1)S(1)}, bf16[64,4096]{1,0:T(8,128)(2,1)S(1)}, u32[]{:S(2)}, u32[]{:S(2)}) collective-permute-start(bf16[64,4096]{1,0:T(8,128)(2,1)S(1)} %collective-permute-done.11), channel_id=1, source_target_pairs={{0,1},{1,0},{8,9},{9,8},{2,3},{3,2},{10,11},{11,10},{4,5},{5,4},{1... | collective-permute-start | bytes 1572872 | tf_op jit(solution)/shard_map/ppermute | solution.py:25
  60.1 2.9 %collective-permute-start.6 = (bf16[128,4096]{1,0:T(8,128)(2,1)S(1)}, bf16[128,4096]{1,0:T(8,128)(2,1)S(1)}, u32[]{:S(2)}, u32[]{:S(2)}) collective-permute-start(bf16[128,4096]{1,0:T(8,128)(2,1)S(1)} %pad_maximum_fusion), channel_id=1, source_target_pairs={{0,1},{1,0},{8,9},{9,8},{2,3},{3,2},{10,11},{11,10},{4,5},{5,4},{1... | collective-permute-start | bytes 3145736 | tf_op jit(solution)/shard_map/ppermute | solution.py:25
  62.0 11.9 %copy-start.2 = (f32[256,4096]{1,0:T(8,128)}, f32[256,4096]{1,0:T(8,128)S(1)}, u32[]{:S(2)}) copy-start(f32[256,4096]{1,0:T(8,128)S(1)} %get-tuple-element.13) | copy-start | bytes 12582916
  62.2 2.7 %collective-permute-start.15 = (bf16[128,4096]{1,0:T(8,128)(2,1)S(1)}, bf16[128,4096]{1,0:T(8,128)(2,1)S(1)}, u32[]{:S(2)}, u32[]{:S(2)}) collective-permute-start(bf16[128,4096]{1,0:T(8,128)(2,1)S(1)} %pad_maximum_fusion.1), channel_id=1, source_target_pairs={{0,1},{1,0},{8,9},{9,8},{2,3},{3,2},{10,11},{11,10},{4,5},{5,4},{1... | collective-permute-start | bytes 3145736 | tf_op jit(solution)/shard_map/ppermute | solution.py:25
  63.3 10.5 %collective-permute-start.7 = (bf16[64,4096]{1,0:T(8,128)(2,1)S(1)}, bf16[64,4096]{1,0:T(8,128)(2,1)S(1)}, u32[]{:S(2)}, u32[]{:S(2)}) collective-permute-start(bf16[64,4096]{1,0:T(8,128)(2,1)S(1)} %fusion.15), channel_id=1, source_target_pairs={{0,16},{1,49},{8,24},{9,57},{2,18},{3,51},{10,26},{11,59},{4,20},{... | collective-permute-start | bytes 1572872 | tf_op jit(solution)/shard_map/ppermute | solution.py:29
  63.5 16.7 %collective-permute-start.9 = (bf16[32,4096]{1,0:T(8,128)(2,1)S(1)}, bf16[32,4096]{1,0:T(8,128)(2,1)S(1)}, u32[]{:S(2)}, u32[]{:S(2)}) collective-permute-start(bf16[32,4096]{1,0:T(8,128)(2,1)S(1)} %fusion.21), channel_id=1, source_target_pairs={{0,8},{1,15},{8,2},{9,1},{2,10},{3,9},{10,4},{11,3},{4,12},{5,11},... | collective-permute-start | bytes 786440 | tf_op jit(solution)/shard_map/ppermute | solution.py:33
  65.1 8.9 %copy-start.4 = (f32[128,4096]{1,0:T(8,128)}, f32[128,4096]{1,0:T(8,128)S(1)}, u32[]{:S(2)}) copy-start(f32[128,4096]{1,0:T(8,128)S(1)} %convert_element_type.68) | copy-start | bytes 6291460
  65.2 14.2 %collective-permute-start.16 = (bf16[64,4096]{1,0:T(8,128)(2,1)S(1)}, bf16[64,4096]{1,0:T(8,128)(2,1)S(1)}, u32[]{:S(2)}, u32[]{:S(2)}) collective-permute-start(bf16[64,4096]{1,0:T(8,128)(2,1)S(1)} %fusion.14), channel_id=1, source_target_pairs={{0,16},{1,49},{8,24},{9,57},{2,18},{3,51},{10,26},{11,59},{4,20},{... | collective-permute-start | bytes 1572872 | tf_op jit(solution)/shard_map/ppermute | solution.py:29
  73.8 6.3 %collective-permute-start.8 = (bf16[32,4096]{1,0:T(8,128)(2,1)S(1)}, bf16[32,4096]{1,0:T(8,128)(2,1)S(1)}, u32[]{:S(2)}, u32[]{:S(2)}) collective-permute-start(bf16[32,4096]{1,0:T(8,128)(2,1)S(1)} %slice.112), channel_id=1, source_target_pairs={{0,1},{1,0},{8,9},{9,8},{2,3},{3,2},{10,11},{11,10},{4,5},{5,4},{1... | collective-permute-start | bytes 786440 | tf_op jit(solution)/shard_map/ppermute | solution.py:25
  74.0 7.8 %collective-permute-start.18 = (bf16[32,4096]{1,0:T(8,128)(2,1)S(1)}, bf16[32,4096]{1,0:T(8,128)(2,1)}, u32[]{:S(2)}, u32[]{:S(2)}) collective-permute-start(bf16[32,4096]{1,0:T(8,128)(2,1)S(1)} %fusion.16), channel_id=1, source_target_pairs={{0,8},{1,15},{8,2},{9,1},{2,10},{3,9},{10,4},{11,3},{4,12},{5,11},... | collective-permute-start | bytes 786440 | tf_op jit(solution)/shard_map/ppermute | solution.py:33
  80.1 1.9 %collective-permute-start.17 = (bf16[32,4096]{1,0:T(8,128)(2,1)}, bf16[32,4096]{1,0:T(8,128)(2,1)}, u32[]{:S(2)}, u32[]{:S(2)}) collective-permute-start(bf16[32,4096]{1,0:T(8,128)(2,1)} %slice.123), channel_id=1, source_target_pairs={{0,1},{1,0},{8,9},{9,8},{2,3},{3,2},{10,11},{11,10},{4,5},{5,4},{1... | collective-permute-start | bytes 786440 | tf_op jit(solution)/shard_map/ppermute | solution.py:25
  84.7 21.5 %all-to-all-start.1 = ((bf16[8,2,4,4096]{3,2,1,0:T(4,128)(2,1)}), bf16[8,2,4,4096]{3,2,1,0:T(4,128)(2,1)S(1)}, u32[]{:S(2)}, u32[]{:S(2)}) async-start(bf16[8,2,4,4096]{3,2,1,0:T(4,128)(2,1)} %pad_maximum_fusion.4), calls=%async_computation.1 | async-start | bytes 1048576 | tf_op jit(solution)/shard_map/all_to_all | solution.py:37
  107.1 5.1 %collective-permute-start.19 = (bf16[4,4096]{1,0:T(4,128)(2,1)S(1)}, bf16[4,4096]{1,0:T(4,128)(2,1)S(1)}, u32[]{:S(2)}, u32[]{:S(2)}) collective-permute-start(bf16[4,4096]{1,0:T(4,128)(2,1)S(1)} %get-tuple-element.10), channel_id=1, source_target_pairs={{0,192},{64,0},{128,64},{192,128},{1,193},{65,1},{129,65},{193,129... | collective-permute-start | bytes 98312 | tf_op jit(solution)/shard_map/ppermute | solution.py:42
  (10 other events, 28.2 us)

commit v2 on v1

v2 whole, which is shorter than its diff:
```python
import jax
import jax.numpy as jnp
from jax import lax
from jax.experimental import pallas as pl
from jax.experimental.pallas import tpu as pltpu
from jax.sharding import PartitionSpec as P

PLANE = ("dp", "tensor")
NY, NZ = 4, 8
BF16 = jnp.bfloat16
F32 = jnp.float32
CHUNK = 1024


def place(y, z, core):
    y, z = y % NY, z % NZ
    return ((y * 2 + z % 2) * 4 + z // 2) * 2 + core


CHIPS = [(y, z) for y in range(NY) for z in range(NZ)]
CORE_SWAP = [(place(y, z, c), place(y, z, 1 - c)) for y, z in CHIPS for c in (0, 1)]
Y_NEXT = [(place(y, z, c), place(y + 1, z, c)) for y, z in CHIPS for c in (0, 1)]
Y_LAST = [(place(y, z, c), place(y - 1, z, c)) for y, z in CHIPS for c in (0, 1)]
Z_STEP = [(place(y, z, c), place(y, z + 1 - 2 * c, c)) for y, z in CHIPS for c in (0, 1)]
COLOURS = [[place(k - 2 * z, z, c) for z in range(NZ)] for k in range(NY) for c in (0, 1)]


def swap(x):
    return lax.ppermute(x, PLANE, CORE_SWAP)


def y_next(x):
    return lax.ppermute(x, PLANE, Y_NEXT)


def y_last(x):
    return lax.ppermute(x, PLANE, Y_LAST)


def z_step(x):
    return lax.ppermute(x, PLANE, Z_STEP)


def colour_all_to_all(x):
    return lax.all_to_all(x, PLANE, 0, 0, axis_index_groups=COLOURS)


def from_behind(x, axis, by):
    length = lax.axis_size(axis)
    return lax.ppermute(x, axis, [(i, (i + by) % length) for i in range(length)])


def contract_rows(left, right):
    return lax.dot_general(left, right, (((0,), (0,)), ((), ())), preferred_element_type=F32)


def contract_cols(left, right):
    return lax.dot_general(left, right, (((1,), (1,)), ((), ())), preferred_element_type=F32)


def local_kernel(body, shapes, *args):
    return pl.pallas_call(
        body,
        out_shape=[jax.ShapeDtypeStruct(shape, dtype) for shape, dtype in shapes],
        in_specs=[pl.BlockSpec(memory_space=pltpu.VMEM)] * len(args),
        out_specs=[pl.BlockSpec(memory_space=pltpu.VMEM)] * len(shapes),
        compiler_params=pltpu.CompilerParams(vmem_limit_bytes=32 * 2**20),
        cost_estimate=pl.CostEstimate(flops=0, bytes_accessed=0, transcendentals=0),
    )(*args)


def load_body(*refs):
    half = (len(refs) - 1) // 2
    done = refs[-1]
    copies = [pltpu.make_async_copy(refs[i], refs[half + i], done.at[i]) for i in range(half)]
    for copy in copies:
        copy.start()
    for copy in copies:
        copy.wait()


def load(*args):
    return pl.pallas_call(
        load_body,
        out_shape=[jax.ShapeDtypeStruct(a.shape, a.dtype) for a in args],
        in_specs=[pl.BlockSpec(memory_space=pl.ANY)] * len(args),
        out_specs=[pl.BlockSpec(memory_space=pl.ANY)] * len(args),
        scratch_shapes=[pltpu.SemaphoreType.DMA((len(args),))],
        compiler_params=pltpu.CompilerParams(vmem_limit_bytes=16 * 2**20),
        cost_estimate=pl.CostEstimate(flops=0, bytes_accessed=0, transcendentals=0),
    )(*args)


def after(x, *earlier):
    return lax.optimization_barrier((x, *earlier))[0]


def split_body(got_ref, own_ref):
    for kind in (0, 1):
        for pair in range(NZ // 2):
            two = [got_ref[2 * pair + i, kind].astype(F32) for i in (0, 1)]
            own_ref[kind, 8 * pair : 8 * pair + 8, :] = jnp.concatenate(two, 0).astype(BF16)


def forward_body(*refs):
    blocks, (gate_w, up_w, down_w), (layer, hidden, swish, rise, other) = refs[:8], refs[8:11], refs[11:]
    for i, block in enumerate(blocks):
        layer[32 * i : 32 * i + 32, :] = block[0]
    gate = jnp.dot(layer[...], gate_w[0], preferred_element_type=F32)
    upper = jnp.dot(layer[...], up_w[0], preferred_element_type=F32)
    sigma = jax.nn.sigmoid(gate)
    swish[...] = gate * sigma
    rise[...] = upper * (sigma * (1.0 + gate * (1.0 - sigma)))
    hidden[...] = (swish[...] * upper).astype(BF16)

    @pl.loop(0, down_w.shape[2], step=CHUNK)
    def _(start):
        columns = pl.ds(pl.multiple_of(start, CHUNK), CHUNK)
        other[:, columns] = jnp.dot(hidden[128:, :], down_w[0, :, columns], preferred_element_type=F32).astype(BF16)


def backward_body(*refs):
    blocks, (down_w, swish, rise), (cotangent, gate_grad, up_grad) = refs[:8], refs[8:11], refs[11:]
    for i, block in enumerate(blocks):
        cotangent[32 * i : 32 * i + 32, :] = block[1]
    hidden_grad = contract_cols(cotangent[...], down_w[0])
    gate_grad[...] = (hidden_grad * rise[...]).astype(BF16)
    up_grad[...] = (hidden_grad * swish[...]).astype(BF16)


def back_other_body(gate_grad, up_grad, gate_w, up_w, other):
    @pl.loop(0, gate_w.shape[1], step=CHUNK)
    def _(start):
        columns = pl.ds(pl.multiple_of(start, CHUNK), CHUNK)
        back = contract_cols(gate_grad[128:, :], gate_w[0, columns, :])
        back += contract_cols(up_grad[128:, :], up_w[0, columns, :])
        other[:, columns] = back.astype(BF16)


def put_sums(sums, columns, own, last, next_, step):
    own[:, columns] = sums[:32]
    last[:, columns] = sums[32:64].astype(BF16)
    next_[:, columns] = sums[64:96].astype(BF16)
    step[:, columns] = sums[96:].astype(BF16)


def out_sums_body(hidden, down_w, got, own, last, next_, step):
    @pl.loop(0, down_w.shape[2], step=CHUNK)
    def _(start):
        columns = pl.ds(pl.multiple_of(start, CHUNK), CHUNK)
        sums = jnp.dot(hidden[:128, :], down_w[0, :, columns], preferred_element_type=F32)
        put_sums(sums + got[:, columns].astype(F32), columns, own, last, next_, step)


def back_sums_body(gate_grad, up_grad, gate_w, up_w, got, own, last, next_, step):
    @pl.loop(0, gate_w.shape[1], step=CHUNK)
    def _(start):
        columns = pl.ds(pl.multiple_of(start, CHUNK), CHUNK)
        sums = contract_cols(gate_grad[:128, :], gate_w[0, columns, :])
        sums += contract_cols(up_grad[:128, :], up_w[0, columns, :])
        put_sums(sums + got[:, columns].astype(F32), columns, own, last, next_, step)


def join_body(*refs):
    joined = refs[8]
    for kind in (0, 1):
        own, *received = refs[4 * kind : 4 * kind + 4]
        for pair in range(NZ // 2):
            rows = slice(8 * pair, 8 * pair + 8)
            sums = own[rows, :]
            for term in received:
                sums = sums + term[rows, :].astype(F32)
            for i in (0, 1):
                joined[2 * pair + i, kind] = sums[4 * i : 4 * i + 4].astype(BF16)


def send_sums(own, last, next_, step):
    return [own, y_last(last), y_next(next_), z_step(step)]


def on_device(activations, w_gate, w_up, w_down, out_grad):
    arrived = from_behind(activations[0], "section", 1)
    mine = jnp.stack([arrived, out_grad[0]])
    _, rows, width = mine.shape
    units = w_down.shape[1]
    tokens = 2 * NY * NZ * rows
    got = colour_all_to_all(jnp.broadcast_to(mine[None], (NZ,) + mine.shape))

    (own,) = local_kernel(split_body, [((2, NZ * rows, width), BF16)], got)
    step, last, next_ = z_step(own), y_last(own), y_next(own)
    w_gate, w_up, w_down = load(after(w_gate, step), w_up, w_down)
    next_, last = lax.optimization_barrier((next_, last, w_gate))[:2]
    blocks = [own, next_, last, step]
    blocks = blocks + [swap(block) for block in blocks]

    send = ((NZ * rows, width), BF16)
    sends = [((NZ * rows, width), F32), send, send, send]
    layer_in, hidden, swish, rise, out_other = local_kernel(
        forward_body,
        [((tokens, width), BF16), ((tokens, units), BF16), ((tokens, units), F32), ((tokens, units), F32),
         ((tokens // 2, width), BF16)],
        *blocks, w_gate, w_up, w_down)
    out_got = swap(out_other)
    cotangent, gate_grad, up_grad = local_kernel(
        backward_body,
        [((tokens, width), BF16), ((tokens, units), BF16), ((tokens, units), BF16)],
        *blocks, w_down, swish, rise)
    (back_other,) = local_kernel(
        back_other_body, [((tokens // 2, width), BF16)], after(gate_grad, out_got), up_grad, w_gate, w_up)
    out_sums = local_kernel(out_sums_body, sends, hidden, w_down, out_got)
    back_got = after(swap(back_other), out_sums[0])
    out_terms = send_sums(*out_sums)
    back_terms = send_sums(*local_kernel(back_sums_body, sends, gate_grad, up_grad, w_gate, w_up, back_got))

    grad_down = contract_rows(hidden, cotangent).astype(BF16)
    grad_gate = contract_rows(layer_in, gate_grad).astype(BF16)
    grad_up = contract_rows(layer_in, up_grad).astype(BF16)

    (sums,) = local_kernel(join_body, [((NZ, 2, rows, width), BF16)], *out_terms, *back_terms)
    arrived = colour_all_to_all(sums)
    arrived, grad_gate, grad_up, grad_down = lax.optimization_barrier((arrived, grad_gate, grad_up, grad_down))
    final = jnp.sum(arrived.astype(F32), 0).astype(BF16)
    returned = from_behind(final[1], "section", -1)
    return (final[0][None], returned[None], grad_gate[None], grad_up[None], grad_down[None])


def solution(mesh):
    return jax.shard_map(
        on_device,
        mesh=mesh,
        in_specs=(
            P("section", PLANE, None),
            P("section", None, PLANE),
            P("section", None, PLANE),
            P("section", PLANE, None),
            P("section", PLANE, None),
        ),
        out_specs=(
            P("section", PLANE, None),
            P("section", PLANE, None),
            P("section", None, PLANE),
            P("section", None, PLANE),
            P("section", PLANE, None),
        ),
        check_vma=False,
    )
```

time: 114 us -> 105 us (0.921)
  Pallas kernels: 0 us -> 9.58 us
  waiting for transfers between devices: 46.5 us -> 37 us
  matrix products: 13.9 us -> 6.22 us
  starting transfers between devices: 13.6 us -> 18.2 us
  other arithmetic: 4.72 us -> 1.05 us
  local copies, waits for them, and re-layouts: 6.14 us -> 4.65 us
    ppermute x4 -> x6, waiting for transfers between devices: 21.6 us -> 6.71 us  [the longest x3 5.26 us: y_last(): return lax.ppermute(x, PLANE, Y_LAST)]
    pallas_call x0 -> x8, Pallas kernels: none -> 9.58 us  [the longest x7 9.13 us: local_kernel(): pl.pallas_call(body, out_shape=[jax.ShapeDtypeStruct(shape, dtype) for sh...]
    ppermute x4 -> x6, starting transfers between devices: 1.92 us -> 6.43 us  [the longest x3 4.19 us: y_last(): return lax.ppermute(x, PLANE, Y_LAST)]
    dot_general x6 -> x0, matrix products: 4.39 us -> none  [the longest x3 2.22 us: contract_cols(): lax.dot_general(left, right, (((1,), (1,)), ((), ())), preferred_element_...]
    ppermute x2, waiting for transfers between devices: 2.57 us -> 6.2 us  [from_behind(): lax.ppermute(x, axis, [(i, (i + by) % length) for i in range(length)])]
    dot_general x3, matrix products: 9.56 us -> 6.22 us  [contract_rows(): lax.dot_general(left, right, (((0,), (0,)), ((), ())), preferred_element_...]
    another operation x3 -> x0, other arithmetic: 2.75 us -> none
    ppermute x4 -> x3, waiting for transfers between devices: 7.1 us -> 8.51 us  [z_step(): return lax.ppermute(x, PLANE, Z_STEP)]
  transfers between devices with their start and end apart: 21 -> 18, of which waited for: 14 -> 11; matrix products, arithmetic and copies ran while one was open for 13% -> 6% of each run, Pallas kernels for 0% -> 4%
where the time goes in v2:
time: 105 us; the launch traced here: 104 us
  waiting for transfers between devices  37 us (35%)
  blocking collectives  26.8 us (26%)
  starting transfers between devices  18.2 us (17%)
  Pallas kernels  9.58 us (9%)
  matrix products  6.22 us (6%)
  local copies, waits for them, and re-layouts  4.65 us (4%)
  other arithmetic  1.05 us (1%)
    all_to_all x1, blocking collectives, colour_all_to_all(): return lax.all_to_all(x, PLANE, 0, 0, axis_index_groups=COLOURS)  26.8 us
    all_to_all x1, waiting for transfers between devices, colour_all_to_all(): return lax.all_to_all(x, PLANE, 0, 0, axis_index_groups=COLOURS)  11.3 us
    pallas_call x7, Pallas kernels, local_kernel(): pl.pallas_call(body, out_shape=[jax.ShapeDtypeStruct(shape, dtype) for sh...  9.13 us
    ppermute x3, waiting for transfers between devices, z_step(): return lax.ppermute(x, PLANE, Z_STEP)  8.51 us
    dot_general x3, matrix products, contract_rows(): lax.dot_general(left, right, (((0,), (0,)), ((), ())), preferred_element_...  6.22 us
    ppermute x2, waiting for transfers between devices, from_behind(): lax.ppermute(x, axis, [(i, (i + by) % length) for i in range(length)])  6.2 us
    ppermute x3, waiting for transfers between devices, y_last(): return lax.ppermute(x, PLANE, Y_LAST)  5.26 us
    ppermute x6, waiting for transfers between devices, swap(): return lax.ppermute(x, PLANE, CORE_SWAP)  4.35 us
  transfers between devices with their start and end apart: 18, of which 11 were waited for; matrix products, arithmetic and copies ran while one was open for 6% of the time, Pallas kernels for 4%

profile of v2, /device:TPU:6, one launch (start us, length us, event | category | flops | bytes accessed | tf_op | source)
XLA Modules:
  0.0 104.3 jit_solution(12763019880594482806)
XLA Ops:
  0.6 2.3 %collective-permute-start = (bf16[4,4096]{1,0:T(4,128)(2,1)}, bf16[4,4096]{1,0:T(4,128)(2,1)S(1)}, u32[]{:S(2)}, u32[]{:S(2)}) collective-permute-start(bf16[4,4096]{1,0:T(4,128)(2,1)} %bitcast.19), channel_id=1, source_target_pairs={{0,64},{64,128},{128,192},{192,0},{1,65},{65,129},{129,193},{193,1... | collective-permute-start | bytes 98312 | tf_op jit(solution)/shard_map/ppermute | solution.py:50
  2.9 1.9 %collective-permute-done = bf16[4,4096]{1,0:T(4,128)(2,1)S(1)} collective-permute-done((bf16[4,4096]{1,0:T(4,128)(2,1)}, bf16[4,4096]{1,0:T(4,128)(2,1)S(1)}, u32[]{:S(2)}, u32[]{:S(2)}) %collective-permute-start) | collective-permute-done | bytes 32800 | tf_op jit(solution)/shard_map/ppermute | solution.py:50
  5.9 26.8 %all_to_all.10.got_ref = bf16[8,2,4,4096]{3,2,1,0:T(4,128)(2,1)S(1)} all-to-all(bf16[8,2,4,4096]{3,2,1,0:T(4,128)(2,1)S(1)} %broadcast_in_dim.18), channel_id=1, replica_groups={{0,40,2,42,4,44,6,46},{1,41,3,43,5,45,7,47},{16,56,18,58,20,60,22,62},{..., dimensions={0} | all-to-all | bytes 1048576 | tf_op jit(solution)/shard_map/all_to_all | solution.py:45
  33.8 1.7 %collective-permute-start.2 = (bf16[2,32,4096]{2,1,0:T(8,128)(2,1)S(1)}, bf16[2,32,4096]{2,1,0:T(8,128)(2,1)S(1)}, u32[]{:S(2)}, u32[]{:S(2)}) collective-permute-start(bf16[2,32,4096]{2,1,0:T(8,128)(2,1)S(1)} %shard_map.92.refs_0_), channel_id=1, source_target_pairs={{0,48},{1,49},{8,56},{9,57},{2,50},{3,51},{10,58},{11,59},{4,52},{... | collective-permute-start | bytes 1572872 | tf_op jit(solution)/shard_map/ppermute | solution.py:37
  35.8 7.4 %collective-permute-done.3.refs_3_ = bf16[2,32,4096]{2,1,0:T(8,128)(2,1)S(1)} collective-permute-done((bf16[2,32,4096]{2,1,0:T(8,128)(2,1)S(1)}, bf16[2,32,4096]{2,1,0:T(8,128)(2,1)S(1)}, u32[]{:S(2)}, u32[]{:S(2)}) %collective-permute-start.3) | collective-permute-done | bytes 524320 | tf_op jit(solution)/shard_map/ppermute | solution.py:41
  43.3 1.6 %copy-done.1 = bf16[1,4096,256]{2,1,0:T(8,128)(2,1)S(1)} copy-done((bf16[1,4096,256]{2,1,0:T(8,128)(2,1)S(1)}, bf16[1,4096,256]{2,1,0:T(8,128)(2,1)}, u32[]{:S(2)}) %copy-start.1) | copy-done | bytes 2097176
  44.8 1.6 %copy-done.2 = bf16[1,256,4096]{2,1,0:T(8,128)(2,1)S(1)} copy-done((bf16[1,256,4096]{2,1,0:T(8,128)(2,1)S(1)}, bf16[1,256,4096]{2,1,0:T(8,128)(2,1)}, u32[]{:S(2)}) %copy-start.2) | copy-done | bytes 2097176
  47.6 2.0 %collective-permute-done.7.refs_7_ = bf16[2,32,4096]{2,1,0:T(8,128)(2,1)S(1)} collective-permute-done((bf16[2,32,4096]{2,1,0:T(8,128)(2,1)S(1)}, bf16[2,32,4096]{2,1,0:T(8,128)(2,1)S(1)}, u32[]{:S(2)}, u32[]{:S(2)}) %collective-permute-start.7) | collective-permute-done | bytes 524320 | tf_op jit(solution)/shard_map/ppermute | solution.py:29
  50.4 2.2 %shard_map.94 = (bf16[256,4096]{1,0:T(8,128)(2,1)S(1)}, bf16[256,256]{1,0:T(8,128)(2,1)S(1)}, f32[256,256]{1,0:T(8,128)S(1)}, f32[256,256]{1,0:T(8,128)S(1)}, bf16[128,4096]{1,0:T(8,128)(2,1)S(1)}) custom-call(bf16[2,32,4096]{2,1,0:T(8,128)(2,1)S(1)} %shard_map.92.refs_0_, bf16[2,32,4096]{2,1,0:T(8,128)(2,1)S(1)} %collective-permute-done.1.refs_1_, ...), custom_call_target="tpu_custom_call" | custom-call | tf_op jit(solution)/shard_map/pallas_call | solution.py:62
  53.8 1.5 %collective-permute-done.8.got = bf16[128,4096]{1,0:T(8,128)(2,1)S(1)} collective-permute-done((bf16[128,4096]{1,0:T(8,128)(2,1)S(1)}, bf16[128,4096]{1,0:T(8,128)(2,1)S(1)}, u32[]{:S(2)}, u32[]{:S(2)}) %collective-permute-start.8) | collective-permute-done | bytes 1048608 | tf_op jit(solution)/shard_map/ppermute | solution.py:29
  55.4 1.9 %shard_map.97 = bf16[128,4096]{1,0:T(8,128)(2,1)S(1)} custom-call(bf16[256,256]{1,0:T(8,128)(2,1)S(1)} %get-tuple-element.49.gate_grad, bf16[256,256]{1,0:T(8,128)(2,1)S(1)} %get-tuple-element.48.up_grad, bf16[1,4096,256]{2,1,0:T(8,128)(2,1)S(1)} %get-tuple-element.34.refs_8_.gate_w, bf16[1,4096,256]{2,1,0:T(8,128)(2,1)S(1)} %get-tuple-element.37.refs_9_.up_w), custom_call_target="tpu_custom_call" | custom-call | tf_op jit(solution)/shard_map/pallas_call | solution.py:62
  59.1 1.5 %collective-permute-start.10 = (bf16[32,4096]{1,0:T(8,128)(2,1)S(1)}, bf16[32,4096]{1,0:T(8,128)(2,1)S(1)}, u32[]{:S(2)}, u32[]{:S(2)}) collective-permute-start(bf16[32,4096]{1,0:T(8,128)(2,1)S(1)} %get-tuple-element.43), channel_id=1, source_target_pairs={{0,16},{1,17},{8,24},{9,25},{2,18},{3,19},{10,26},{11,27},{4,20},{... | collective-permute-start | bytes 786440 | tf_op jit(solution)/shard_map/ppermute | solution.py:33
  60.6 1.3 %collective-permute-start.11 = (bf16[32,4096]{1,0:T(8,128)(2,1)S(1)}, bf16[32,4096]{1,0:T(8,128)(2,1)S(1)}, u32[]{:S(2)}, u32[]{:S(2)}) collective-permute-start(bf16[32,4096]{1,0:T(8,128)(2,1)S(1)} %get-tuple-element.44), channel_id=1, source_target_pairs={{0,8},{1,15},{8,2},{9,1},{2,10},{3,9},{10,4},{11,3},{4,12},{5,11},... | collective-permute-start | bytes 786440 | tf_op jit(solution)/shard_map/ppermute | solution.py:41
  62.0 1.9 %shard_map.98 = (f32[32,4096]{1,0:T(8,128)S(1)}, bf16[32,4096]{1,0:T(8,128)(2,1)S(1)}, bf16[32,4096]{1,0:T(8,128)(2,1)S(1)}, bf16[32,4096]{1,0:T(8,128)(2,1)S(1)}) custom-call(bf16[256,256]{1,0:T(8,128)(2,1)S(1)} %get-tuple-element.49.gate_grad, bf16[256,256]{1,0:T(8,128)(2,1)S(1)} %get-tuple-element.48.up_grad, ...), custom_call_target="tpu_custom_call" | custom-call | tf_op jit(solution)/shard_map/pallas_call | solution.py:62
  63.9 1.9 %collective-permute-start.13 = (bf16[32,4096]{1,0:T(8,128)(2,1)S(1)}, bf16[32,4096]{1,0:T(8,128)(2,1)S(1)}, u32[]{:S(2)}, u32[]{:S(2)}) collective-permute-start(bf16[32,4096]{1,0:T(8,128)(2,1)S(1)} %get-tuple-element.52), channel_id=1, source_target_pairs={{0,48},{1,49},{8,56},{9,57},{2,50},{3,51},{10,58},{11,59},{4,52},{... | collective-permute-start | bytes 786440 | tf_op jit(solution)/shard_map/ppermute | solution.py:37
  66.2 1.5 %collective-permute-done.9.refs_1_ = bf16[32,4096]{1,0:T(8,128)(2,1)S(1)} collective-permute-done((bf16[32,4096]{1,0:T(8,128)(2,1)S(1)}, bf16[32,4096]{1,0:T(8,128)(2,1)S(1)}, u32[]{:S(2)}, u32[]{:S(2)}) %collective-permute-start.9) | collective-permute-done | bytes 262176 | tf_op jit(solution)/shard_map/ppermute | solution.py:37
  69.1 3.7 %collective-permute-done.13.refs_5_ = bf16[32,4096]{1,0:T(8,128)(2,1)S(1)} collective-permute-done((bf16[32,4096]{1,0:T(8,128)(2,1)S(1)}, bf16[32,4096]{1,0:T(8,128)(2,1)S(1)}, u32[]{:S(2)}, u32[]{:S(2)}) %collective-permute-start.13) | collective-permute-done | bytes 262176 | tf_op jit(solution)/shard_map/ppermute | solution.py:37
  72.8 1.4 %collective-permute-done.14.refs_6_ = bf16[32,4096]{1,0:T(8,128)(2,1)S(1)} collective-permute-done((bf16[32,4096]{1,0:T(8,128)(2,1)S(1)}, bf16[32,4096]{1,0:T(8,128)(2,1)S(1)}, u32[]{:S(2)}, u32[]{:S(2)}) %collective-permute-start.14) | collective-permute-done | bytes 262176 | tf_op jit(solution)/shard_map/ppermute | solution.py:33
  76.4 3.8 %all-to-all-start.1 = ((bf16[8,2,4,4096]{3,2,1,0:T(4,128)(2,1)}), bf16[8,2,4,4096]{3,2,1,0:T(4,128)(2,1)S(1)}, u32[]{:S(2)}, u32[]{:S(2)}) async-start(bf16[8,2,4,4096]{3,2,1,0:T(4,128)(2,1)} %shard_map.99), calls=%async_computation.1 | async-start | bytes 1048576 | tf_op jit(solution)/shard_map/all_to_all | solution.py:45
  80.2 2.1 %convolution_convert_fusion.1 = bf16[4096,256]{1,0:T(8,128)(2,1)} fusion(bf16[256,4096]{1,0:T(8,128)(2,1)S(1)} %get-tuple-element.55, bf16[256,256]{1,0:T(8,128)(2,1)S(1)} %get-tuple-element.48.up_grad), kind=kOutput, calls=%fused_computation.1 | convolution fusion | flops 537919488 | bytes 4325376 | tf_op jit(solution)/shard_map/dot_general | solution.py:54
  82.3 2.1 %convolution_convert_fusion.2 = bf16[4096,256]{1,0:T(8,128)(2,1)} fusion(bf16[256,4096]{1,0:T(8,128)(2,1)S(1)} %get-tuple-element.55, bf16[256,256]{1,0:T(8,128)(2,1)S(1)} %get-tuple-element.49.gate_grad), kind=kOutput, calls=%fused_computation.2 | convolution fusion | flops 537919488 | bytes 4325376 | tf_op jit(solution)/shard_map/dot_general | solution.py:54
  84.4 2.1 %convolution_convert_fusion = bf16[256,4096]{1,0:T(8,128)(2,1)} fusion(bf16[256,256]{1,0:T(8,128)(2,1)S(1)} %get-tuple-element.39.hidden, bf16[256,4096]{1,0:T(8,128)(2,1)S(1)} %copy-done.4), kind=kOutput, calls=%fused_computation | convolution fusion | flops 537919488 | bytes 4325376 | tf_op jit(solution)/shard_map/dot_general | solution.py:54
  86.4 11.3 %all-to-all-done.1 = bf16[8,2,4,4096]{3,2,1,0:T(4,128)(2,1)S(1)} async-done(((bf16[8,2,4,4096]{3,2,1,0:T(4,128)(2,1)}), bf16[8,2,4,4096]{3,2,1,0:T(4,128)(2,1)S(1)}, u32[]{:S(2)}, u32[]{:S(2)}) %all-to-all-start.1) | async-done | bytes 524320 | tf_op jit(solution)/shard_map/all_to_all | solution.py:45
  99.4 4.3 %collective-permute-done.16 = bf16[4,4096]{1,0:T(4,128)(2,1)S(1)} collective-permute-done((bf16[4,4096]{1,0:T(4,128)(2,1)S(1)}, bf16[4,4096]{1,0:T(4,128)(2,1)S(1)}, u32[]{:S(2)}, u32[]{:S(2)}) %collective-permute-start.16) | collective-permute-done | bytes 32800 | tf_op jit(solution)/shard_map/ppermute | solution.py:50
  (39 shorter events, 13.6 us)
Async XLA Ops:
  0.6 42.6 %copy-start = (bf16[1,4096,256]{2,1,0:T(8,128)(2,1)S(1)}, bf16[1,4096,256]{2,1,0:T(8,128)(2,1)}, u32[]{:S(2)}) copy-start(bf16[1,4096,256]{2,1,0:T(8,128)(2,1)} %refs_0_) | copy-start | bytes 6291460
  0.6 4.2 %collective-permute-start = (bf16[4,4096]{1,0:T(4,128)(2,1)}, bf16[4,4096]{1,0:T(4,128)(2,1)S(1)}, u32[]{:S(2)}, u32[]{:S(2)}) collective-permute-start(bf16[4,4096]{1,0:T(4,128)(2,1)} %bitcast.19), channel_id=1, source_target_pairs={{0,64},{64,128},{128,192},{192,0},{1,65},{65,129},{129,193},{193,1... | collective-permute-start | bytes 98312 | tf_op jit(solution)/shard_map/ppermute | solution.py:50
  32.8 10.5 %collective-permute-start.3 = (bf16[2,32,4096]{2,1,0:T(8,128)(2,1)S(1)}, bf16[2,32,4096]{2,1,0:T(8,128)(2,1)S(1)}, u32[]{:S(2)}, u32[]{:S(2)}) collective-permute-start(bf16[2,32,4096]{2,1,0:T(8,128)(2,1)S(1)} %shard_map.92.refs_0_), channel_id=1, source_target_pairs={{0,8},{1,15},{8,2},{9,1},{2,10},{3,9},{10,4},{11,3},{4,12},{5,11},... | collective-permute-start | bytes 1572872 | tf_op jit(solution)/shard_map/ppermute | solution.py:41
  33.8 13.1 %collective-permute-start.2 = (bf16[2,32,4096]{2,1,0:T(8,128)(2,1)S(1)}, bf16[2,32,4096]{2,1,0:T(8,128)(2,1)S(1)}, u32[]{:S(2)}, u32[]{:S(2)}) collective-permute-start(bf16[2,32,4096]{2,1,0:T(8,128)(2,1)S(1)} %shard_map.92.refs_0_), channel_id=1, source_target_pairs={{0,48},{1,49},{8,56},{9,57},{2,50},{3,51},{10,58},{11,59},{4,52},{... | collective-permute-start | bytes 1572872 | tf_op jit(solution)/shard_map/ppermute | solution.py:37
  35.5 11.4 %collective-permute-start.1 = (bf16[2,32,4096]{2,1,0:T(8,128)(2,1)S(1)}, bf16[2,32,4096]{2,1,0:T(8,128)(2,1)S(1)}, u32[]{:S(2)}, u32[]{:S(2)}) collective-permute-start(bf16[2,32,4096]{2,1,0:T(8,128)(2,1)S(1)} %shard_map.92.refs_0_), channel_id=1, source_target_pairs={{0,16},{1,17},{8,24},{9,25},{2,18},{3,19},{10,26},{11,27},{4,20},{... | collective-permute-start | bytes 1572872 | tf_op jit(solution)/shard_map/ppermute | solution.py:33
  35.8 11.8 %collective-permute-start.4 = (bf16[2,32,4096]{2,1,0:T(8,128)(2,1)S(1)}, bf16[2,32,4096]{2,1,0:T(8,128)(2,1)S(1)}, u32[]{:S(2)}, u32[]{:S(2)}) collective-permute-start(bf16[2,32,4096]{2,1,0:T(8,128)(2,1)S(1)} %shard_map.92.refs_0_), channel_id=1, source_target_pairs={{0,1},{1,0},{8,9},{9,8},{2,3},{3,2},{10,11},{11,10},{4,5},{5,4},{1... | collective-permute-start | bytes 1572872 | tf_op jit(solution)/shard_map/ppermute | solution.py:29
  43.2 1.6 %copy-start.1 = (bf16[1,4096,256]{2,1,0:T(8,128)(2,1)S(1)}, bf16[1,4096,256]{2,1,0:T(8,128)(2,1)}, u32[]{:S(2)}) copy-start(bf16[1,4096,256]{2,1,0:T(8,128)(2,1)} %refs_1_.1) | copy-start | bytes 6291460
  44.8 1.6 %copy-start.2 = (bf16[1,256,4096]{2,1,0:T(8,128)(2,1)S(1)}, bf16[1,256,4096]{2,1,0:T(8,128)(2,1)}, u32[]{:S(2)}) copy-start(bf16[1,256,4096]{2,1,0:T(8,128)(2,1)} %refs_2_.1) | copy-start | bytes 6291460
  46.9 2.8 %collective-permute-start.5 = (bf16[2,32,4096]{2,1,0:T(8,128)(2,1)S(1)}, bf16[2,32,4096]{2,1,0:T(8,128)(2,1)S(1)}, u32[]{:S(2)}, u32[]{:S(2)}) collective-permute-start(bf16[2,32,4096]{2,1,0:T(8,128)(2,1)S(1)} %collective-permute-done.1.refs_1_), channel_id=1, source_target_pairs={{0,1},{1,0},{8,9},{9,8},{2,3},{3,2},{10,11},{11,10},{4,5},{5,4},{1... | collective-permute-start | bytes 1572872 | tf_op jit(solution)/shard_map/ppermute | solution.py:29
  47.0 2.6 %collective-permute-start.7 = (bf16[2,32,4096]{2,1,0:T(8,128)(2,1)S(1)}, bf16[2,32,4096]{2,1,0:T(8,128)(2,1)S(1)}, u32[]{:S(2)}, u32[]{:S(2)}) collective-permute-start(bf16[2,32,4096]{2,1,0:T(8,128)(2,1)S(1)} %collective-permute-done.3.refs_3_), channel_id=1, source_target_pairs={{0,1},{1,0},{8,9},{9,8},{2,3},{3,2},{10,11},{11,10},{4,5},{5,4},{1... | collective-permute-start | bytes 1572872 | tf_op jit(solution)/shard_map/ppermute | solution.py:29
  47.5 2.9 %collective-permute-start.6 = (bf16[2,32,4096]{2,1,0:T(8,128)(2,1)S(1)}, bf16[2,32,4096]{2,1,0:T(8,128)(2,1)S(1)}, u32[]{:S(2)}, u32[]{:S(2)}) collective-permute-start(bf16[2,32,4096]{2,1,0:T(8,128)(2,1)S(1)} %collective-permute-done.2.refs_2_), channel_id=1, source_target_pairs={{0,1},{1,0},{8,9},{9,8},{2,3},{3,2},{10,11},{11,10},{4,5},{5,4},{1... | collective-permute-start | bytes 1572872 | tf_op jit(solution)/shard_map/ppermute | solution.py:29
  52.6 2.7 %collective-permute-start.8 = (bf16[128,4096]{1,0:T(8,128)(2,1)S(1)}, bf16[128,4096]{1,0:T(8,128)(2,1)S(1)}, u32[]{:S(2)}, u32[]{:S(2)}) collective-permute-start(bf16[128,4096]{1,0:T(8,128)(2,1)S(1)} %get-tuple-element.40), channel_id=1, source_target_pairs={{0,1},{1,0},{8,9},{9,8},{2,3},{3,2},{10,11},{11,10},{4,5},{5,4},{1... | collective-permute-start | bytes 3145736 | tf_op jit(solution)/shard_map/ppermute | solution.py:29
  53.8 3.5 %copy-start.3 = (bf16[256,4096]{1,0:T(8,128)(2,1)}, bf16[256,4096]{1,0:T(8,128)(2,1)S(1)}, u32[]{:S(2)}) copy-start(bf16[256,4096]{1,0:T(8,128)(2,1)S(1)} %get-tuple-element.56) | copy-start | bytes 6291460
  57.3 4.6 %collective-permute-start.12 = (bf16[128,4096]{1,0:T(8,128)(2,1)S(1)}, bf16[128,4096]{1,0:T(8,128)(2,1)S(1)}, u32[]{:S(2)}, u32[]{:S(2)}) collective-permute-start(bf16[128,4096]{1,0:T(8,128)(2,1)S(1)} %shard_map.97), channel_id=1, source_target_pairs={{0,1},{1,0},{8,9},{9,8},{2,3},{3,2},{10,11},{11,10},{4,5},{5,4},{1... | collective-permute-start | bytes 3145736 | tf_op jit(solution)/shard_map/ppermute | solution.py:29
  58.5 9.2 %collective-permute-start.9 = (bf16[32,4096]{1,0:T(8,128)(2,1)S(1)}, bf16[32,4096]{1,0:T(8,128)(2,1)S(1)}, u32[]{:S(2)}, u32[]{:S(2)}) collective-permute-start(bf16[32,4096]{1,0:T(8,128)(2,1)S(1)} %get-tuple-element.42), channel_id=1, source_target_pairs={{0,48},{1,49},{8,56},{9,57},{2,50},{3,51},{10,58},{11,59},{4,52},{... | collective-permute-start | bytes 786440 | tf_op jit(solution)/shard_map/ppermute | solution.py:37
  59.1 10.0 %collective-permute-start.10 = (bf16[32,4096]{1,0:T(8,128)(2,1)S(1)}, bf16[32,4096]{1,0:T(8,128)(2,1)S(1)}, u32[]{:S(2)}, u32[]{:S(2)}) collective-permute-start(bf16[32,4096]{1,0:T(8,128)(2,1)S(1)} %get-tuple-element.43), channel_id=1, source_target_pairs={{0,16},{1,17},{8,24},{9,25},{2,18},{3,19},{10,26},{11,27},{4,20},{... | collective-permute-start | bytes 786440 | tf_op jit(solution)/shard_map/ppermute | solution.py:33
  60.6 8.4 %collective-permute-start.11 = (bf16[32,4096]{1,0:T(8,128)(2,1)S(1)}, bf16[32,4096]{1,0:T(8,128)(2,1)S(1)}, u32[]{:S(2)}, u32[]{:S(2)}) collective-permute-start(bf16[32,4096]{1,0:T(8,128)(2,1)S(1)} %get-tuple-element.44), channel_id=1, source_target_pairs={{0,8},{1,15},{8,2},{9,1},{2,10},{3,9},{10,4},{11,3},{4,12},{5,11},... | collective-permute-start | bytes 786440 | tf_op jit(solution)/shard_map/ppermute | solution.py:41
  63.9 8.9 %collective-permute-start.13 = (bf16[32,4096]{1,0:T(8,128)(2,1)S(1)}, bf16[32,4096]{1,0:T(8,128)(2,1)S(1)}, u32[]{:S(2)}, u32[]{:S(2)}) collective-permute-start(bf16[32,4096]{1,0:T(8,128)(2,1)S(1)} %get-tuple-element.52), channel_id=1, source_target_pairs={{0,48},{1,49},{8,56},{9,57},{2,50},{3,51},{10,58},{11,59},{4,52},{... | collective-permute-start | bytes 786440 | tf_op jit(solution)/shard_map/ppermute | solution.py:37
  65.8 8.5 %collective-permute-start.14 = (bf16[32,4096]{1,0:T(8,128)(2,1)S(1)}, bf16[32,4096]{1,0:T(8,128)(2,1)S(1)}, u32[]{:S(2)}, u32[]{:S(2)}) collective-permute-start(bf16[32,4096]{1,0:T(8,128)(2,1)S(1)} %get-tuple-element.53), channel_id=1, source_target_pairs={{0,16},{1,17},{8,24},{9,25},{2,18},{3,19},{10,26},{11,27},{4,20},{... | collective-permute-start | bytes 786440 | tf_op jit(solution)/shard_map/ppermute | solution.py:33
  67.7 7.6 %collective-permute-start.15 = (bf16[32,4096]{1,0:T(8,128)(2,1)S(1)}, bf16[32,4096]{1,0:T(8,128)(2,1)S(1)}, u32[]{:S(2)}, u32[]{:S(2)}) collective-permute-start(bf16[32,4096]{1,0:T(8,128)(2,1)S(1)} %get-tuple-element.54), channel_id=1, source_target_pairs={{0,8},{1,15},{8,2},{9,1},{2,10},{3,9},{10,4},{11,3},{4,12},{5,11},... | collective-permute-start | bytes 786440 | tf_op jit(solution)/shard_map/ppermute | solution.py:41
  76.4 21.3 %all-to-all-start.1 = ((bf16[8,2,4,4096]{3,2,1,0:T(4,128)(2,1)}), bf16[8,2,4,4096]{3,2,1,0:T(4,128)(2,1)S(1)}, u32[]{:S(2)}, u32[]{:S(2)}) async-start(bf16[8,2,4,4096]{3,2,1,0:T(4,128)(2,1)} %shard_map.99), calls=%async_computation.1 | async-start | bytes 1048576 | tf_op jit(solution)/shard_map/all_to_all | solution.py:45
  82.3 2.1 %copy-start.4 = (bf16[256,4096]{1,0:T(8,128)(2,1)S(1)}, bf16[256,4096]{1,0:T(8,128)(2,1)}, u32[]{:S(2)}) copy-start(bf16[256,4096]{1,0:T(8,128)(2,1)} %copy-done.3) | copy-start | bytes 6291460
  98.6 5.1 %collective-permute-start.16 = (bf16[4,4096]{1,0:T(4,128)(2,1)S(1)}, bf16[4,4096]{1,0:T(4,128)(2,1)S(1)}, u32[]{:S(2)}, u32[]{:S(2)}) collective-permute-start(bf16[4,4096]{1,0:T(4,128)(2,1)S(1)} %get-tuple-element.61), channel_id=1, source_target_pairs={{0,192},{64,0},{128,64},{192,128},{1,193},{65,1},{129,65},{193,129... | collective-permute-start | bytes 98312 | tf_op jit(solution)/shard_map/ppermute | solution.py:50

commit v3 on v2

v3 whole, which is shorter than its diff:
```python
import jax
import jax.numpy as jnp
from jax import lax
from jax.experimental import pallas as pl
from jax.experimental.pallas import tpu as pltpu
from jax.sharding import PartitionSpec as P

PLANE = ("dp", "tensor")
NY, NZ = 4, 8
BF16 = jnp.bfloat16
F32 = jnp.float32
CHUNK = 1024


def place(y, z, core):
    y, z = y % NY, z % NZ
    return ((y * 2 + z % 2) * 4 + z // 2) * 2 + core


CHIPS = [(y, z) for y in range(NY) for z in range(NZ)]
CORE_SWAP = [(place(y, z, c), place(y, z, 1 - c)) for y, z in CHIPS for c in (0, 1)]
Y_NEXT = [(place(y, z, c), place(y + 1, z, c)) for y, z in CHIPS for c in (0, 1)]
Y_LAST = [(place(y, z, c), place(y - 1, z, c)) for y, z in CHIPS for c in (0, 1)]
Z_STEP = [(place(y, z, c), place(y, z + 1 - 2 * c, c)) for y, z in CHIPS for c in (0, 1)]
COLOURS = [[place(k - 2 * z, z, c) for z in range(NZ)] for k in range(NY) for c in (0, 1)]


def swap(x):
    return lax.ppermute(x, PLANE, CORE_SWAP)


def y_next(x):
    return lax.ppermute(x, PLANE, Y_NEXT)


def y_last(x):
    return lax.ppermute(x, PLANE, Y_LAST)


def z_step(x):
    return lax.ppermute(x, PLANE, Z_STEP)


def colour_all_to_all(x):
    return lax.all_to_all(x, PLANE, 0, 0, axis_index_groups=COLOURS)


def from_behind(x, axis, by):
    length = lax.axis_size(axis)
    return lax.ppermute(x, axis, [(i, (i + by) % length) for i in range(length)])


def contract_rows(left, right):
    return lax.dot_general(left, right, (((0,), (0,)), ((), ())), preferred_element_type=F32)


def contract_cols(left, right):
    return lax.dot_general(left, right, (((1,), (1,)), ((), ())), preferred_element_type=F32)


def local_kernel(body, shapes, *args, scratch=()):
    return pl.pallas_call(
        body,
        out_shape=[jax.ShapeDtypeStruct(shape, dtype) for shape, dtype in shapes],
        in_specs=[pl.BlockSpec(memory_space=pltpu.VMEM)] * len(args),
        out_specs=[pl.BlockSpec(memory_space=pltpu.VMEM)] * len(shapes),
        scratch_shapes=list(scratch),
        compiler_params=pltpu.CompilerParams(vmem_limit_bytes=32 * 2**20),
        cost_estimate=pl.CostEstimate(flops=0, bytes_accessed=0, transcendentals=0),
    )(*args)


def load_body(*refs):
    half = (len(refs) - 1) // 2
    done = refs[-1]
    copies = [pltpu.make_async_copy(refs[i], refs[half + i], done.at[i]) for i in range(half)]
    for copy in copies:
        copy.start()
    for copy in copies:
        copy.wait()


def load(*args):
    return pl.pallas_call(
        load_body,
        out_shape=[jax.ShapeDtypeStruct(a.shape, a.dtype) for a in args],
        in_specs=[pl.BlockSpec(memory_space=pl.ANY)] * len(args),
        out_specs=[pl.BlockSpec(memory_space=pl.ANY)] * len(args),
        scratch_shapes=[pltpu.SemaphoreType.DMA((len(args),))],
        compiler_params=pltpu.CompilerParams(vmem_limit_bytes=16 * 2**20),
        cost_estimate=pl.CostEstimate(flops=0, bytes_accessed=0, transcendentals=0),
    )(*args)


def after(x, *earlier):
    return lax.optimization_barrier((x, *earlier))[0]


def split_body(got_ref, own_ref):
    for kind in (0, 1):
        for pair in range(NZ // 2):
            two = [got_ref[2 * pair + i, kind].astype(F32) for i in (0, 1)]
            own_ref[kind, 8 * pair : 8 * pair + 8, :] = jnp.concatenate(two, 0).astype(BF16)


def put_sums(sums, columns, own, last, next_, step):
    own[:, columns] = sums[:32]
    last[:, columns] = sums[32:64].astype(BF16)
    next_[:, columns] = sums[64:96].astype(BF16)
    step[:, columns] = sums[96:].astype(BF16)


def forward_body(*refs):
    blocks, gate_ws, up_ws, down_ws = refs[:4], refs[4:6], refs[6:8], refs[8:10]
    hiddens, swish, rise, sends, layer = refs[10:12], refs[12], refs[13], refs[14:18], refs[18]
    for i, block in enumerate(blocks):
        layer[32 * i : 32 * i + 32, :] = block[0]
    for core in (0, 1):
        gate = jnp.dot(layer[...], gate_ws[core][0], preferred_element_type=F32)
        upper = jnp.dot(layer[...], up_ws[core][0], preferred_element_type=F32)
        sigma = jax.nn.sigmoid(gate)
        swish[core] = gate * sigma
        rise[core] = upper * (sigma * (1.0 + gate * (1.0 - sigma)))
        hiddens[core][...] = (swish[core] * upper).astype(BF16)

    @pl.loop(0, down_ws[0].shape[2], step=CHUNK)
    def _(start):
        columns = pl.ds(pl.multiple_of(start, CHUNK), CHUNK)
        sums = sum(
            jnp.dot(hiddens[core][...], down_ws[core][0, :, columns], preferred_element_type=F32) for core in (0, 1)
        )
        put_sums(sums, columns, *sends)


def backward_body(*refs):
    blocks, gate_ws, up_ws, down_ws, (swish, rise, hidden) = refs[:4], refs[4:6], refs[6:8], refs[8:10], refs[10:13]
    gate_grads, up_grads, sends, cotangent = (refs[13], refs[15].at[0]), (refs[14], refs[15].at[1]), refs[16:20], refs[20]
    refs[15][2] = hidden[...]
    for i, block in enumerate(blocks):
        cotangent[32 * i : 32 * i + 32, :] = block[1]
    for core in (0, 1):
        hidden_grad = contract_cols(cotangent[...], down_ws[core][0])
        gate_grads[core][...] = (hidden_grad * rise[core]).astype(BF16)
        up_grads[core][...] = (hidden_grad * swish[core]).astype(BF16)

    @pl.loop(0, gate_ws[0].shape[1], step=CHUNK)
    def _(start):
        columns = pl.ds(pl.multiple_of(start, CHUNK), CHUNK)
        sums = sum(
            contract_cols(gate_grads[core][...], gate_ws[core][0, columns, :])
            + contract_cols(up_grads[core][...], up_ws[core][0, columns, :])
            for core in (0, 1)
        )
        put_sums(sums, columns, *sends)


def weight_grads_body(*refs):
    blocks = refs[:8]
    gate_grad, up_grad, hidden = [(refs[8 + i], refs[11].at[i]) for i in range(3)]
    into_gate, into_up, into_down = refs[12:]
    layer = jnp.concatenate([block[0] for block in blocks], 0)
    for grad, into in ((gate_grad, into_gate), (up_grad, into_up)):
        grad = jnp.concatenate([grad[0][...], grad[1][...]], 0)
        into[0] = contract_rows(layer, grad).astype(BF16)
    hidden = jnp.concatenate([hidden[0][...], hidden[1][...]], 0)
    cotangent = jnp.concatenate([block[1] for block in blocks], 0)
    into_down[0] = contract_rows(hidden, cotangent).astype(BF16)


def weight_grads(*args):
    _, rows, width = args[0].shape
    tokens, units = args[8].shape
    part = width // 8
    streamed = [pl.BlockSpec((2, rows, part), lambda i: (0, 0, i))] * 8
    whole = [pl.BlockSpec((tokens, units), lambda i: (0, 0))] * 3 + [pl.BlockSpec((3, tokens, units), lambda i: (0, 0, 0))]
    across = [pl.BlockSpec((1, part, units), lambda i: (0, i, 0))] * 2
    along = [pl.BlockSpec((1, units, part), lambda i: (0, 0, i))]
    shapes = [(1, width, units), (1, width, units), (1, units, width)]
    return pl.pallas_call(
        weight_grads_body,
        grid=(width // part,),
        out_shape=[jax.ShapeDtypeStruct(shape, BF16) for shape in shapes],
        in_specs=streamed + whole,
        out_specs=across + along,
        compiler_params=pltpu.CompilerParams(vmem_limit_bytes=32 * 2**20),
        cost_estimate=pl.CostEstimate(flops=0, bytes_accessed=0, transcendentals=0),
    )(*args)


def join_body(*refs):
    joined = refs[8]
    for kind in (0, 1):
        own, *received = refs[4 * kind : 4 * kind + 4]
        for pair in range(NZ // 2):
            rows = slice(8 * pair, 8 * pair + 8)
            sums = own[rows, :]
            for term in received:
                sums = sums + term[rows, :].astype(F32)
            for i in (0, 1):
                joined[2 * pair + i, kind] = sums[4 * i : 4 * i + 4].astype(BF16)


def send_sums(own, last, next_, step):
    return [own, y_last(last), y_next(next_), z_step(step)]


def on_device(activations, w_gate, w_up, w_down, out_grad):
    arrived = from_behind(activations[0], "section", 1)
    mine = jnp.stack([arrived, out_grad[0]])
    _, rows, width = mine.shape
    units = w_down.shape[1]
    tokens = NY * NZ * rows
    got = colour_all_to_all(jnp.broadcast_to(mine[None], (NZ,) + mine.shape))

    got, *partner = lax.optimization_barrier((got, swap(w_gate), swap(w_up), swap(w_down)))

    (own,) = local_kernel(split_body, [((2, NZ * rows, width), BF16)], got)
    step, last, next_ = z_step(own), y_last(own), y_next(own)
    loaded = load(after(w_gate, step), w_up, w_down)
    blocks = [own, after(next_, loaded[0]), last, step]
    weights = [w for pair in zip(loaded, partner) for w in pair]

    send = ((NZ * rows, width), BF16)
    sends = [((NZ * rows, width), F32), send, send, send]
    some = ((tokens, units), BF16)
    scratch = [pltpu.VMEM((tokens, width), BF16)]
    kept = ((2, tokens, units), F32)
    hidden, hidden_other, swish, rise, *out_sums = local_kernel(
        forward_body, [some, some, kept, kept, *sends], *blocks, *weights, scratch=scratch)
    out_terms = send_sums(*out_sums)
    gate_grad, up_grad, give, *back_sums = local_kernel(
        backward_body, [some, some, ((3, tokens, units), BF16), *sends],
        *blocks, *weights, swish, rise, hidden_other, scratch=scratch)
    back_terms = send_sums(*back_sums)

    (sums,) = local_kernel(join_body, [((NZ, 2, rows, width), BF16)], *out_terms, *back_terms)

    *blocks, give = lax.optimization_barrier((*blocks, give, sums))[:-1]
    grad_gate, grad_up, grad_down = weight_grads(
        *blocks, *[swap(block) for block in blocks], gate_grad, up_grad, hidden, swap(give))
    arrived = colour_all_to_all(sums)
    arrived, grad_gate, grad_up, grad_down = lax.optimization_barrier((arrived, grad_gate, grad_up, grad_down))
    final = jnp.sum(arrived.astype(F32), 0).astype(BF16)
    returned = from_behind(final[1], "section", -1)
    return (final[0][None], returned[None], grad_gate, grad_up, grad_down)


def solution(mesh):
    return jax.shard_map(
        on_device,
        mesh=mesh,
        in_specs=(
            P("section", PLANE, None),
            P("section", None, PLANE),
            P("section", None, PLANE),
            P("section", PLANE, None),
            P("section", PLANE, None),
        ),
        out_specs=(
            P("section", PLANE, None),
            P("section", PLANE, None),
            P("section", None, PLANE),
            P("section", None, PLANE),
            P("section", PLANE, None),
        ),
        check_vma=False,
    )
```

time: 105 us -> 95.9 us (0.913)
  waiting for transfers between devices: 37 us -> 25.9 us
  matrix products: 6.22 us -> 0 us
  Pallas kernels: 9.58 us -> 14.5 us
  starting transfers between devices: 18.2 us -> 21.3 us
    all_to_all x1, waiting for transfers between devices: 11.3 us -> 3.22 us  [colour_all_to_all(): return lax.all_to_all(x, PLANE, 0, 0, axis_index_groups=COLOURS)]
    dot_general x3 -> x0, matrix products: 6.22 us -> none  [contract_rows(): lax.dot_general(left, right, (((0,), (0,)), ((), ())), preferred_element_...]
    pallas_call x0 -> x1, Pallas kernels: none -> 5.61 us  [weight_grads(): pl.pallas_call(weight_grads_body, grid=(width // part,), out_shape=[jax.S...]
    ppermute x3, starting transfers between devices: 4.19 us -> 7.69 us  [y_last(): return lax.ppermute(x, PLANE, Y_LAST)]
    ppermute x3, waiting for transfers between devices: 8.51 us -> 6.24 us  [z_step(): return lax.ppermute(x, PLANE, Z_STEP)]
    ppermute x3, waiting for transfers between devices: 1.44 us -> 3.7 us  [y_next(): return lax.ppermute(x, PLANE, Y_NEXT)]
    ppermute x3, waiting for transfers between devices: 5.26 us -> 3.18 us  [y_last(): return lax.ppermute(x, PLANE, Y_LAST)]
    ppermute x3, starting transfers between devices: 2.24 us -> 0.95 us  [y_next(): return lax.ppermute(x, PLANE, Y_NEXT)]
  transfers between devices with their start and end apart: 18 -> 20, of which waited for: 11 -> 7; matrix products, arithmetic and copies ran while one was open for 6% -> 1% of each run, Pallas kernels for 4% -> 11%
where the time goes in v3:
time: 95.9 us; the launch traced here: 95.6 us
  blocking collectives  27.4 us (29%)
  waiting for transfers between devices  25.9 us (27%)
  starting transfers between devices  21.3 us (22%)
  Pallas kernels  14.5 us (15%)
  local copies, waits for them, and re-layouts  4.64 us (5%)
  other arithmetic  1.05 us (1%)
    all_to_all x1, blocking collectives, colour_all_to_all(): return lax.all_to_all(x, PLANE, 0, 0, axis_index_groups=COLOURS)  27.4 us
    pallas_call x4, Pallas kernels, local_kernel(): pl.pallas_call(body, out_shape=[jax.ShapeDtypeStruct(shape, dtype) for sh...  8.49 us
    ppermute x3, starting transfers between devices, y_last(): return lax.ppermute(x, PLANE, Y_LAST)  7.69 us
    ppermute x3, waiting for transfers between devices, z_step(): return lax.ppermute(x, PLANE, Z_STEP)  6.24 us
    ppermute x2, waiting for transfers between devices, from_behind(): lax.ppermute(x, axis, [(i, (i + by) % length) for i in range(length)])  6.24 us
    pallas_call x1, Pallas kernels, weight_grads(): pl.pallas_call(weight_grads_body, grid=(width // part,), out_shape=[jax.S...  5.61 us
    all_to_all x1, starting transfers between devices, colour_all_to_all(): return lax.all_to_all(x, PLANE, 0, 0, axis_index_groups=COLOURS)  4.62 us
    unnamed x7, local copies, waits for them, and re-layouts  3.8 us
  transfers between devices with their start and end apart: 20, of which 7 were waited for; matrix products, arithmetic and copies ran while one was open for 1% of the time, Pallas kernels for 11%

profile of v3, /device:TPU:6, one launch (start us, length us, event | category | flops | bytes accessed | tf_op | source)
XLA Modules:
  0.0 95.6 jit_solution(2917656633394985620)
XLA Ops:
  1.3 2.2 %collective-permute-start = (bf16[4,4096]{1,0:T(4,128)(2,1)}, bf16[4,4096]{1,0:T(4,128)(2,1)S(1)}, u32[]{:S(2)}, u32[]{:S(2)}) collective-permute-start(bf16[4,4096]{1,0:T(4,128)(2,1)} %bitcast.7), channel_id=1, source_target_pairs={{0,64},{64,128},{128,192},{192,0},{1,65},{65,129},{129,193},{193,1... | collective-permute-start | bytes 98312 | tf_op jit(solution)/shard_map/ppermute | solution.py:50
  3.6 1.9 %collective-permute-done = bf16[4,4096]{1,0:T(4,128)(2,1)S(1)} collective-permute-done((bf16[4,4096]{1,0:T(4,128)(2,1)}, bf16[4,4096]{1,0:T(4,128)(2,1)S(1)}, u32[]{:S(2)}, u32[]{:S(2)}) %collective-permute-start) | collective-permute-done | bytes 32800 | tf_op jit(solution)/shard_map/ppermute | solution.py:50
  5.5 0.8 pad_maximum_fusion
  6.5 27.4 %all_to_all.10.got_ref = bf16[8,2,4,4096]{3,2,1,0:T(4,128)(2,1)S(1)} all-to-all(bf16[8,2,4,4096]{3,2,1,0:T(4,128)(2,1)S(1)} %broadcast_in_dim.4), channel_id=1, replica_groups={{0,40,2,42,4,44,6,46},{1,41,3,43,5,45,7,47},{16,56,18,58,20,60,22,62},{..., dimensions={0} | all-to-all | bytes 1048576 | tf_op jit(solution)/shard_map/all_to_all | solution.py:45
  34.0 1.0 %collective-permute-start.5 = (bf16[2,32,4096]{2,1,0:T(8,128)(2,1)S(1)}, bf16[2,32,4096]{2,1,0:T(8,128)(2,1)S(1)}, u32[]{:S(2)}, u32[]{:S(2)}) collective-permute-start(bf16[2,32,4096]{2,1,0:T(8,128)(2,1)S(1)} %shard_map.92.refs_0_), channel_id=1, source_target_pairs={{0,8},{1,15},{8,2},{9,1},{2,10},{3,9},{10,4},{11,3},{4,12},{5,11},... | collective-permute-start | bytes 1572872 | tf_op jit(solution)/shard_map/ppermute | solution.py:41
  35.0 0.8 collective-permute-start.4
  35.8 2.4 %collective-permute-start.6 = (bf16[2,32,4096]{2,1,0:T(8,128)(2,1)S(1)}, bf16[2,32,4096]{2,1,0:T(8,128)(2,1)S(1)}, u32[]{:S(2)}, u32[]{:S(2)}) collective-permute-start(bf16[2,32,4096]{2,1,0:T(8,128)(2,1)S(1)} %shard_map.92.refs_0_), channel_id=1, source_target_pairs={{0,48},{1,49},{8,56},{9,57},{2,50},{3,51},{10,58},{11,59},{4,52},{... | collective-permute-start | bytes 1572872 | tf_op jit(solution)/shard_map/ppermute | solution.py:37
  38.2 6.2 %collective-permute-done.5.refs_3_ = bf16[2,32,4096]{2,1,0:T(8,128)(2,1)S(1)} collective-permute-done((bf16[2,32,4096]{2,1,0:T(8,128)(2,1)S(1)}, bf16[2,32,4096]{2,1,0:T(8,128)(2,1)S(1)}, u32[]{:S(2)}, u32[]{:S(2)}) %collective-permute-start.5) | collective-permute-done | bytes 524320 | tf_op jit(solution)/shard_map/ppermute | solution.py:41
  44.5 1.6 %copy-done.1 = bf16[1,4096,256]{2,1,0:T(8,128)(2,1)S(1)} copy-done((bf16[1,4096,256]{2,1,0:T(8,128)(2,1)S(1)}, bf16[1,4096,256]{2,1,0:T(8,128)(2,1)}, u32[]{:S(2)}) %copy-start.1) | copy-done | bytes 2097176
  46.1 1.6 %copy-done.2 = bf16[1,256,4096]{2,1,0:T(8,128)(2,1)S(1)} copy-done((bf16[1,256,4096]{2,1,0:T(8,128)(2,1)S(1)}, bf16[1,256,4096]{2,1,0:T(8,128)(2,1)}, u32[]{:S(2)}) %copy-start.2) | copy-done | bytes 2097176
  48.1 2.5 %shard_map.94 = (bf16[128,256]{1,0:T(8,128)(2,1)S(1)}, bf16[128,256]{1,0:T(8,128)(2,1)S(1)}, f32[2,128,256]{2,1,0:T(8,128)S(1)}, f32[2,128,256]{2,1,0:T(8,128)S(...) custom-call(bf16[2,32,4096]{2,1,0:T(8,128)(2,1)S(1)} %shard_map.92.r, ...), custom_call_target="tpu_custom_call" | custom-call | tf_op jit(solution)/shard_map/pallas_call | solution.py:62
  50.7 2.0 %collective-permute-start.7 = (bf16[32,4096]{1,0:T(8,128)(2,1)S(1)}, bf16[32,4096]{1,0:T(8,128)(2,1)S(1)}, u32[]{:S(2)}, u32[]{:S(2)}) collective-permute-start(bf16[32,4096]{1,0:T(8,128)(2,1)S(1)} %get-tuple-element.51), channel_id=1, source_target_pairs={{0,48},{1,49},{8,56},{9,57},{2,50},{3,51},{10,58},{11,59},{4,52},{... | collective-permute-start | bytes 786440 | tf_op jit(solution)/shard_map/ppermute | solution.py:37
  52.8 1.5 %collective-permute-start.9 = (bf16[32,4096]{1,0:T(8,128)(2,1)S(1)}, bf16[32,4096]{1,0:T(8,128)(2,1)S(1)}, u32[]{:S(2)}, u32[]{:S(2)}) collective-permute-start(bf16[32,4096]{1,0:T(8,128)(2,1)S(1)} %get-tuple-element.53), channel_id=1, source_target_pairs={{0,8},{1,15},{8,2},{9,1},{2,10},{3,9},{10,4},{11,3},{4,12},{5,11},... | collective-permute-start | bytes 786440 | tf_op jit(solution)/shard_map/ppermute | solution.py:41
  54.3 4.8 %shard_map.95 = (bf16[128,256]{1,0:T(8,128)(2,1)S(1)}, bf16[128,256]{1,0:T(8,128)(2,1)S(1)}, bf16[3,128,256]{2,1,0:T(8,128)(2,1)S(1)}, f32[32,4096]{1,0:T(8,128)...) custom-call(bf16[2,32,4096]{2,1,0:T(8,128)(2,1)S(1)} %shard_map.92.refs_0_, ...), custom_call_target="tpu_custom_call" | custom-call | tf_op jit(solution)/shard_map/pallas_call | solution.py:62
  59.1 3.3 %collective-permute-start.10 = (bf16[32,4096]{1,0:T(8,128)(2,1)S(1)}, bf16[32,4096]{1,0:T(8,128)(2,1)S(1)}, u32[]{:S(2)}, u32[]{:S(2)}) collective-permute-start(bf16[32,4096]{1,0:T(8,128)(2,1)S(1)} %get-tuple-element.58), channel_id=1, source_target_pairs={{0,48},{1,49},{8,56},{9,57},{2,50},{3,51},{10,58},{11,59},{4,52},{... | collective-permute-start | bytes 786440 | tf_op jit(solution)/shard_map/ppermute | solution.py:37
  63.1 3.2 %collective-permute-done.10.refs_5_ = bf16[32,4096]{1,0:T(8,128)(2,1)S(1)} collective-permute-done((bf16[32,4096]{1,0:T(8,128)(2,1)S(1)}, bf16[32,4096]{1,0:T(8,128)(2,1)S(1)}, u32[]{:S(2)}, u32[]{:S(2)}) %collective-permute-start.10) | collective-permute-done | bytes 262176 | tf_op jit(solution)/shard_map/ppermute | solution.py:37
  66.3 3.7 %collective-permute-done.11.refs_6_ = bf16[32,4096]{1,0:T(8,128)(2,1)S(1)} collective-permute-done((bf16[32,4096]{1,0:T(8,128)(2,1)S(1)}, bf16[32,4096]{1,0:T(8,128)(2,1)S(1)}, u32[]{:S(2)}, u32[]{:S(2)}) %collective-permute-start.11) | collective-permute-done | bytes 262176 | tf_op jit(solution)/shard_map/ppermute | solution.py:33
  70.0 1.1 %shard_map.96 = bf16[8,2,4,4096]{3,2,1,0:T(4,128)(2,1)} custom-call(f32[32,4096]{1,0:T(8,128)S(1)} %get-tuple-element.50.refs_0_, bf16[32,4096]{1,0:T(8,128)(2,1)S(1)} %collective-permute-done.7.refs_1_, bf16[32,4096]{1,0:T(8,128)(2,1)S(1)} %collective-permute-done.8.refs_2_, bf16[32,4096]{1,0:T(8,128)(2,1)S(1)} %collective-permute-done.9.refs_3_, ...), custom_call_target="tpu_custom_call" | custom-call | tf_op jit(solution)/shard_map/pallas_call | solution.py:62
  71.0 4.6 %all-to-all-start.1 = ((bf16[8,2,4,4096]{3,2,1,0:T(4,128)(2,1)}), bf16[8,2,4,4096]{3,2,1,0:T(4,128)(2,1)S(1)}, u32[]{:S(2)}, u32[]{:S(2)}) async-start(bf16[8,2,4,4096]{3,2,1,0:T(4,128)(2,1)} %shard_map.96), calls=%async_computation.1 | async-start | bytes 1048576 | tf_op jit(solution)/shard_map/all_to_all | solution.py:45
  76.8 3.3 %collective-permute-done.17.refs_11_ = bf16[3,128,256]{2,1,0:T(8,128)(2,1)S(1)} collective-permute-done((bf16[3,128,256]{2,1,0:T(8,128)(2,1)S(1)}, bf16[3,128,256]{2,1,0:T(8,128)(2,1)S(1)}, u32[]{:S(2)}, u32[]{:S(2)}) %collective-permute-start.17) | collective-permute-done | bytes 196640 | tf_op jit(solution)/shard_map/ppermute | solution.py:29
  80.1 5.6 %shard_map.97 = (bf16[1,4096,256]{2,1,0:T(8,128)(2,1)}, bf16[1,4096,256]{2,1,0:T(8,128)(2,1)}, bf16[1,256,4096]{2,1,0:T(8,128)(2,1)}) custom-call(bf16[2,32,4096]{2,1,0:T(8,128)(2,1)S(1)} %shard_map.92.refs_0_, bf16[2,32,4096]{2,1,0:T(8,128)(2,1)S(1)} %collective-permute-done.4.refs_1_, bf16[2,32,4096]{2,1,0:T(8,128)(2,1)S(1)} %collective-permute-done.6.refs_2_, ...), custom_call_target="tpu_custom_call" | custom-call | tf_op jit(solution)/shard_map/pallas_call | solution.py:179
  85.7 3.2 %all-to-all-done.1 = bf16[8,2,4,4096]{3,2,1,0:T(4,128)(2,1)S(1)} async-done(((bf16[8,2,4,4096]{3,2,1,0:T(4,128)(2,1)}), bf16[8,2,4,4096]{3,2,1,0:T(4,128)(2,1)S(1)}, u32[]{:S(2)}, u32[]{:S(2)}) %all-to-all-start.1) | async-done | bytes 524320 | tf_op jit(solution)/shard_map/all_to_all | solution.py:45
  89.8 0.8 collective-permute-start.18
  90.6 4.3 %collective-permute-done.18 = bf16[4,4096]{1,0:T(4,128)(2,1)S(1)} collective-permute-done((bf16[4,4096]{1,0:T(4,128)(2,1)S(1)}, bf16[4,4096]{1,0:T(4,128)(2,1)S(1)}, u32[]{:S(2)}, u32[]{:S(2)}) %collective-permute-start.18) | collective-permute-done | bytes 32800 | tf_op jit(solution)/shard_map/ppermute | solution.py:50
  (34 shorter events, 4.9 us)
Async XLA Ops:
  0.6 43.8 %copy-start = (bf16[1,4096,256]{2,1,0:T(8,128)(2,1)S(1)}, bf16[1,4096,256]{2,1,0:T(8,128)(2,1)}, u32[]{:S(2)}) copy-start(bf16[1,4096,256]{2,1,0:T(8,128)(2,1)} %refs_0_) | copy-start | bytes 6291460
  0.6 33.2 %collective-permute-start.1 = (bf16[1,4096,256]{2,1,0:T(8,128)(2,1)}, bf16[1,4096,256]{2,1,0:T(8,128)(2,1)S(1)}, u32[]{:S(2)}, u32[]{:S(2)}) collective-permute-start(bf16[1,4096,256]{2,1,0:T(8,128)(2,1)} %refs_0_), channel_id=1, source_target_pairs={{0,1},{1,0},{8,9},{9,8},{2,3},{3,2},{10,11},{11,10},{4,5},{5,4},{1... | collective-permute-start | bytes 6291464 | tf_op jit(solution)/shard_map/ppermute | solution.py:29
  0.7 33.1 %collective-permute-start.2 = (bf16[1,4096,256]{2,1,0:T(8,128)(2,1)}, bf16[1,4096,256]{2,1,0:T(8,128)(2,1)S(1)}, u32[]{:S(2)}, u32[]{:S(2)}) collective-permute-start(bf16[1,4096,256]{2,1,0:T(8,128)(2,1)} %refs_1_.1), channel_id=1, source_target_pairs={{0,1},{1,0},{8,9},{9,8},{2,3},{3,2},{10,11},{11,10},{4,5},{5,4},{1... | collective-permute-start | bytes 6291464 | tf_op jit(solution)/shard_map/ppermute | solution.py:29
  1.2 32.6 %collective-permute-start.3 = (bf16[1,256,4096]{2,1,0:T(8,128)(2,1)}, bf16[1,256,4096]{2,1,0:T(8,128)(2,1)S(1)}, u32[]{:S(2)}, u32[]{:S(2)}) collective-permute-start(bf16[1,256,4096]{2,1,0:T(8,128)(2,1)} %refs_2_.1), channel_id=1, source_target_pairs={{0,1},{1,0},{8,9},{9,8},{2,3},{3,2},{10,11},{11,10},{4,5},{5,4},{1... | collective-permute-start | bytes 6291464 | tf_op jit(solution)/shard_map/ppermute | solution.py:29
  1.3 4.1 %collective-permute-start = (bf16[4,4096]{1,0:T(4,128)(2,1)}, bf16[4,4096]{1,0:T(4,128)(2,1)S(1)}, u32[]{:S(2)}, u32[]{:S(2)}) collective-permute-start(bf16[4,4096]{1,0:T(4,128)(2,1)} %bitcast.7), channel_id=1, source_target_pairs={{0,64},{64,128},{128,192},{192,0},{1,65},{65,129},{129,193},{193,1... | collective-permute-start | bytes 98312 | tf_op jit(solution)/shard_map/ppermute | solution.py:50
  34.0 10.5 %collective-permute-start.5 = (bf16[2,32,4096]{2,1,0:T(8,128)(2,1)S(1)}, bf16[2,32,4096]{2,1,0:T(8,128)(2,1)S(1)}, u32[]{:S(2)}, u32[]{:S(2)}) collective-permute-start(bf16[2,32,4096]{2,1,0:T(8,128)(2,1)S(1)} %shard_map.92.refs_0_), channel_id=1, source_target_pairs={{0,8},{1,15},{8,2},{9,1},{2,10},{3,9},{10,4},{11,3},{4,12},{5,11},... | collective-permute-start | bytes 1572872 | tf_op jit(solution)/shard_map/ppermute | solution.py:41
  35.0 13.1 %collective-permute-start.4 = (bf16[2,32,4096]{2,1,0:T(8,128)(2,1)S(1)}, bf16[2,32,4096]{2,1,0:T(8,128)(2,1)S(1)}, u32[]{:S(2)}, u32[]{:S(2)}) collective-permute-start(bf16[2,32,4096]{2,1,0:T(8,128)(2,1)S(1)} %shard_map.92.refs_0_), channel_id=1, source_target_pairs={{0,16},{1,17},{8,24},{9,25},{2,18},{3,19},{10,26},{11,27},{4,20},{... | collective-permute-start | bytes 1572872 | tf_op jit(solution)/shard_map/ppermute | solution.py:33
  35.8 12.3 %collective-permute-start.6 = (bf16[2,32,4096]{2,1,0:T(8,128)(2,1)S(1)}, bf16[2,32,4096]{2,1,0:T(8,128)(2,1)S(1)}, u32[]{:S(2)}, u32[]{:S(2)}) collective-permute-start(bf16[2,32,4096]{2,1,0:T(8,128)(2,1)S(1)} %shard_map.92.refs_0_), channel_id=1, source_target_pairs={{0,48},{1,49},{8,56},{9,57},{2,50},{3,51},{10,58},{11,59},{4,52},{... | collective-permute-start | bytes 1572872 | tf_op jit(solution)/shard_map/ppermute | solution.py:37
  44.5 1.6 %copy-start.1 = (bf16[1,4096,256]{2,1,0:T(8,128)(2,1)S(1)}, bf16[1,4096,256]{2,1,0:T(8,128)(2,1)}, u32[]{:S(2)}) copy-start(bf16[1,4096,256]{2,1,0:T(8,128)(2,1)} %refs_1_.1) | copy-start | bytes 6291460
  46.1 1.6 %copy-start.2 = (bf16[1,256,4096]{2,1,0:T(8,128)(2,1)S(1)}, bf16[1,256,4096]{2,1,0:T(8,128)(2,1)}, u32[]{:S(2)}) copy-start(bf16[1,256,4096]{2,1,0:T(8,128)(2,1)} %refs_2_.1) | copy-start | bytes 6291460
  50.7 11.7 %collective-permute-start.7 = (bf16[32,4096]{1,0:T(8,128)(2,1)S(1)}, bf16[32,4096]{1,0:T(8,128)(2,1)S(1)}, u32[]{:S(2)}, u32[]{:S(2)}) collective-permute-start(bf16[32,4096]{1,0:T(8,128)(2,1)S(1)} %get-tuple-element.51), channel_id=1, source_target_pairs={{0,48},{1,49},{8,56},{9,57},{2,50},{3,51},{10,58},{11,59},{4,52},{... | collective-permute-start | bytes 786440 | tf_op jit(solution)/shard_map/ppermute | solution.py:37
  52.7 10.4 %collective-permute-start.8 = (bf16[32,4096]{1,0:T(8,128)(2,1)S(1)}, bf16[32,4096]{1,0:T(8,128)(2,1)S(1)}, u32[]{:S(2)}, u32[]{:S(2)}) collective-permute-start(bf16[32,4096]{1,0:T(8,128)(2,1)S(1)} %get-tuple-element.52), channel_id=1, source_target_pairs={{0,16},{1,17},{8,24},{9,25},{2,18},{3,19},{10,26},{11,27},{4,20},{... | collective-permute-start | bytes 786440 | tf_op jit(solution)/shard_map/ppermute | solution.py:33
  52.8 10.3 %collective-permute-start.9 = (bf16[32,4096]{1,0:T(8,128)(2,1)S(1)}, bf16[32,4096]{1,0:T(8,128)(2,1)S(1)}, u32[]{:S(2)}, u32[]{:S(2)}) collective-permute-start(bf16[32,4096]{1,0:T(8,128)(2,1)S(1)} %get-tuple-element.53), channel_id=1, source_target_pairs={{0,8},{1,15},{8,2},{9,1},{2,10},{3,9},{10,4},{11,3},{4,12},{5,11},... | collective-permute-start | bytes 786440 | tf_op jit(solution)/shard_map/ppermute | solution.py:41
  59.1 7.2 %collective-permute-start.10 = (bf16[32,4096]{1,0:T(8,128)(2,1)S(1)}, bf16[32,4096]{1,0:T(8,128)(2,1)S(1)}, u32[]{:S(2)}, u32[]{:S(2)}) collective-permute-start(bf16[32,4096]{1,0:T(8,128)(2,1)S(1)} %get-tuple-element.58), channel_id=1, source_target_pairs={{0,48},{1,49},{8,56},{9,57},{2,50},{3,51},{10,58},{11,59},{4,52},{... | collective-permute-start | bytes 786440 | tf_op jit(solution)/shard_map/ppermute | solution.py:37
  62.4 7.6 %collective-permute-start.11 = (bf16[32,4096]{1,0:T(8,128)(2,1)S(1)}, bf16[32,4096]{1,0:T(8,128)(2,1)S(1)}, u32[]{:S(2)}, u32[]{:S(2)}) collective-permute-start(bf16[32,4096]{1,0:T(8,128)(2,1)S(1)} %get-tuple-element.59), channel_id=1, source_target_pairs={{0,16},{1,17},{8,24},{9,25},{2,18},{3,19},{10,26},{11,27},{4,20},{... | collective-permute-start | bytes 786440 | tf_op jit(solution)/shard_map/ppermute | solution.py:33
  62.4 7.6 %collective-permute-start.12 = (bf16[32,4096]{1,0:T(8,128)(2,1)S(1)}, bf16[32,4096]{1,0:T(8,128)(2,1)S(1)}, u32[]{:S(2)}, u32[]{:S(2)}) collective-permute-start(bf16[32,4096]{1,0:T(8,128)(2,1)S(1)} %get-tuple-element.60), channel_id=1, source_target_pairs={{0,8},{1,15},{8,2},{9,1},{2,10},{3,9},{10,4},{11,3},{4,12},{5,11},... | collective-permute-start | bytes 786440 | tf_op jit(solution)/shard_map/ppermute | solution.py:41
  71.0 17.9 %all-to-all-start.1 = ((bf16[8,2,4,4096]{3,2,1,0:T(4,128)(2,1)}), bf16[8,2,4,4096]{3,2,1,0:T(4,128)(2,1)S(1)}, u32[]{:S(2)}, u32[]{:S(2)}) async-start(bf16[8,2,4,4096]{3,2,1,0:T(4,128)(2,1)} %shard_map.96), calls=%async_computation.1 | async-start | bytes 1048576 | tf_op jit(solution)/shard_map/all_to_all | solution.py:45
  75.7 4.4 %collective-permute-start.13 = (bf16[2,32,4096]{2,1,0:T(8,128)(2,1)S(1)}, bf16[2,32,4096]{2,1,0:T(8,128)(2,1)S(1)}, u32[]{:S(2)}, u32[]{:S(2)}) collective-permute-start(bf16[2,32,4096]{2,1,0:T(8,128)(2,1)S(1)} %shard_map.92.refs_0_), channel_id=1, source_target_pairs={{0,1},{1,0},{8,9},{9,8},{2,3},{3,2},{10,11},{11,10},{4,5},{5,4},{1... | collective-permute-start | bytes 1572872 | tf_op jit(solution)/shard_map/ppermute | solution.py:29
  75.7 4.4 %collective-permute-start.14 = (bf16[2,32,4096]{2,1,0:T(8,128)(2,1)S(1)}, bf16[2,32,4096]{2,1,0:T(8,128)(2,1)S(1)}, u32[]{:S(2)}, u32[]{:S(2)}) collective-permute-start(bf16[2,32,4096]{2,1,0:T(8,128)(2,1)S(1)} %collective-permute-done.4.refs_1_), channel_id=1, source_target_pairs={{0,1},{1,0},{8,9},{9,8},{2,3},{3,2},{10,11},{11,10},{4,5},{5,4},{1... | collective-permute-start | bytes 1572872 | tf_op jit(solution)/shard_map/ppermute | solution.py:29
  76.2 3.9 %collective-permute-start.15 = (bf16[2,32,4096]{2,1,0:T(8,128)(2,1)S(1)}, bf16[2,32,4096]{2,1,0:T(8,128)(2,1)S(1)}, u32[]{:S(2)}, u32[]{:S(2)}) collective-permute-start(bf16[2,32,4096]{2,1,0:T(8,128)(2,1)S(1)} %collective-permute-done.6.refs_2_), channel_id=1, source_target_pairs={{0,1},{1,0},{8,9},{9,8},{2,3},{3,2},{10,11},{11,10},{4,5},{5,4},{1... | collective-permute-start | bytes 1572872 | tf_op jit(solution)/shard_map/ppermute | solution.py:29
  76.3 3.9 %collective-permute-start.16 = (bf16[2,32,4096]{2,1,0:T(8,128)(2,1)S(1)}, bf16[2,32,4096]{2,1,0:T(8,128)(2,1)S(1)}, u32[]{:S(2)}, u32[]{:S(2)}) collective-permute-start(bf16[2,32,4096]{2,1,0:T(8,128)(2,1)S(1)} %collective-permute-done.5.refs_3_), channel_id=1, source_target_pairs={{0,1},{1,0},{8,9},{9,8},{2,3},{3,2},{10,11},{11,10},{4,5},{5,4},{1... | collective-permute-start | bytes 1572872 | tf_op jit(solution)/shard_map/ppermute | solution.py:29
  76.7 3.4 %collective-permute-start.17 = (bf16[3,128,256]{2,1,0:T(8,128)(2,1)S(1)}, bf16[3,128,256]{2,1,0:T(8,128)(2,1)S(1)}, u32[]{:S(2)}, u32[]{:S(2)}) collective-permute-start(bf16[3,128,256]{2,1,0:T(8,128)(2,1)S(1)} %get-tuple-element.69), channel_id=1, source_target_pairs={{0,1},{1,0},{8,9},{9,8},{2,3},{3,2},{10,11},{11,10},{4,5},{5,4},{1... | collective-permute-start | bytes 589832 | tf_op jit(solution)/shard_map/ppermute | solution.py:29
  89.8 5.1 %collective-permute-start.18 = (bf16[4,4096]{1,0:T(4,128)(2,1)S(1)}, bf16[4,4096]{1,0:T(4,128)(2,1)S(1)}, u32[]{:S(2)}, u32[]{:S(2)}) collective-permute-start(bf16[4,4096]{1,0:T(4,128)(2,1)S(1)} %get-tuple-element.77), channel_id=1, source_target_pairs={{0,192},{64,0},{128,64},{192,128},{1,193},{65,1},{129,65},{193,129... | collective-permute-start | bytes 98312 | tf_op jit(solution)/shard_map/ppermute | solution.py:50

commit v4 on v3

--- a/solution.py
+++ b/solution.py
@@ -65,7 +65,7 @@
         in_specs=[pl.BlockSpec(memory_space=pltpu.VMEM)] * len(args),
         out_specs=[pl.BlockSpec(memory_space=pltpu.VMEM)] * len(shapes),
         scratch_shapes=list(scratch),
-        compiler_params=pltpu.CompilerParams(vmem_limit_bytes=32 * 2**20),
+        compiler_params=pltpu.CompilerParams(vmem_limit_bytes=24 * 2**20),
         cost_estimate=pl.CostEstimate(flops=0, bytes_accessed=0, transcendentals=0),
     )(*args)
 
@@ -94,6 +94,17 @@
 
 def after(x, *earlier):
     return lax.optimization_barrier((x, *earlier))[0]
+
+
+def fan_body(layer, cotangent, fan):
+    for i in range(NZ):
+        fan[i, 0] = layer[...]
+        fan[i, 1] = cotangent[0]
+
+
+def total_body(arrived, output, back):
+    for kind, total in enumerate((output, back)):
+        total[0] = sum(arrived[i, kind].astype(F32) for i in range(NZ)).astype(BF16)
 
 
 def split_body(got_ref, own_ref):
@@ -132,26 +143,42 @@
         put_sums(sums, columns, *sends)
 
 
+def turn_body(gate_w, up_w, gate_x, up_x, down_w, down_x, across, down):
+    units = gate_w.shape[2]
+    for i, source in enumerate((gate_w, up_w, gate_x, up_x)):
+
+        @pl.loop(0, source.shape[1], step=CHUNK)
+        def _(start):
+            columns = pl.ds(pl.multiple_of(start, CHUNK), CHUNK)
+            across[i * units : (i + 1) * units, columns] = source[0, columns, :].T
+
+    for i, source in enumerate((down_w, down_x)):
+
+        @pl.loop(0, source.shape[2], step=CHUNK)
+        def _(start):
+            columns = pl.ds(pl.multiple_of(start, CHUNK), CHUNK)
+            down[columns, i * units : (i + 1) * units] = source[0, :, columns].T
+
+
 def backward_body(*refs):
-    blocks, gate_ws, up_ws, down_ws, (swish, rise, hidden) = refs[:4], refs[4:6], refs[6:8], refs[8:10], refs[10:13]
-    gate_grads, up_grads, sends, cotangent = (refs[13], refs[15].at[0]), (refs[14], refs[15].at[1]), refs[16:20], refs[20]
-    refs[15][2] = hidden[...]
+    blocks, across, down, (swish, rise, hidden) = refs[:4], refs[4], refs[5], refs[6:9]
+    gate_grad, up_grad, give, sends, cotangent, grads = refs[9], refs[10], refs[11], refs[12:16], refs[16], refs[17]
+    units = hidden.shape[1]
+    give[2] = hidden[...]
     for i, block in enumerate(blocks):
         cotangent[32 * i : 32 * i + 32, :] = block[1]
-    for core in (0, 1):
-        hidden_grad = contract_cols(cotangent[...], down_ws[core][0])
-        gate_grads[core][...] = (hidden_grad * rise[core]).astype(BF16)
-        up_grads[core][...] = (hidden_grad * swish[core]).astype(BF16)
-
-    @pl.loop(0, gate_ws[0].shape[1], step=CHUNK)
+    hidden_grads = jnp.dot(cotangent[...], down[...], preferred_element_type=F32)
+    for core, (to_gate, to_up) in enumerate(((gate_grad, up_grad), (give.at[0], give.at[1]))):
+        hidden_grad = hidden_grads[:, core * units : (core + 1) * units]
+        to_gate[...] = (hidden_grad * rise[core]).astype(BF16)
+        to_up[...] = (hidden_grad * swish[core]).astype(BF16)
+        grads[:, 2 * core * units : (2 * core + 1) * units] = to_gate[...]
+        grads[:, (2 * core + 1) * units : 2 * (core + 1) * units] = to_up[...]
+
+    @pl.loop(0, across.shape[1], step=CHUNK)
     def _(start):
         columns = pl.ds(pl.multiple_of(start, CHUNK), CHUNK)
-        sums = sum(
-            contract_cols(gate_grads[core][...], gate_ws[core][0, columns, :])
-            + contract_cols(up_grads[core][...], up_ws[core][0, columns, :])
-            for core in (0, 1)
-        )
-        put_sums(sums, columns, *sends)
+        put_sums(jnp.dot(grads[...], across[:, columns], preferred_element_type=F32), columns, *sends)
 
 
 def weight_grads_body(*refs):
@@ -182,7 +209,7 @@
         out_shape=[jax.ShapeDtypeStruct(shape, BF16) for shape in shapes],
         in_specs=streamed + whole,
         out_specs=across + along,
-        compiler_params=pltpu.CompilerParams(vmem_limit_bytes=32 * 2**20),
+        compiler_params=pltpu.CompilerParams(vmem_limit_bytes=24 * 2**20),
         cost_estimate=pl.CostEstimate(flops=0, bytes_accessed=0, transcendentals=0),
     )(*args)
 
@@ -206,19 +233,22 @@
 
 def on_device(activations, w_gate, w_up, w_down, out_grad):
     arrived = from_behind(activations[0], "section", 1)
-    mine = jnp.stack([arrived, out_grad[0]])
-    _, rows, width = mine.shape
+    rows, width = arrived.shape
     units = w_down.shape[1]
     tokens = NY * NZ * rows
-    got = colour_all_to_all(jnp.broadcast_to(mine[None], (NZ,) + mine.shape))
+    (mine,) = local_kernel(fan_body, [((NZ, 2, rows, width), BF16)], arrived, out_grad)
+    got = colour_all_to_all(mine)
 
     got, *partner = lax.optimization_barrier((got, swap(w_gate), swap(w_up), swap(w_down)))
 
     (own,) = local_kernel(split_body, [((2, NZ * rows, width), BF16)], got)
     step, last, next_ = z_step(own), y_last(own), y_next(own)
-    loaded = load(after(w_gate, step), w_up, w_down)
-    blocks = [own, after(next_, loaded[0]), last, step]
+    loaded = load(after(w_gate, own), w_up, w_down)
     weights = [w for pair in zip(loaded, partner) for w in pair]
+    turned = local_kernel(
+        turn_body, [((4 * units, width), BF16), ((width, 2 * units), BF16)],
+        loaded[0], loaded[1], partner[0], partner[1], loaded[2], partner[2])
+    blocks = [own, after(next_, *turned), last, step]
 
     send = ((NZ * rows, width), BF16)
     sends = [((NZ * rows, width), F32), send, send, send]
@@ -230,7 +260,8 @@
     out_terms = send_sums(*out_sums)
     gate_grad, up_grad, give, *back_sums = local_kernel(
         backward_body, [some, some, ((3, tokens, units), BF16), *sends],
-        *blocks, *weights, swish, rise, hidden_other, scratch=scratch)
+        *blocks, *turned, swish, rise, hidden_other,
+        scratch=scratch + [pltpu.VMEM((tokens, 4 * units), BF16)])
     back_terms = send_sums(*back_sums)
 
     (sums,) = local_kernel(join_body, [((NZ, 2, rows, width), BF16)], *out_terms, *back_terms)
@@ -240,9 +271,8 @@
         *blocks, *[swap(block) for block in blocks], gate_grad, up_grad, hidden, swap(give))
     arrived = colour_all_to_all(sums)
     arrived, grad_gate, grad_up, grad_down = lax.optimization_barrier((arrived, grad_gate, grad_up, grad_down))
-    final = jnp.sum(arrived.astype(F32), 0).astype(BF16)
-    returned = from_behind(final[1], "section", -1)
-    return (final[0][None], returned[None], grad_gate, grad_up, grad_down)
+    output, back = local_kernel(total_body, [((1, rows, width), BF16)] * 2, arrived)
+    return (output, from_behind(back, "section", -1), grad_gate, grad_up, grad_down)
 
 
 def solution(mesh):

time: 95.9 us -> 93.4 us (0.974)
  waiting for transfers between devices: 25.9 us -> 19.7 us
  Pallas kernels: 14.5 us -> 17.8 us
  starting transfers between devices: 21.3 us -> 22.4 us
  other arithmetic: 1.05 us -> 0 us
    ppermute x3, waiting for transfers between devices: 6.24 us -> 0.01 us  [z_step(): return lax.ppermute(x, PLANE, Z_STEP)]
    pallas_call x4 -> x7, Pallas kernels: 8.49 us -> 11.7 us  [local_kernel(): pl.pallas_call(body, out_shape=[jax.ShapeDtypeStruct(shape, dtype) for sh...]
    ppermute x3, starting transfers between devices: 7.69 us -> 8.74 us  [y_last(): return lax.ppermute(x, PLANE, Y_LAST)]
    unnamed x7 -> x9, local copies, waits for them, and re-layouts: 3.8 us -> 4.56 us
  transfers between devices with their start and end apart: 20 -> 20, of which waited for: 7 -> 7; matrix products, arithmetic and copies ran while one was open for 1% -> 0% of each run, Pallas kernels for 11% -> 14%
where the time goes in v4:
time: 93.4 us; the launch traced here: 92.6 us
  blocking collectives  27.4 us (29%)
  starting transfers between devices  22.4 us (24%)
  waiting for transfers between devices  19.7 us (21%)
  Pallas kernels  17.8 us (19%)
  local copies, waits for them, and re-layouts  4.56 us (5%)
    all_to_all x1, blocking collectives, colour_all_to_all(): return lax.all_to_all(x, PLANE, 0, 0, axis_index_groups=COLOURS)  27.4 us
    pallas_call x7, Pallas kernels, local_kernel(): pl.pallas_call(body, out_shape=[jax.ShapeDtypeStruct(shape, dtype) for sh...  11.7 us
    ppermute x3, starting transfers between devices, y_last(): return lax.ppermute(x, PLANE, Y_LAST)  8.74 us
    ppermute x2, waiting for transfers between devices, from_behind(): lax.ppermute(x, axis, [(i, (i + by) % length) for i in range(length)])  6.2 us
    pallas_call x1, Pallas kernels, weight_grads(): pl.pallas_call(weight_grads_body, grid=(width // part,), out_shape=[jax.S...  5.61 us
    all_to_all x1, starting transfers between devices, colour_all_to_all(): return lax.all_to_all(x, PLANE, 0, 0, axis_index_groups=COLOURS)  4.62 us
    unnamed x9, local copies, waits for them, and re-layouts  4.56 us
    ppermute x3, waiting for transfers between devices, y_next(): return lax.ppermute(x, PLANE, Y_NEXT)  4.08 us
  transfers between devices with their start and end apart: 20, of which 7 were waited for; matrix products, arithmetic and copies ran while one was open for 0% of the time, Pallas kernels for 14%

profile of v4, /device:TPU:6, one launch (start us, length us, event | category | flops | bytes accessed | tf_op | source)
XLA Modules:
  0.0 92.6 jit_solution(15914933535628077213)
XLA Ops:
  1.3 2.2 %collective-permute-start = (bf16[4,4096]{1,0:T(4,128)(2,1)}, bf16[4,4096]{1,0:T(4,128)(2,1)S(1)}, u32[]{:S(2)}, u32[]{:S(2)}) collective-permute-start(bf16[4,4096]{1,0:T(4,128)(2,1)} %bitcast.1), channel_id=1, source_target_pairs={{0,64},{64,128},{128,192},{192,0},{1,65},{65,129},{129,193},{193,1... | collective-permute-start | bytes 98312 | tf_op jit(solution)/shard_map/ppermute | solution.py:50
  3.6 1.9 %collective-permute-done.layer = bf16[4,4096]{1,0:T(4,128)(2,1)S(1)} collective-permute-done((bf16[4,4096]{1,0:T(4,128)(2,1)}, bf16[4,4096]{1,0:T(4,128)(2,1)S(1)}, u32[]{:S(2)}, u32[]{:S(2)}) %collective-permute-start) | collective-permute-done | bytes 32800 | tf_op jit(solution)/shard_map/ppermute | solution.py:50
  5.5 0.8 copy-done.3
  6.3 27.4 %all_to_all.10.got_ref = bf16[8,2,4,4096]{3,2,1,0:T(4,128)(2,1)S(1)} all-to-all(bf16[8,2,4,4096]{3,2,1,0:T(4,128)(2,1)S(1)} %shard_map.92), channel_id=1, replica_groups={{0,40,2,42,4,44,6,46},{1,41,3,43,5,45,7,47},{16,56,18,58,20,60,22,62},{..., dimensions={0} | all-to-all | bytes 1048576 | tf_op jit(solution)/shard_map/all_to_all | solution.py:45
  33.8 0.8 collective-permute-start.4
  34.5 1.1 %collective-permute-start.6 = (bf16[2,32,4096]{2,1,0:T(8,128)(2,1)S(1)}, bf16[2,32,4096]{2,1,0:T(8,128)(2,1)S(1)}, u32[]{:S(2)}, u32[]{:S(2)}) collective-permute-start(bf16[2,32,4096]{2,1,0:T(8,128)(2,1)S(1)} %shard_map.93.refs_0_), channel_id=1, source_target_pairs={{0,8},{1,15},{8,2},{9,1},{2,10},{3,9},{10,4},{11,3},{4,12},{5,11},... | collective-permute-start | bytes 1572872 | tf_op jit(solution)/shard_map/ppermute | solution.py:41
  35.6 2.4 %collective-permute-start.5 = (bf16[2,32,4096]{2,1,0:T(8,128)(2,1)S(1)}, bf16[2,32,4096]{2,1,0:T(8,128)(2,1)S(1)}, u32[]{:S(2)}, u32[]{:S(2)}) collective-permute-start(bf16[2,32,4096]{2,1,0:T(8,128)(2,1)S(1)} %shard_map.93.refs_0_), channel_id=1, source_target_pairs={{0,48},{1,49},{8,56},{9,57},{2,50},{3,51},{10,58},{11,59},{4,52},{... | collective-permute-start | bytes 1572872 | tf_op jit(solution)/shard_map/ppermute | solution.py:37
  38.0 1.6 %copy-done.1 = bf16[1,4096,256]{2,1,0:T(8,128)(2,1)S(1)} copy-done((bf16[1,4096,256]{2,1,0:T(8,128)(2,1)S(1)}, bf16[1,4096,256]{2,1,0:T(8,128)(2,1)}, u32[]{:S(2)}) %copy-start.1) | copy-done | bytes 2097176
  39.6 1.6 %copy-done.2 = bf16[1,256,4096]{2,1,0:T(8,128)(2,1)S(1)} copy-done((bf16[1,256,4096]{2,1,0:T(8,128)(2,1)S(1)}, bf16[1,256,4096]{2,1,0:T(8,128)(2,1)}, u32[]{:S(2)}) %copy-start.2) | copy-done | bytes 2097176
  41.7 4.7 %shard_map.95 = (bf16[1024,4096]{1,0:T(8,128)(2,1)S(1)}, bf16[4096,512]{1,0:T(8,128)(2,1)S(1)}) custom-call(bf16[1,4096,256]{2,1,0:T(8,128)(2,1)S(1)} %get-tuple-element.47.gate_w.refs_4_, bf16[1,4096,256]{2,1,0:T(8,128)(2,1)S(1)} %get-tuple-element.48.up_w.refs_6_, bf16[1,4096,256]{2,1,0:T(8,128)(2,1)S(1)} %collective-permute-done.1.gate_x.refs_5_, ...), custom_call_target="tpu_custom_call" | custom-call | tf_op jit(solution)/shard_map/pallas_call | solution.py:62
  46.8 2.5 %shard_map.96 = (bf16[128,256]{1,0:T(8,128)(2,1)S(1)}, bf16[128,256]{1,0:T(8,128)(2,1)S(1)}, f32[2,128,256]{2,1,0:T(8,128)S(1)}, f32[2,128,256]{2,1,0:T(8,128)S(...) custom-call(bf16[2,32,4096]{2,1,0:T(8,128)(2,1)S(1)} %shard_map.93.r, ...), custom_call_target="tpu_custom_call" | custom-call | tf_op jit(solution)/shard_map/pallas_call | solution.py:62
  49.3 3.0 %collective-permute-start.7 = (bf16[32,4096]{1,0:T(8,128)(2,1)S(1)}, bf16[32,4096]{1,0:T(8,128)(2,1)S(1)}, u32[]{:S(2)}, u32[]{:S(2)}) collective-permute-start(bf16[32,4096]{1,0:T(8,128)(2,1)S(1)} %get-tuple-element.57), channel_id=1, source_target_pairs={{0,48},{1,49},{8,56},{9,57},{2,50},{3,51},{10,58},{11,59},{4,52},{... | collective-permute-start | bytes 786440 | tf_op jit(solution)/shard_map/ppermute | solution.py:37
  52.4 1.7 %collective-permute-start.9 = (bf16[32,4096]{1,0:T(8,128)(2,1)S(1)}, bf16[32,4096]{1,0:T(8,128)(2,1)S(1)}, u32[]{:S(2)}, u32[]{:S(2)}) collective-permute-start(bf16[32,4096]{1,0:T(8,128)(2,1)S(1)} %get-tuple-element.59), channel_id=1, source_target_pairs={{0,8},{1,15},{8,2},{9,1},{2,10},{3,9},{10,4},{11,3},{4,12},{5,11},... | collective-permute-start | bytes 786440 | tf_op jit(solution)/shard_map/ppermute | solution.py:41
  54.1 2.6 %shard_map.97 = (bf16[128,256]{1,0:T(8,128)(2,1)S(1)}, bf16[128,256]{1,0:T(8,128)(2,1)S(1)}, bf16[3,128,256]{2,1,0:T(8,128)(2,1)S(1)}, f32[32,4096]{1,0:T(8,128)...) custom-call(bf16[2,32,4096]{2,1,0:T(8,128)(2,1)S(1)} %shard_map.93.refs_0_, ...), custom_call_target="tpu_custom_call" | custom-call | tf_op jit(solution)/shard_map/pallas_call | solution.py:62
  56.7 3.3 %collective-permute-start.10 = (bf16[32,4096]{1,0:T(8,128)(2,1)S(1)}, bf16[32,4096]{1,0:T(8,128)(2,1)S(1)}, u32[]{:S(2)}, u32[]{:S(2)}) collective-permute-start(bf16[32,4096]{1,0:T(8,128)(2,1)S(1)} %get-tuple-element.64), channel_id=1, source_target_pairs={{0,48},{1,49},{8,56},{9,57},{2,50},{3,51},{10,58},{11,59},{4,52},{... | collective-permute-start | bytes 786440 | tf_op jit(solution)/shard_map/ppermute | solution.py:37
  60.7 3.2 %collective-permute-done.10.refs_5_ = bf16[32,4096]{1,0:T(8,128)(2,1)S(1)} collective-permute-done((bf16[32,4096]{1,0:T(8,128)(2,1)S(1)}, bf16[32,4096]{1,0:T(8,128)(2,1)S(1)}, u32[]{:S(2)}, u32[]{:S(2)}) %collective-permute-start.10) | collective-permute-done | bytes 262176 | tf_op jit(solution)/shard_map/ppermute | solution.py:37
  63.8 3.7 %collective-permute-done.11.refs_6_ = bf16[32,4096]{1,0:T(8,128)(2,1)S(1)} collective-permute-done((bf16[32,4096]{1,0:T(8,128)(2,1)S(1)}, bf16[32,4096]{1,0:T(8,128)(2,1)S(1)}, u32[]{:S(2)}, u32[]{:S(2)}) %collective-permute-start.11) | collective-permute-done | bytes 262176 | tf_op jit(solution)/shard_map/ppermute | solution.py:33
  67.5 1.1 %shard_map.98 = bf16[8,2,4,4096]{3,2,1,0:T(4,128)(2,1)} custom-call(f32[32,4096]{1,0:T(8,128)S(1)} %get-tuple-element.56.refs_0_, bf16[32,4096]{1,0:T(8,128)(2,1)S(1)} %collective-permute-done.7.refs_1_, bf16[32,4096]{1,0:T(8,128)(2,1)S(1)} %collective-permute-done.8.refs_2_, bf16[32,4096]{1,0:T(8,128)(2,1)S(1)} %collective-permute-done.9.refs_3_, ...), custom_call_target="tpu_custom_call" | custom-call | tf_op jit(solution)/shard_map/pallas_call | solution.py:62
  68.6 4.6 %all-to-all-start.1 = ((bf16[8,2,4,4096]{3,2,1,0:T(4,128)(2,1)}), bf16[8,2,4,4096]{3,2,1,0:T(4,128)(2,1)S(1)}, u32[]{:S(2)}, u32[]{:S(2)}) async-start(bf16[8,2,4,4096]{3,2,1,0:T(4,128)(2,1)} %shard_map.98), calls=%async_computation.1 | async-start | bytes 1048576 | tf_op jit(solution)/shard_map/all_to_all | solution.py:45
  74.4 3.3 %collective-permute-done.17.refs_11_ = bf16[3,128,256]{2,1,0:T(8,128)(2,1)S(1)} collective-permute-done((bf16[3,128,256]{2,1,0:T(8,128)(2,1)S(1)}, bf16[3,128,256]{2,1,0:T(8,128)(2,1)S(1)}, u32[]{:S(2)}, u32[]{:S(2)}) %collective-permute-start.17) | collective-permute-done | bytes 196640 | tf_op jit(solution)/shard_map/ppermute | solution.py:29
  77.7 5.6 %shard_map.99 = (bf16[1,4096,256]{2,1,0:T(8,128)(2,1)}, bf16[1,4096,256]{2,1,0:T(8,128)(2,1)}, bf16[1,256,4096]{2,1,0:T(8,128)(2,1)}) custom-call(bf16[2,32,4096]{2,1,0:T(8,128)(2,1)S(1)} %shard_map.93.refs_0_, bf16[2,32,4096]{2,1,0:T(8,128)(2,1)S(1)} %collective-permute-done.4.refs_1_, bf16[2,32,4096]{2,1,0:T(8,128)(2,1)S(1)} %collective-permute-done.5.refs_2_, ...), custom_call_target="tpu_custom_call" | custom-call | tf_op jit(solution)/shard_map/pallas_call | solution.py:206
  83.3 2.8 %all-to-all-done.1.arrived = bf16[8,2,4,4096]{3,2,1,0:T(4,128)(2,1)S(1)} async-done(((bf16[8,2,4,4096]{3,2,1,0:T(4,128)(2,1)}), bf16[8,2,4,4096]{3,2,1,0:T(4,128)(2,1)S(1)}, u32[]{:S(2)}, u32[]{:S(2)}) %all-to-all-start.1) | async-done | bytes 524320 | tf_op jit(solution)/shard_map/all_to_all | solution.py:45
  86.8 0.8 collective-permute-start.18
  87.6 4.3 %collective-permute-done.18 = bf16[1,4,4096]{2,1,0:T(4,128)(2,1)S(1)} collective-permute-done((bf16[1,4,4096]{2,1,0:T(4,128)(2,1)S(1)}, bf16[1,4,4096]{2,1,0:T(4,128)(2,1)S(1)}, u32[]{:S(2)}, u32[]{:S(2)}) %collective-permute-start.18) | collective-permute-done | bytes 32800 | tf_op jit(solution)/shard_map/ppermute | solution.py:50
  (35 shorter events, 4.8 us)
Async XLA Ops:
  0.6 37.4 %copy-start = (bf16[1,4096,256]{2,1,0:T(8,128)(2,1)S(1)}, bf16[1,4096,256]{2,1,0:T(8,128)(2,1)}, u32[]{:S(2)}) copy-start(bf16[1,4096,256]{2,1,0:T(8,128)(2,1)} %refs_0_) | copy-start | bytes 6291460
  0.6 33.0 %collective-permute-start.1 = (bf16[1,4096,256]{2,1,0:T(8,128)(2,1)}, bf16[1,4096,256]{2,1,0:T(8,128)(2,1)S(1)}, u32[]{:S(2)}, u32[]{:S(2)}) collective-permute-start(bf16[1,4096,256]{2,1,0:T(8,128)(2,1)} %refs_0_), channel_id=1, source_target_pairs={{0,1},{1,0},{8,9},{9,8},{2,3},{3,2},{10,11},{11,10},{4,5},{5,4},{1... | collective-permute-start | bytes 6291464 | tf_op jit(solution)/shard_map/ppermute | solution.py:29
  0.7 32.9 %collective-permute-start.2 = (bf16[1,4096,256]{2,1,0:T(8,128)(2,1)}, bf16[1,4096,256]{2,1,0:T(8,128)(2,1)S(1)}, u32[]{:S(2)}, u32[]{:S(2)}) collective-permute-start(bf16[1,4096,256]{2,1,0:T(8,128)(2,1)} %refs_1_.1), channel_id=1, source_target_pairs={{0,1},{1,0},{8,9},{9,8},{2,3},{3,2},{10,11},{11,10},{4,5},{5,4},{1... | collective-permute-start | bytes 6291464 | tf_op jit(solution)/shard_map/ppermute | solution.py:29
  1.2 32.4 %collective-permute-start.3 = (bf16[1,256,4096]{2,1,0:T(8,128)(2,1)}, bf16[1,256,4096]{2,1,0:T(8,128)(2,1)S(1)}, u32[]{:S(2)}, u32[]{:S(2)}) collective-permute-start(bf16[1,256,4096]{2,1,0:T(8,128)(2,1)} %refs_2_.1), channel_id=1, source_target_pairs={{0,1},{1,0},{8,9},{9,8},{2,3},{3,2},{10,11},{11,10},{4,5},{5,4},{1... | collective-permute-start | bytes 6291464 | tf_op jit(solution)/shard_map/ppermute | solution.py:29
  1.3 4.1 %collective-permute-start = (bf16[4,4096]{1,0:T(4,128)(2,1)}, bf16[4,4096]{1,0:T(4,128)(2,1)S(1)}, u32[]{:S(2)}, u32[]{:S(2)}) collective-permute-start(bf16[4,4096]{1,0:T(4,128)(2,1)} %bitcast.1), channel_id=1, source_target_pairs={{0,64},{64,128},{128,192},{192,0},{1,65},{65,129},{129,193},{193,1... | collective-permute-start | bytes 98312 | tf_op jit(solution)/shard_map/ppermute | solution.py:50
  5.5 0.8 copy-start.3
  33.8 13.0 %collective-permute-start.4 = (bf16[2,32,4096]{2,1,0:T(8,128)(2,1)S(1)}, bf16[2,32,4096]{2,1,0:T(8,128)(2,1)S(1)}, u32[]{:S(2)}, u32[]{:S(2)}) collective-permute-start(bf16[2,32,4096]{2,1,0:T(8,128)(2,1)S(1)} %shard_map.93.refs_0_), channel_id=1, source_target_pairs={{0,16},{1,17},{8,24},{9,25},{2,18},{3,19},{10,26},{11,27},{4,20},{... | collective-permute-start | bytes 1572872 | tf_op jit(solution)/shard_map/ppermute | solution.py:33
  34.5 12.2 %collective-permute-start.6 = (bf16[2,32,4096]{2,1,0:T(8,128)(2,1)S(1)}, bf16[2,32,4096]{2,1,0:T(8,128)(2,1)S(1)}, u32[]{:S(2)}, u32[]{:S(2)}) collective-permute-start(bf16[2,32,4096]{2,1,0:T(8,128)(2,1)S(1)} %shard_map.93.refs_0_), channel_id=1, source_target_pairs={{0,8},{1,15},{8,2},{9,1},{2,10},{3,9},{10,4},{11,3},{4,12},{5,11},... | collective-permute-start | bytes 1572872 | tf_op jit(solution)/shard_map/ppermute | solution.py:41
  35.6 11.2 %collective-permute-start.5 = (bf16[2,32,4096]{2,1,0:T(8,128)(2,1)S(1)}, bf16[2,32,4096]{2,1,0:T(8,128)(2,1)S(1)}, u32[]{:S(2)}, u32[]{:S(2)}) collective-permute-start(bf16[2,32,4096]{2,1,0:T(8,128)(2,1)S(1)} %shard_map.93.refs_0_), channel_id=1, source_target_pairs={{0,48},{1,49},{8,56},{9,57},{2,50},{3,51},{10,58},{11,59},{4,52},{... | collective-permute-start | bytes 1572872 | tf_op jit(solution)/shard_map/ppermute | solution.py:37
  38.0 1.6 %copy-start.1 = (bf16[1,4096,256]{2,1,0:T(8,128)(2,1)S(1)}, bf16[1,4096,256]{2,1,0:T(8,128)(2,1)}, u32[]{:S(2)}) copy-start(bf16[1,4096,256]{2,1,0:T(8,128)(2,1)} %refs_1_.1) | copy-start | bytes 6291460
  39.6 1.6 %copy-start.2 = (bf16[1,256,4096]{2,1,0:T(8,128)(2,1)S(1)}, bf16[1,256,4096]{2,1,0:T(8,128)(2,1)}, u32[]{:S(2)}) copy-start(bf16[1,256,4096]{2,1,0:T(8,128)(2,1)} %refs_2_.1) | copy-start | bytes 6291460
  49.3 10.6 %collective-permute-start.7 = (bf16[32,4096]{1,0:T(8,128)(2,1)S(1)}, bf16[32,4096]{1,0:T(8,128)(2,1)S(1)}, u32[]{:S(2)}, u32[]{:S(2)}) collective-permute-start(bf16[32,4096]{1,0:T(8,128)(2,1)S(1)} %get-tuple-element.57), channel_id=1, source_target_pairs={{0,48},{1,49},{8,56},{9,57},{2,50},{3,51},{10,58},{11,59},{4,52},{... | collective-permute-start | bytes 786440 | tf_op jit(solution)/shard_map/ppermute | solution.py:37
  52.4 8.3 %collective-permute-start.8 = (bf16[32,4096]{1,0:T(8,128)(2,1)S(1)}, bf16[32,4096]{1,0:T(8,128)(2,1)S(1)}, u32[]{:S(2)}, u32[]{:S(2)}) collective-permute-start(bf16[32,4096]{1,0:T(8,128)(2,1)S(1)} %get-tuple-element.58), channel_id=1, source_target_pairs={{0,16},{1,17},{8,24},{9,25},{2,18},{3,19},{10,26},{11,27},{4,20},{... | collective-permute-start | bytes 786440 | tf_op jit(solution)/shard_map/ppermute | solution.py:33
  52.4 8.3 %collective-permute-start.9 = (bf16[32,4096]{1,0:T(8,128)(2,1)S(1)}, bf16[32,4096]{1,0:T(8,128)(2,1)S(1)}, u32[]{:S(2)}, u32[]{:S(2)}) collective-permute-start(bf16[32,4096]{1,0:T(8,128)(2,1)S(1)} %get-tuple-element.59), channel_id=1, source_target_pairs={{0,8},{1,15},{8,2},{9,1},{2,10},{3,9},{10,4},{11,3},{4,12},{5,11},... | collective-permute-start | bytes 786440 | tf_op jit(solution)/shard_map/ppermute | solution.py:41
  56.7 7.2 %collective-permute-start.10 = (bf16[32,4096]{1,0:T(8,128)(2,1)S(1)}, bf16[32,4096]{1,0:T(8,128)(2,1)S(1)}, u32[]{:S(2)}, u32[]{:S(2)}) collective-permute-start(bf16[32,4096]{1,0:T(8,128)(2,1)S(1)} %get-tuple-element.64), channel_id=1, source_target_pairs={{0,48},{1,49},{8,56},{9,57},{2,50},{3,51},{10,58},{11,59},{4,52},{... | collective-permute-start | bytes 786440 | tf_op jit(solution)/shard_map/ppermute | solution.py:37
  60.0 7.6 %collective-permute-start.11 = (bf16[32,4096]{1,0:T(8,128)(2,1)S(1)}, bf16[32,4096]{1,0:T(8,128)(2,1)S(1)}, u32[]{:S(2)}, u32[]{:S(2)}) collective-permute-start(bf16[32,4096]{1,0:T(8,128)(2,1)S(1)} %get-tuple-element.65), channel_id=1, source_target_pairs={{0,16},{1,17},{8,24},{9,25},{2,18},{3,19},{10,26},{11,27},{4,20},{... | collective-permute-start | bytes 786440 | tf_op jit(solution)/shard_map/ppermute | solution.py:33
  60.0 7.6 %collective-permute-start.12 = (bf16[32,4096]{1,0:T(8,128)(2,1)S(1)}, bf16[32,4096]{1,0:T(8,128)(2,1)S(1)}, u32[]{:S(2)}, u32[]{:S(2)}) collective-permute-start(bf16[32,4096]{1,0:T(8,128)(2,1)S(1)} %get-tuple-element.66), channel_id=1, source_target_pairs={{0,8},{1,15},{8,2},{9,1},{2,10},{3,9},{10,4},{11,3},{4,12},{5,11},... | collective-permute-start | bytes 786440 | tf_op jit(solution)/shard_map/ppermute | solution.py:41
  68.6 17.5 %all-to-all-start.1 = ((bf16[8,2,4,4096]{3,2,1,0:T(4,128)(2,1)}), bf16[8,2,4,4096]{3,2,1,0:T(4,128)(2,1)S(1)}, u32[]{:S(2)}, u32[]{:S(2)}) async-start(bf16[8,2,4,4096]{3,2,1,0:T(4,128)(2,1)} %shard_map.98), calls=%async_computation.1 | async-start | bytes 1048576 | tf_op jit(solution)/shard_map/all_to_all | solution.py:45
  73.2 4.4 %collective-permute-start.13 = (bf16[2,32,4096]{2,1,0:T(8,128)(2,1)S(1)}, bf16[2,32,4096]{2,1,0:T(8,128)(2,1)S(1)}, u32[]{:S(2)}, u32[]{:S(2)}) collective-permute-start(bf16[2,32,4096]{2,1,0:T(8,128)(2,1)S(1)} %shard_map.93.refs_0_), channel_id=1, source_target_pairs={{0,1},{1,0},{8,9},{9,8},{2,3},{3,2},{10,11},{11,10},{4,5},{5,4},{1... | collective-permute-start | bytes 1572872 | tf_op jit(solution)/shard_map/ppermute | solution.py:29
  73.3 4.4 %collective-permute-start.14 = (bf16[2,32,4096]{2,1,0:T(8,128)(2,1)S(1)}, bf16[2,32,4096]{2,1,0:T(8,128)(2,1)S(1)}, u32[]{:S(2)}, u32[]{:S(2)}) collective-permute-start(bf16[2,32,4096]{2,1,0:T(8,128)(2,1)S(1)} %collective-permute-done.4.refs_1_), channel_id=1, source_target_pairs={{0,1},{1,0},{8,9},{9,8},{2,3},{3,2},{10,11},{11,10},{4,5},{5,4},{1... | collective-permute-start | bytes 1572872 | tf_op jit(solution)/shard_map/ppermute | solution.py:29
  73.8 3.9 %collective-permute-start.15 = (bf16[2,32,4096]{2,1,0:T(8,128)(2,1)S(1)}, bf16[2,32,4096]{2,1,0:T(8,128)(2,1)S(1)}, u32[]{:S(2)}, u32[]{:S(2)}) collective-permute-start(bf16[2,32,4096]{2,1,0:T(8,128)(2,1)S(1)} %collective-permute-done.5.refs_2_), channel_id=1, source_target_pairs={{0,1},{1,0},{8,9},{9,8},{2,3},{3,2},{10,11},{11,10},{4,5},{5,4},{1... | collective-permute-start | bytes 1572872 | tf_op jit(solution)/shard_map/ppermute | solution.py:29
  73.9 3.9 %collective-permute-start.16 = (bf16[2,32,4096]{2,1,0:T(8,128)(2,1)S(1)}, bf16[2,32,4096]{2,1,0:T(8,128)(2,1)S(1)}, u32[]{:S(2)}, u32[]{:S(2)}) collective-permute-start(bf16[2,32,4096]{2,1,0:T(8,128)(2,1)S(1)} %collective-permute-done.6.refs_3_), channel_id=1, source_target_pairs={{0,1},{1,0},{8,9},{9,8},{2,3},{3,2},{10,11},{11,10},{4,5},{5,4},{1... | collective-permute-start | bytes 1572872 | tf_op jit(solution)/shard_map/ppermute | solution.py:29
  74.3 3.4 %collective-permute-start.17 = (bf16[3,128,256]{2,1,0:T(8,128)(2,1)S(1)}, bf16[3,128,256]{2,1,0:T(8,128)(2,1)S(1)}, u32[]{:S(2)}, u32[]{:S(2)}) collective-permute-start(bf16[3,128,256]{2,1,0:T(8,128)(2,1)S(1)} %get-tuple-element.75), channel_id=1, source_target_pairs={{0,1},{1,0},{8,9},{9,8},{2,3},{3,2},{10,11},{11,10},{4,5},{5,4},{1... | collective-permute-start | bytes 589832 | tf_op jit(solution)/shard_map/ppermute | solution.py:29
  86.8 5.1 %collective-permute-start.18 = (bf16[1,4,4096]{2,1,0:T(4,128)(2,1)S(1)}, bf16[1,4,4096]{2,1,0:T(4,128)(2,1)S(1)}, u32[]{:S(2)}, u32[]{:S(2)}) collective-permute-start(bf16[1,4,4096]{2,1,0:T(4,128)(2,1)S(1)} %get-tuple-element.81), channel_id=1, source_target_pairs={{0,192},{64,0},{128,64},{192,128},{1,193},{65,1},{129,65},{193,129... | collective-permute-start | bytes 98312 | tf_op jit(solution)/shard_map/ppermute | solution.py:50

commit v5 on v4

--- a/solution.py
+++ b/solution.py
@@ -214,17 +214,30 @@
     )(*args)
 
 
-def join_body(*refs):
-    joined = refs[8]
-    for kind in (0, 1):
-        own, *received = refs[4 * kind : 4 * kind + 4]
-        for pair in range(NZ // 2):
-            rows = slice(8 * pair, 8 * pair + 8)
-            sums = own[rows, :]
-            for term in received:
-                sums = sums + term[rows, :].astype(F32)
-            for i in (0, 1):
-                joined[2 * pair + i, kind] = sums[4 * i : 4 * i + 4].astype(BF16)
+def add_terms(terms, joined, at):
+    own, *received = terms
+    for pair in range(NZ // 2):
+        rows = slice(8 * pair, 8 * pair + 8)
+        sums = own[rows, :]
+        for term in received:
+            sums = sums + term[rows, :].astype(F32)
+        for i in (0, 1):
+            joined[(2 * pair + i, *at)] = sums[4 * i : 4 * i + 4].astype(BF16)
+
+
+def out_total_body(*refs):
+    add_terms(refs[:4], refs[4], ())
+
+
+def join_body(out_total, *refs):
+    joined = refs[4]
+    for i in range(NZ):
+        joined[i, 0] = out_total[i]
+    add_terms(refs[:4], joined, (1,))
+
+
+def copy_body(source, target):
+    target[...] = source[...]
 
 
 def send_sums(own, last, next_, step):
@@ -236,19 +249,21 @@
     rows, width = arrived.shape
     units = w_down.shape[1]
     tokens = NY * NZ * rows
+    (out_grad,) = local_kernel(copy_body, [(out_grad.shape, BF16)], out_grad)
     (mine,) = local_kernel(fan_body, [((NZ, 2, rows, width), BF16)], arrived, out_grad)
     got = colour_all_to_all(mine)
 
     got, *partner = lax.optimization_barrier((got, swap(w_gate), swap(w_up), swap(w_down)))
 
     (own,) = local_kernel(split_body, [((2, NZ * rows, width), BF16)], got)
-    step, last, next_ = z_step(own), y_last(own), y_next(own)
+    next_, last, step = y_next(own), y_last(own), z_step(own)
     loaded = load(after(w_gate, own), w_up, w_down)
     weights = [w for pair in zip(loaded, partner) for w in pair]
     turned = local_kernel(
         turn_body, [((4 * units, width), BF16), ((width, 2 * units), BF16)],
         loaded[0], loaded[1], partner[0], partner[1], loaded[2], partner[2])
-    blocks = [own, after(next_, *turned), last, step]
+    next_, last = lax.optimization_barrier((next_, last, *turned))[:2]
+    blocks = [own, next_, last, step]
 
     send = ((NZ * rows, width), BF16)
     sends = [((NZ * rows, width), F32), send, send, send]
@@ -264,7 +279,8 @@
         scratch=scratch + [pltpu.VMEM((tokens, 4 * units), BF16)])
     back_terms = send_sums(*back_sums)
 
-    (sums,) = local_kernel(join_body, [((NZ, 2, rows, width), BF16)], *out_terms, *back_terms)
+    (out_total,) = local_kernel(out_total_body, [((NZ, rows, width), BF16)], *out_terms)
+    (sums,) = local_kernel(join_body, [((NZ, 2, rows, width), BF16)], out_total, *back_terms)
 
     *blocks, give = lax.optimization_barrier((*blocks, give, sums))[:-1]
     grad_gate, grad_up, grad_down = weight_grads(

time: 93.4 us -> 90.9 us (0.973)
  starting transfers between devices: 22.4 us -> 21 us
    ppermute x3, starting transfers between devices: 8.74 us -> 3.18 us  [y_last(): return lax.ppermute(x, PLANE, Y_LAST)]
    ppermute x3, starting transfers between devices: 0.76 us -> 3.13 us  [y_next(): return lax.ppermute(x, PLANE, Y_NEXT)]
    ppermute x3, starting transfers between devices: 3.48 us -> 5.28 us  [z_step(): return lax.ppermute(x, PLANE, Z_STEP)]
    ppermute x3, waiting for transfers between devices: 3.2 us -> 2.13 us  [y_last(): return lax.ppermute(x, PLANE, Y_LAST)]
    pallas_call x7 -> x9, Pallas kernels: 11.7 us -> 11.7 us  [local_kernel(): pl.pallas_call(body, out_shape=[jax.ShapeDtypeStruct(shape, dtype) for sh...]
  transfers between devices with their start and end apart: 20 -> 20, of which waited for: 7 -> 9; matrix products, arithmetic and copies ran while one was open for 0% -> 0% of each run, Pallas kernels for 14% -> 15%
where the time goes in v5:
time: 90.9 us; the launch traced here: 90.6 us
  blocking collectives  27.4 us (30%)
  starting transfers between devices  21 us (23%)
  waiting for transfers between devices  19.1 us (21%)
  Pallas kernels  17.8 us (20%)
  local copies, waits for them, and re-layouts  4.56 us (5%)
    all_to_all x1, blocking collectives, colour_all_to_all(): return lax.all_to_all(x, PLANE, 0, 0, axis_index_groups=COLOURS)  27.4 us
    pallas_call x9, Pallas kernels, local_kernel(): pl.pallas_call(body, out_shape=[jax.ShapeDtypeStruct(shape, dtype) for sh...  11.7 us
    pallas_call x1, Pallas kernels, weight_grads(): pl.pallas_call(weight_grads_body, grid=(width // part,), out_shape=[jax.S...  5.61 us
    ppermute x2, waiting for transfers between devices, from_behind(): lax.ppermute(x, axis, [(i, (i + by) % length) for i in range(length)])  5.43 us
    ppermute x3, starting transfers between devices, z_step(): return lax.ppermute(x, PLANE, Z_STEP)  5.28 us
    all_to_all x1, starting transfers between devices, colour_all_to_all(): return lax.all_to_all(x, PLANE, 0, 0, axis_index_groups=COLOURS)  4.57 us
    unnamed x9, local copies, waits for them, and re-layouts  4.56 us
    ppermute x3, waiting for transfers between devices, y_next(): return lax.ppermute(x, PLANE, Y_NEXT)  4.53 us
  transfers between devices with their start and end apart: 20, of which 9 were waited for; matrix products, arithmetic and copies ran while one was open for 0% of the time, Pallas kernels for 15%

profile of v5, /device:TPU:6, one launch (start us, length us, event | category | flops | bytes accessed | tf_op | source)
XLA Modules:
  0.0 90.6 jit_solution(5016869162418947443)
XLA Ops:
  1.3 2.2 %collective-permute-start = (bf16[4,4096]{1,0:T(4,128)(2,1)}, bf16[4,4096]{1,0:T(4,128)(2,1)S(1)}, u32[]{:S(2)}, u32[]{:S(2)}) collective-permute-start(bf16[4,4096]{1,0:T(4,128)(2,1)} %bitcast.1), channel_id=1, source_target_pairs={{0,64},{64,128},{128,192},{192,0},{1,65},{65,129},{129,193},{193,1... | collective-permute-start | bytes 98312 | tf_op jit(solution)/shard_map/ppermute | solution.py:50
  4.3 1.2 %collective-permute-done.layer = bf16[4,4096]{1,0:T(4,128)(2,1)S(1)} collective-permute-done((bf16[4,4096]{1,0:T(4,128)(2,1)}, bf16[4,4096]{1,0:T(4,128)(2,1)S(1)}, u32[]{:S(2)}, u32[]{:S(2)}) %collective-permute-start) | collective-permute-done | bytes 32800 | tf_op jit(solution)/shard_map/ppermute | solution.py:50
  5.5 27.4 %all_to_all.10.got_ref = bf16[8,2,4,4096]{3,2,1,0:T(4,128)(2,1)S(1)} all-to-all(bf16[8,2,4,4096]{3,2,1,0:T(4,128)(2,1)S(1)} %shard_map.93), channel_id=1, replica_groups={{0,40,2,42,4,44,6,46},{1,41,3,43,5,45,7,47},{16,56,18,58,20,60,22,62},{..., dimensions={0} | all-to-all | bytes 1048576 | tf_op jit(solution)/shard_map/all_to_all | solution.py:45
  33.5 1.6 %collective-permute-start.4 = (bf16[2,32,4096]{2,1,0:T(8,128)(2,1)S(1)}, bf16[2,32,4096]{2,1,0:T(8,128)(2,1)S(1)}, u32[]{:S(2)}, u32[]{:S(2)}) collective-permute-start(bf16[2,32,4096]{2,1,0:T(8,128)(2,1)S(1)} %shard_map.94.refs_0_), channel_id=1, source_target_pairs={{0,16},{1,17},{8,24},{9,25},{2,18},{3,19},{10,26},{11,27},{4,20},{... | collective-permute-start | bytes 1572872 | tf_op jit(solution)/shard_map/ppermute | solution.py:33
  35.1 0.9 %collective-permute-start.6 = (bf16[2,32,4096]{2,1,0:T(8,128)(2,1)S(1)}, bf16[2,32,4096]{2,1,0:T(8,128)(2,1)S(1)}, u32[]{:S(2)}, u32[]{:S(2)}) collective-permute-start(bf16[2,32,4096]{2,1,0:T(8,128)(2,1)S(1)} %shard_map.94.refs_0_), channel_id=1, source_target_pairs={{0,8},{1,15},{8,2},{9,1},{2,10},{3,9},{10,4},{11,3},{4,12},{5,11},... | collective-permute-start | bytes 1572872 | tf_op jit(solution)/shard_map/ppermute | solution.py:41
  36.1 1.6 %copy-done.1 = bf16[1,4096,256]{2,1,0:T(8,128)(2,1)S(1)} copy-done((bf16[1,4096,256]{2,1,0:T(8,128)(2,1)S(1)}, bf16[1,4096,256]{2,1,0:T(8,128)(2,1)}, u32[]{:S(2)}) %copy-start.1) | copy-done | bytes 2097176
  37.7 1.6 %copy-done.2 = bf16[1,256,4096]{2,1,0:T(8,128)(2,1)S(1)} copy-done((bf16[1,256,4096]{2,1,0:T(8,128)(2,1)S(1)}, bf16[1,256,4096]{2,1,0:T(8,128)(2,1)}, u32[]{:S(2)}) %copy-start.2) | copy-done | bytes 2097176
  39.7 4.7 %shard_map.96 = (bf16[1024,4096]{1,0:T(8,128)(2,1)S(1)}, bf16[4096,512]{1,0:T(8,128)(2,1)S(1)}) custom-call(bf16[1,4096,256]{2,1,0:T(8,128)(2,1)S(1)} %get-tuple-element.48.gate_w.refs_4_, bf16[1,4096,256]{2,1,0:T(8,128)(2,1)S(1)} %get-tuple-element.49.up_w.refs_6_, bf16[1,4096,256]{2,1,0:T(8,128)(2,1)S(1)} %collective-permute-done.1.gate_x.refs_5_, ...), custom_call_target="tpu_custom_call" | custom-call | tf_op jit(solution)/shard_map/pallas_call | solution.py:62
  44.8 1.7 %collective-permute-done.4.refs_1_ = bf16[2,32,4096]{2,1,0:T(8,128)(2,1)S(1)} collective-permute-done((bf16[2,32,4096]{2,1,0:T(8,128)(2,1)S(1)}, bf16[2,32,4096]{2,1,0:T(8,128)(2,1)S(1)}, u32[]{:S(2)}, u32[]{:S(2)}) %collective-permute-start.4) | collective-permute-done | bytes 524320 | tf_op jit(solution)/shard_map/ppermute | solution.py:33
  46.5 2.5 %shard_map.97 = (bf16[128,256]{1,0:T(8,128)(2,1)S(1)}, bf16[128,256]{1,0:T(8,128)(2,1)S(1)}, f32[2,128,256]{2,1,0:T(8,128)S(1)}, f32[2,128,256]{2,1,0:T(8,128)S(...) custom-call(bf16[2,32,4096]{2,1,0:T(8,128)(2,1)S(1)} %shard_map.94.r, ...), custom_call_target="tpu_custom_call" | custom-call | tf_op jit(solution)/shard_map/pallas_call | solution.py:62
  49.0 1.0 %collective-permute-start.7 = (bf16[32,4096]{1,0:T(8,128)(2,1)S(1)}, bf16[32,4096]{1,0:T(8,128)(2,1)S(1)}, u32[]{:S(2)}, u32[]{:S(2)}) collective-permute-start(bf16[32,4096]{1,0:T(8,128)(2,1)S(1)} %get-tuple-element.59), channel_id=1, source_target_pairs={{0,48},{1,49},{8,56},{9,57},{2,50},{3,51},{10,58},{11,59},{4,52},{... | collective-permute-start | bytes 786440 | tf_op jit(solution)/shard_map/ppermute | solution.py:37
  50.0 1.1 %collective-permute-start.8 = (bf16[32,4096]{1,0:T(8,128)(2,1)S(1)}, bf16[32,4096]{1,0:T(8,128)(2,1)S(1)}, u32[]{:S(2)}, u32[]{:S(2)}) collective-permute-start(bf16[32,4096]{1,0:T(8,128)(2,1)S(1)} %get-tuple-element.60), channel_id=1, source_target_pairs={{0,16},{1,17},{8,24},{9,25},{2,18},{3,19},{10,26},{11,27},{4,20},{... | collective-permute-start | bytes 786440 | tf_op jit(solution)/shard_map/ppermute | solution.py:33
  51.2 1.9 %collective-permute-start.9 = (bf16[32,4096]{1,0:T(8,128)(2,1)S(1)}, bf16[32,4096]{1,0:T(8,128)(2,1)S(1)}, u32[]{:S(2)}, u32[]{:S(2)}) collective-permute-start(bf16[32,4096]{1,0:T(8,128)(2,1)S(1)} %get-tuple-element.61), channel_id=1, source_target_pairs={{0,8},{1,15},{8,2},{9,1},{2,10},{3,9},{10,4},{11,3},{4,12},{5,11},... | collective-permute-start | bytes 786440 | tf_op jit(solution)/shard_map/ppermute | solution.py:41
  53.0 2.6 %shard_map.99 = (bf16[128,256]{1,0:T(8,128)(2,1)S(1)}, bf16[128,256]{1,0:T(8,128)(2,1)S(1)}, bf16[3,128,256]{2,1,0:T(8,128)(2,1)S(1)}, f32[32,4096]{1,0:T(8,128)...) custom-call(bf16[2,32,4096]{2,1,0:T(8,128)(2,1)S(1)} %shard_map.94.refs_0_, ...), custom_call_target="tpu_custom_call" | custom-call | tf_op jit(solution)/shard_map/pallas_call | solution.py:62
  55.6 1.7 %collective-permute-start.10 = (bf16[32,4096]{1,0:T(8,128)(2,1)S(1)}, bf16[32,4096]{1,0:T(8,128)(2,1)S(1)}, u32[]{:S(2)}, u32[]{:S(2)}) collective-permute-start(bf16[32,4096]{1,0:T(8,128)(2,1)S(1)} %get-tuple-element.66), channel_id=1, source_target_pairs={{0,48},{1,49},{8,56},{9,57},{2,50},{3,51},{10,58},{11,59},{4,52},{... | collective-permute-start | bytes 786440 | tf_op jit(solution)/shard_map/ppermute | solution.py:37
  57.7 2.5 %collective-permute-start.12 = (bf16[32,4096]{1,0:T(8,128)(2,1)S(1)}, bf16[32,4096]{1,0:T(8,128)(2,1)S(1)}, u32[]{:S(2)}, u32[]{:S(2)}) collective-permute-start(bf16[32,4096]{1,0:T(8,128)(2,1)S(1)} %get-tuple-element.68), channel_id=1, source_target_pairs={{0,8},{1,15},{8,2},{9,1},{2,10},{3,9},{10,4},{11,3},{4,12},{5,11},... | collective-permute-start | bytes 786440 | tf_op jit(solution)/shard_map/ppermute | solution.py:41
  60.3 1.7 %collective-permute-done.10.refs_1_ = bf16[32,4096]{1,0:T(8,128)(2,1)S(1)} collective-permute-done((bf16[32,4096]{1,0:T(8,128)(2,1)S(1)}, bf16[32,4096]{1,0:T(8,128)(2,1)S(1)}, u32[]{:S(2)}, u32[]{:S(2)}) %collective-permute-start.10) | collective-permute-done | bytes 262176 | tf_op jit(solution)/shard_map/ppermute | solution.py:37
  62.1 2.8 %collective-permute-done.11.refs_2_ = bf16[32,4096]{1,0:T(8,128)(2,1)S(1)} collective-permute-done((bf16[32,4096]{1,0:T(8,128)(2,1)S(1)}, bf16[32,4096]{1,0:T(8,128)(2,1)S(1)}, u32[]{:S(2)}, u32[]{:S(2)}) %collective-permute-start.11) | collective-permute-done | bytes 262176 | tf_op jit(solution)/shard_map/ppermute | solution.py:33
  65.3 1.0 %shard_map.100 = bf16[8,2,4,4096]{3,2,1,0:T(4,128)(2,1)} custom-call(bf16[8,4,4096]{2,1,0:T(4,128)(2,1)S(1)} %shard_map.98.out_total, f32[32,4096]{1,0:T(8,128)S(1)} %get-tuple-element.65.refs_0_, bf16[32,4096]{1,0:T(8,128)(2,1)S(1)} %collective-permute-done.10.refs_1_, bf16[32,4096]{1,0:T(8,128)(2,1)S(1)} %collective-permute-done.11.refs_2_, ...), custom_call_target="tpu_custom_call" | custom-call | tf_op jit(solution)/shard_map/pallas_call | solution.py:62
  66.3 4.6 %all-to-all-start.1 = ((bf16[8,2,4,4096]{3,2,1,0:T(4,128)(2,1)}), bf16[8,2,4,4096]{3,2,1,0:T(4,128)(2,1)S(1)}, u32[]{:S(2)}, u32[]{:S(2)}) async-start(bf16[8,2,4,4096]{3,2,1,0:T(4,128)(2,1)} %shard_map.100), calls=%async_computation.1 | async-start | bytes 1048576 | tf_op jit(solution)/shard_map/all_to_all | solution.py:45
  72.0 3.3 %collective-permute-done.17.refs_11_ = bf16[3,128,256]{2,1,0:T(8,128)(2,1)S(1)} collective-permute-done((bf16[3,128,256]{2,1,0:T(8,128)(2,1)S(1)}, bf16[3,128,256]{2,1,0:T(8,128)(2,1)S(1)}, u32[]{:S(2)}, u32[]{:S(2)}) %collective-permute-start.17) | collective-permute-done | bytes 196640 | tf_op jit(solution)/shard_map/ppermute | solution.py:29
  75.3 5.6 %shard_map.101 = (bf16[1,4096,256]{2,1,0:T(8,128)(2,1)}, bf16[1,4096,256]{2,1,0:T(8,128)(2,1)}, bf16[1,256,4096]{2,1,0:T(8,128)(2,1)}) custom-call(bf16[2,32,4096]{2,1,0:T(8,128)(2,1)S(1)} %shard_map.94.refs_0_, bf16[2,32,4096]{2,1,0:T(8,128)(2,1)S(1)} %collective-permute-done.4.refs_1_, bf16[2,32,4096]{2,1,0:T(8,128)(2,1)S(1)} %collective-permute-done.5.refs_2_, ...), custom_call_target="tpu_custom_call" | custom-call | tf_op jit(solution)/shard_map/pallas_call | solution.py:206
  80.9 3.2 %all-to-all-done.1.arrived = bf16[8,2,4,4096]{3,2,1,0:T(4,128)(2,1)S(1)} async-done(((bf16[8,2,4,4096]{3,2,1,0:T(4,128)(2,1)}), bf16[8,2,4,4096]{3,2,1,0:T(4,128)(2,1)S(1)}, u32[]{:S(2)}, u32[]{:S(2)}) %all-to-all-start.1) | async-done | bytes 524320 | tf_op jit(solution)/shard_map/all_to_all | solution.py:45
  85.7 4.3 %collective-permute-done.18 = bf16[1,4,4096]{2,1,0:T(4,128)(2,1)S(1)} collective-permute-done((bf16[1,4,4096]{2,1,0:T(4,128)(2,1)S(1)}, bf16[1,4,4096]{2,1,0:T(4,128)(2,1)S(1)}, u32[]{:S(2)}, u32[]{:S(2)}) %collective-permute-start.18) | collective-permute-done | bytes 32800 | tf_op jit(solution)/shard_map/ppermute | solution.py:50
  (37 shorter events, 7.1 us)
Async XLA Ops:
  0.6 35.4 %copy-start = (bf16[1,4096,256]{2,1,0:T(8,128)(2,1)S(1)}, bf16[1,4096,256]{2,1,0:T(8,128)(2,1)}, u32[]{:S(2)}) copy-start(bf16[1,4096,256]{2,1,0:T(8,128)(2,1)} %refs_0_) | copy-start | bytes 6291460
  0.6 32.3 %collective-permute-start.1 = (bf16[1,4096,256]{2,1,0:T(8,128)(2,1)}, bf16[1,4096,256]{2,1,0:T(8,128)(2,1)S(1)}, u32[]{:S(2)}, u32[]{:S(2)}) collective-permute-start(bf16[1,4096,256]{2,1,0:T(8,128)(2,1)} %refs_0_), channel_id=1, source_target_pairs={{0,1},{1,0},{8,9},{9,8},{2,3},{3,2},{10,11},{11,10},{4,5},{5,4},{1... | collective-permute-start | bytes 6291464 | tf_op jit(solution)/shard_map/ppermute | solution.py:29
  0.7 32.2 %collective-permute-start.2 = (bf16[1,4096,256]{2,1,0:T(8,128)(2,1)}, bf16[1,4096,256]{2,1,0:T(8,128)(2,1)S(1)}, u32[]{:S(2)}, u32[]{:S(2)}) collective-permute-start(bf16[1,4096,256]{2,1,0:T(8,128)(2,1)} %refs_1_.1), channel_id=1, source_target_pairs={{0,1},{1,0},{8,9},{9,8},{2,3},{3,2},{10,11},{11,10},{4,5},{5,4},{1... | collective-permute-start | bytes 6291464 | tf_op jit(solution)/shard_map/ppermute | solution.py:29
  1.2 31.7 %collective-permute-start.3 = (bf16[1,256,4096]{2,1,0:T(8,128)(2,1)}, bf16[1,256,4096]{2,1,0:T(8,128)(2,1)S(1)}, u32[]{:S(2)}, u32[]{:S(2)}) collective-permute-start(bf16[1,256,4096]{2,1,0:T(8,128)(2,1)} %refs_2_.1), channel_id=1, source_target_pairs={{0,1},{1,0},{8,9},{9,8},{2,3},{3,2},{10,11},{11,10},{4,5},{5,4},{1... | collective-permute-start | bytes 6291464 | tf_op jit(solution)/shard_map/ppermute | solution.py:29
  1.3 4.1 %collective-permute-start = (bf16[4,4096]{1,0:T(4,128)(2,1)}, bf16[4,4096]{1,0:T(4,128)(2,1)S(1)}, u32[]{:S(2)}, u32[]{:S(2)}) collective-permute-start(bf16[4,4096]{1,0:T(4,128)(2,1)} %bitcast.1), channel_id=1, source_target_pairs={{0,64},{64,128},{128,192},{192,0},{1,65},{65,129},{129,193},{193,1... | collective-permute-start | bytes 98312 | tf_op jit(solution)/shard_map/ppermute | solution.py:50
  3.6 0.8 copy-start.3
  33.0 11.8 %collective-permute-start.5 = (bf16[2,32,4096]{2,1,0:T(8,128)(2,1)S(1)}, bf16[2,32,4096]{2,1,0:T(8,128)(2,1)S(1)}, u32[]{:S(2)}, u32[]{:S(2)}) collective-permute-start(bf16[2,32,4096]{2,1,0:T(8,128)(2,1)S(1)} %shard_map.94.refs_0_), channel_id=1, source_target_pairs={{0,48},{1,49},{8,56},{9,57},{2,50},{3,51},{10,58},{11,59},{4,52},{... | collective-permute-start | bytes 1572872 | tf_op jit(solution)/shard_map/ppermute | solution.py:37
  33.5 13.0 %collective-permute-start.4 = (bf16[2,32,4096]{2,1,0:T(8,128)(2,1)S(1)}, bf16[2,32,4096]{2,1,0:T(8,128)(2,1)S(1)}, u32[]{:S(2)}, u32[]{:S(2)}) collective-permute-start(bf16[2,32,4096]{2,1,0:T(8,128)(2,1)S(1)} %shard_map.94.refs_0_), channel_id=1, source_target_pairs={{0,16},{1,17},{8,24},{9,25},{2,18},{3,19},{10,26},{11,27},{4,20},{... | collective-permute-start | bytes 1572872 | tf_op jit(solution)/shard_map/ppermute | solution.py:33
  35.1 11.4 %collective-permute-start.6 = (bf16[2,32,4096]{2,1,0:T(8,128)(2,1)S(1)}, bf16[2,32,4096]{2,1,0:T(8,128)(2,1)S(1)}, u32[]{:S(2)}, u32[]{:S(2)}) collective-permute-start(bf16[2,32,4096]{2,1,0:T(8,128)(2,1)S(1)} %shard_map.94.refs_0_), channel_id=1, source_target_pairs={{0,8},{1,15},{8,2},{9,1},{2,10},{3,9},{10,4},{11,3},{4,12},{5,11},... | collective-permute-start | bytes 1572872 | tf_op jit(solution)/shard_map/ppermute | solution.py:41
  36.1 1.6 %copy-start.1 = (bf16[1,4096,256]{2,1,0:T(8,128)(2,1)S(1)}, bf16[1,4096,256]{2,1,0:T(8,128)(2,1)}, u32[]{:S(2)}) copy-start(bf16[1,4096,256]{2,1,0:T(8,128)(2,1)} %refs_1_.1) | copy-start | bytes 6291460
  37.7 1.6 %copy-start.2 = (bf16[1,256,4096]{2,1,0:T(8,128)(2,1)S(1)}, bf16[1,256,4096]{2,1,0:T(8,128)(2,1)}, u32[]{:S(2)}) copy-start(bf16[1,256,4096]{2,1,0:T(8,128)(2,1)} %refs_2_.1) | copy-start | bytes 6291460
  49.0 8.7 %collective-permute-start.7 = (bf16[32,4096]{1,0:T(8,128)(2,1)S(1)}, bf16[32,4096]{1,0:T(8,128)(2,1)S(1)}, u32[]{:S(2)}, u32[]{:S(2)}) collective-permute-start(bf16[32,4096]{1,0:T(8,128)(2,1)S(1)} %get-tuple-element.59), channel_id=1, source_target_pairs={{0,48},{1,49},{8,56},{9,57},{2,50},{3,51},{10,58},{11,59},{4,52},{... | collective-permute-start | bytes 786440 | tf_op jit(solution)/shard_map/ppermute | solution.py:37
  50.0 10.2 %collective-permute-start.8 = (bf16[32,4096]{1,0:T(8,128)(2,1)S(1)}, bf16[32,4096]{1,0:T(8,128)(2,1)S(1)}, u32[]{:S(2)}, u32[]{:S(2)}) collective-permute-start(bf16[32,4096]{1,0:T(8,128)(2,1)S(1)} %get-tuple-element.60), channel_id=1, source_target_pairs={{0,16},{1,17},{8,24},{9,25},{2,18},{3,19},{10,26},{11,27},{4,20},{... | collective-permute-start | bytes 786440 | tf_op jit(solution)/shard_map/ppermute | solution.py:33
  51.2 9.0 %collective-permute-start.9 = (bf16[32,4096]{1,0:T(8,128)(2,1)S(1)}, bf16[32,4096]{1,0:T(8,128)(2,1)S(1)}, u32[]{:S(2)}, u32[]{:S(2)}) collective-permute-start(bf16[32,4096]{1,0:T(8,128)(2,1)S(1)} %get-tuple-element.61), channel_id=1, source_target_pairs={{0,8},{1,15},{8,2},{9,1},{2,10},{3,9},{10,4},{11,3},{4,12},{5,11},... | collective-permute-start | bytes 786440 | tf_op jit(solution)/shard_map/ppermute | solution.py:41
  55.6 6.4 %collective-permute-start.10 = (bf16[32,4096]{1,0:T(8,128)(2,1)S(1)}, bf16[32,4096]{1,0:T(8,128)(2,1)S(1)}, u32[]{:S(2)}, u32[]{:S(2)}) collective-permute-start(bf16[32,4096]{1,0:T(8,128)(2,1)S(1)} %get-tuple-element.66), channel_id=1, source_target_pairs={{0,48},{1,49},{8,56},{9,57},{2,50},{3,51},{10,58},{11,59},{4,52},{... | collective-permute-start | bytes 786440 | tf_op jit(solution)/shard_map/ppermute | solution.py:37
  57.3 7.6 %collective-permute-start.11 = (bf16[32,4096]{1,0:T(8,128)(2,1)S(1)}, bf16[32,4096]{1,0:T(8,128)(2,1)S(1)}, u32[]{:S(2)}, u32[]{:S(2)}) collective-permute-start(bf16[32,4096]{1,0:T(8,128)(2,1)S(1)} %get-tuple-element.67), channel_id=1, source_target_pairs={{0,16},{1,17},{8,24},{9,25},{2,18},{3,19},{10,26},{11,27},{4,20},{... | collective-permute-start | bytes 786440 | tf_op jit(solution)/shard_map/ppermute | solution.py:33
  57.7 7.6 %collective-permute-start.12 = (bf16[32,4096]{1,0:T(8,128)(2,1)S(1)}, bf16[32,4096]{1,0:T(8,128)(2,1)S(1)}, u32[]{:S(2)}, u32[]{:S(2)}) collective-permute-start(bf16[32,4096]{1,0:T(8,128)(2,1)S(1)} %get-tuple-element.68), channel_id=1, source_target_pairs={{0,8},{1,15},{8,2},{9,1},{2,10},{3,9},{10,4},{11,3},{4,12},{5,11},... | collective-permute-start | bytes 786440 | tf_op jit(solution)/shard_map/ppermute | solution.py:41
  66.3 17.9 %all-to-all-start.1 = ((bf16[8,2,4,4096]{3,2,1,0:T(4,128)(2,1)}), bf16[8,2,4,4096]{3,2,1,0:T(4,128)(2,1)S(1)}, u32[]{:S(2)}, u32[]{:S(2)}) async-start(bf16[8,2,4,4096]{3,2,1,0:T(4,128)(2,1)} %shard_map.100), calls=%async_computation.1 | async-start | bytes 1048576 | tf_op jit(solution)/shard_map/all_to_all | solution.py:45
  70.9 4.4 %collective-permute-start.13 = (bf16[2,32,4096]{2,1,0:T(8,128)(2,1)S(1)}, bf16[2,32,4096]{2,1,0:T(8,128)(2,1)S(1)}, u32[]{:S(2)}, u32[]{:S(2)}) collective-permute-start(bf16[2,32,4096]{2,1,0:T(8,128)(2,1)S(1)} %shard_map.94.refs_0_), channel_id=1, source_target_pairs={{0,1},{1,0},{8,9},{9,8},{2,3},{3,2},{10,11},{11,10},{4,5},{5,4},{1... | collective-permute-start | bytes 1572872 | tf_op jit(solution)/shard_map/ppermute | solution.py:29
  70.9 4.4 %collective-permute-start.14 = (bf16[2,32,4096]{2,1,0:T(8,128)(2,1)S(1)}, bf16[2,32,4096]{2,1,0:T(8,128)(2,1)S(1)}, u32[]{:S(2)}, u32[]{:S(2)}) collective-permute-start(bf16[2,32,4096]{2,1,0:T(8,128)(2,1)S(1)} %collective-permute-done.4.refs_1_), channel_id=1, source_target_pairs={{0,1},{1,0},{8,9},{9,8},{2,3},{3,2},{10,11},{11,10},{4,5},{5,4},{1... | collective-permute-start | bytes 1572872 | tf_op jit(solution)/shard_map/ppermute | solution.py:29
  71.4 3.9 %collective-permute-start.15 = (bf16[2,32,4096]{2,1,0:T(8,128)(2,1)S(1)}, bf16[2,32,4096]{2,1,0:T(8,128)(2,1)S(1)}, u32[]{:S(2)}, u32[]{:S(2)}) collective-permute-start(bf16[2,32,4096]{2,1,0:T(8,128)(2,1)S(1)} %collective-permute-done.5.refs_2_), channel_id=1, source_target_pairs={{0,1},{1,0},{8,9},{9,8},{2,3},{3,2},{10,11},{11,10},{4,5},{5,4},{1... | collective-permute-start | bytes 1572872 | tf_op jit(solution)/shard_map/ppermute | solution.py:29
  71.5 3.9 %collective-permute-start.16 = (bf16[2,32,4096]{2,1,0:T(8,128)(2,1)S(1)}, bf16[2,32,4096]{2,1,0:T(8,128)(2,1)S(1)}, u32[]{:S(2)}, u32[]{:S(2)}) collective-permute-start(bf16[2,32,4096]{2,1,0:T(8,128)(2,1)S(1)} %collective-permute-done.6.refs_3_), channel_id=1, source_target_pairs={{0,1},{1,0},{8,9},{9,8},{2,3},{3,2},{10,11},{11,10},{4,5},{5,4},{1... | collective-permute-start | bytes 1572872 | tf_op jit(solution)/shard_map/ppermute | solution.py:29
  71.9 3.4 %collective-permute-start.17 = (bf16[3,128,256]{2,1,0:T(8,128)(2,1)S(1)}, bf16[3,128,256]{2,1,0:T(8,128)(2,1)S(1)}, u32[]{:S(2)}, u32[]{:S(2)}) collective-permute-start(bf16[3,128,256]{2,1,0:T(8,128)(2,1)S(1)} %get-tuple-element.77), channel_id=1, source_target_pairs={{0,1},{1,0},{8,9},{9,8},{2,3},{3,2},{10,11},{11,10},{4,5},{5,4},{1... | collective-permute-start | bytes 589832 | tf_op jit(solution)/shard_map/ppermute | solution.py:29
  84.8 5.1 %collective-permute-start.18 = (bf16[1,4,4096]{2,1,0:T(4,128)(2,1)S(1)}, bf16[1,4,4096]{2,1,0:T(4,128)(2,1)S(1)}, u32[]{:S(2)}, u32[]{:S(2)}) collective-permute-start(bf16[1,4,4096]{2,1,0:T(4,128)(2,1)S(1)} %get-tuple-element.83), channel_id=1, source_target_pairs={{0,192},{64,0},{128,64},{192,128},{1,193},{65,1},{129,65},{193,129... | collective-permute-start | bytes 98312 | tf_op jit(solution)/shard_map/ppermute | solution.py:50

commit v6 on v5

--- a/solution.py
+++ b/solution.py
@@ -1,3 +1,5 @@
+import functools
+
 import jax
 import jax.numpy as jnp
 from jax import lax
@@ -9,7 +11,7 @@
 NY, NZ = 4, 8
 BF16 = jnp.bfloat16
 F32 = jnp.float32
-CHUNK = 1024
+CHUNK = 4096
 
 
 def place(y, z, core):
@@ -102,9 +104,8 @@
         fan[i, 1] = cotangent[0]
 
 
-def total_body(arrived, output, back):
-    for kind, total in enumerate((output, back)):
-        total[0] = sum(arrived[i, kind].astype(F32) for i in range(NZ)).astype(BF16)
+def total_body(kind, arrived, total):
+    total[0] = sum(arrived[i, kind].astype(F32) for i in range(NZ)).astype(BF16)
 
 
 def split_body(got_ref, own_ref):
@@ -197,7 +198,7 @@
 def weight_grads(*args):
     _, rows, width = args[0].shape
     tokens, units = args[8].shape
-    part = width // 8
+    part = width // 4
     streamed = [pl.BlockSpec((2, rows, part), lambda i: (0, 0, i))] * 8
     whole = [pl.BlockSpec((tokens, units), lambda i: (0, 0))] * 3 + [pl.BlockSpec((3, tokens, units), lambda i: (0, 0, 0))]
     across = [pl.BlockSpec((1, part, units), lambda i: (0, i, 0))] * 2
@@ -287,8 +288,11 @@
         *blocks, *[swap(block) for block in blocks], gate_grad, up_grad, hidden, swap(give))
     arrived = colour_all_to_all(sums)
     arrived, grad_gate, grad_up, grad_down = lax.optimization_barrier((arrived, grad_gate, grad_up, grad_down))
-    output, back = local_kernel(total_body, [((1, rows, width), BF16)] * 2, arrived)
-    return (output, from_behind(back, "section", -1), grad_gate, grad_up, grad_down)
+    total = ((1, rows, width), BF16)
+    (back,) = local_kernel(functools.partial(total_body, 1), [total], arrived)
+    returned = from_behind(back, "section", -1)
+    (output,) = local_kernel(functools.partial(total_body, 0), [total], arrived)
+    return (output, returned, grad_gate, grad_up, grad_down)
 
 
 def solution(mesh):

time: 90.9 us -> 89.6 us (0.986)
  Pallas kernels: 17.8 us -> 14 us
  waiting for transfers between devices: 19.1 us -> 22.8 us
  starting transfers between devices: 21 us -> 19.7 us
    pallas_call x9 -> x10, Pallas kernels: 11.7 us -> 9.31 us  [local_kernel(): pl.pallas_call(body, out_shape=[jax.ShapeDtypeStruct(shape, dtype) for sh...]
    ppermute x3, waiting for transfers between devices: 2.13 us -> 4.26 us  [y_last(): return lax.ppermute(x, PLANE, Y_LAST)]
    all_to_all x1, waiting for transfers between devices: 3.22 us -> 4.63 us  [colour_all_to_all(): return lax.all_to_all(x, PLANE, 0, 0, axis_index_groups=COLOURS)]
    pallas_call x1, Pallas kernels: 5.61 us -> 4.2 us  [weight_grads(): pl.pallas_call(weight_grads_body, grid=(width // part,), out_shape=[jax.S...]
    ppermute x3, waiting for transfers between devices: 0.41 us -> 1.43 us  [z_step(): return lax.ppermute(x, PLANE, Z_STEP)]
  transfers between devices with their start and end apart: 20 -> 20, of which waited for: 9 -> 10; matrix products, arithmetic and copies ran while one was open for 0% -> 0% of each run, Pallas kernels for 15% -> 12%
where the time goes in v6:
time: 89.6 us; the launch traced here: 89.2 us
  blocking collectives  27.4 us (31%)
  waiting for transfers between devices  22.8 us (25%)
  starting transfers between devices  19.7 us (22%)
  Pallas kernels  14 us (16%)
  local copies, waits for them, and re-layouts  4.56 us (5%)
    all_to_all x1, blocking collectives, colour_all_to_all(): return lax.all_to_all(x, PLANE, 0, 0, axis_index_groups=COLOURS)  27.4 us
    pallas_call x10, Pallas kernels, local_kernel(): pl.pallas_call(body, out_shape=[jax.ShapeDtypeStruct(shape, dtype) for sh...  9.31 us
    ppermute x2, waiting for transfers between devices, from_behind(): lax.ppermute(x, axis, [(i, (i + by) % length) for i in range(length)])  4.8 us
    all_to_all x1, waiting for transfers between devices, colour_all_to_all(): return lax.all_to_all(x, PLANE, 0, 0, axis_index_groups=COLOURS)  4.63 us
    unnamed x9, local copies, waits for them, and re-layouts  4.56 us
    ppermute x3, starting transfers between devices, z_step(): return lax.ppermute(x, PLANE, Z_STEP)  4.41 us
    ppermute x3, waiting for transfers between devices, y_next(): return lax.ppermute(x, PLANE, Y_NEXT)  4.38 us
    ppermute x3, waiting for transfers between devices, y_last(): return lax.ppermute(x, PLANE, Y_LAST)  4.26 us
  transfers between devices with their start and end apart: 20, of which 10 were waited for; matrix products, arithmetic and copies ran while one was open for 0% of the time, Pallas kernels for 12%

profile of v6, /device:TPU:6, one launch (start us, length us, event | category | flops | bytes accessed | tf_op | source)
XLA Modules:
  0.0 89.2 jit_solution(8853713051261347926)
XLA Ops:
  1.3 2.2 %collective-permute-start = (bf16[4,4096]{1,0:T(4,128)(2,1)}, bf16[4,4096]{1,0:T(4,128)(2,1)S(1)}, u32[]{:S(2)}, u32[]{:S(2)}) collective-permute-start(bf16[4,4096]{1,0:T(4,128)(2,1)} %bitcast.1), channel_id=1, source_target_pairs={{0,64},{64,128},{128,192},{192,0},{1,65},{65,129},{129,193},{193,1... | collective-permute-start | bytes 98312 | tf_op jit(solution)/shard_map/ppermute | solution.py:52
  4.3 1.2 %collective-permute-done.layer = bf16[4,4096]{1,0:T(4,128)(2,1)S(1)} collective-permute-done((bf16[4,4096]{1,0:T(4,128)(2,1)}, bf16[4,4096]{1,0:T(4,128)(2,1)S(1)}, u32[]{:S(2)}, u32[]{:S(2)}) %collective-permute-start) | collective-permute-done | bytes 32800 | tf_op jit(solution)/shard_map/ppermute | solution.py:52
  5.5 27.4 %all_to_all.10.got_ref = bf16[8,2,4,4096]{3,2,1,0:T(4,128)(2,1)S(1)} all-to-all(bf16[8,2,4,4096]{3,2,1,0:T(4,128)(2,1)S(1)} %shard_map.93), channel_id=1, replica_groups={{0,40,2,42,4,44,6,46},{1,41,3,43,5,45,7,47},{16,56,18,58,20,60,22,62},{..., dimensions={0} | all-to-all | bytes 1048576 | tf_op jit(solution)/shard_map/all_to_all | solution.py:47
  33.5 1.6 %collective-permute-start.4 = (bf16[2,32,4096]{2,1,0:T(8,128)(2,1)S(1)}, bf16[2,32,4096]{2,1,0:T(8,128)(2,1)S(1)}, u32[]{:S(2)}, u32[]{:S(2)}) collective-permute-start(bf16[2,32,4096]{2,1,0:T(8,128)(2,1)S(1)} %shard_map.94.refs_0_), channel_id=1, source_target_pairs={{0,16},{1,17},{8,24},{9,25},{2,18},{3,19},{10,26},{11,27},{4,20},{... | collective-permute-start | bytes 1572872 | tf_op jit(solution)/shard_map/ppermute | solution.py:35
  36.1 1.6 %copy-done.1 = bf16[1,4096,256]{2,1,0:T(8,128)(2,1)S(1)} copy-done((bf16[1,4096,256]{2,1,0:T(8,128)(2,1)S(1)}, bf16[1,4096,256]{2,1,0:T(8,128)(2,1)}, u32[]{:S(2)}) %copy-start.1) | copy-done | bytes 2097176
  37.7 1.6 %copy-done.2 = bf16[1,256,4096]{2,1,0:T(8,128)(2,1)S(1)} copy-done((bf16[1,256,4096]{2,1,0:T(8,128)(2,1)S(1)}, bf16[1,256,4096]{2,1,0:T(8,128)(2,1)}, u32[]{:S(2)}) %copy-start.2) | copy-done | bytes 2097176
  39.7 3.5 %shard_map.96 = (bf16[1024,4096]{1,0:T(8,128)(2,1)S(1)}, bf16[4096,512]{1,0:T(8,128)(2,1)S(1)}) custom-call(bf16[1,4096,256]{2,1,0:T(8,128)(2,1)S(1)} %get-tuple-element.46.gate_w.refs_4_, bf16[1,4096,256]{2,1,0:T(8,128)(2,1)S(1)} %get-tuple-element.47.up_w.refs_6_, bf16[1,4096,256]{2,1,0:T(8,128)(2,1)S(1)} %collective-permute-done.1.gate_x.refs_5_, ...), custom_call_target="tpu_custom_call" | custom-call | tf_op jit(solution)/shard_map/pallas_call | solution.py:64
  43.2 1.6 %collective-permute-done.5.refs_2_ = bf16[2,32,4096]{2,1,0:T(8,128)(2,1)S(1)} collective-permute-done((bf16[2,32,4096]{2,1,0:T(8,128)(2,1)S(1)}, bf16[2,32,4096]{2,1,0:T(8,128)(2,1)S(1)}, u32[]{:S(2)}, u32[]{:S(2)}) %collective-permute-start.5) | collective-permute-done | bytes 524320 | tf_op jit(solution)/shard_map/ppermute | solution.py:39
  44.8 1.7 %collective-permute-done.4.refs_1_ = bf16[2,32,4096]{2,1,0:T(8,128)(2,1)S(1)} collective-permute-done((bf16[2,32,4096]{2,1,0:T(8,128)(2,1)S(1)}, bf16[2,32,4096]{2,1,0:T(8,128)(2,1)S(1)}, u32[]{:S(2)}, u32[]{:S(2)}) %collective-permute-start.4) | collective-permute-done | bytes 524320 | tf_op jit(solution)/shard_map/ppermute | solution.py:35
  46.5 2.0 %shard_map.97 = (bf16[128,256]{1,0:T(8,128)(2,1)S(1)}, bf16[128,256]{1,0:T(8,128)(2,1)S(1)}, f32[2,128,256]{2,1,0:T(8,128)S(1)}, f32[2,128,256]{2,1,0:T(8,128)S(...) custom-call(bf16[2,32,4096]{2,1,0:T(8,128)(2,1)S(1)} %shard_map.94.r, ...), custom_call_target="tpu_custom_call" | custom-call | tf_op jit(solution)/shard_map/pallas_call | solution.py:64
  49.2 1.4 %collective-permute-start.8 = (bf16[32,4096]{1,0:T(8,128)(2,1)S(1)}, bf16[32,4096]{1,0:T(8,128)(2,1)S(1)}, u32[]{:S(2)}, u32[]{:S(2)}) collective-permute-start(bf16[32,4096]{1,0:T(8,128)(2,1)S(1)} %get-tuple-element.58), channel_id=1, source_target_pairs={{0,16},{1,17},{8,24},{9,25},{2,18},{3,19},{10,26},{11,27},{4,20},{... | collective-permute-start | bytes 786440 | tf_op jit(solution)/shard_map/ppermute | solution.py:35
  50.6 1.9 %collective-permute-start.9 = (bf16[32,4096]{1,0:T(8,128)(2,1)S(1)}, bf16[32,4096]{1,0:T(8,128)(2,1)S(1)}, u32[]{:S(2)}, u32[]{:S(2)}) collective-permute-start(bf16[32,4096]{1,0:T(8,128)(2,1)S(1)} %get-tuple-element.59), channel_id=1, source_target_pairs={{0,8},{1,15},{8,2},{9,1},{2,10},{3,9},{10,4},{11,3},{4,12},{5,11},... | collective-permute-start | bytes 786440 | tf_op jit(solution)/shard_map/ppermute | solution.py:43
  52.5 2.0 %shard_map.99 = (bf16[128,256]{1,0:T(8,128)(2,1)S(1)}, bf16[128,256]{1,0:T(8,128)(2,1)S(1)}, bf16[3,128,256]{2,1,0:T(8,128)(2,1)S(1)}, f32[32,4096]{1,0:T(8,128)...) custom-call(bf16[2,32,4096]{2,1,0:T(8,128)(2,1)S(1)} %shard_map.94.refs_0_, ...), custom_call_target="tpu_custom_call" | custom-call | tf_op jit(solution)/shard_map/pallas_call | solution.py:64
  54.4 1.6 %collective-permute-start.10 = (bf16[32,4096]{1,0:T(8,128)(2,1)S(1)}, bf16[32,4096]{1,0:T(8,128)(2,1)S(1)}, u32[]{:S(2)}, u32[]{:S(2)}) collective-permute-start(bf16[32,4096]{1,0:T(8,128)(2,1)S(1)} %get-tuple-element.64), channel_id=1, source_target_pairs={{0,48},{1,49},{8,56},{9,57},{2,50},{3,51},{10,58},{11,59},{4,52},{... | collective-permute-start | bytes 786440 | tf_op jit(solution)/shard_map/ppermute | solution.py:39
  57.4 1.6 %collective-permute-start.12 = (bf16[32,4096]{1,0:T(8,128)(2,1)S(1)}, bf16[32,4096]{1,0:T(8,128)(2,1)S(1)}, u32[]{:S(2)}, u32[]{:S(2)}) collective-permute-start(bf16[32,4096]{1,0:T(8,128)(2,1)S(1)} %get-tuple-element.66), channel_id=1, source_target_pairs={{0,8},{1,15},{8,2},{9,1},{2,10},{3,9},{10,4},{11,3},{4,12},{5,11},... | collective-permute-start | bytes 786440 | tf_op jit(solution)/shard_map/ppermute | solution.py:43
  59.1 1.7 %collective-permute-done.10.refs_1_ = bf16[32,4096]{1,0:T(8,128)(2,1)S(1)} collective-permute-done((bf16[32,4096]{1,0:T(8,128)(2,1)S(1)}, bf16[32,4096]{1,0:T(8,128)(2,1)S(1)}, u32[]{:S(2)}, u32[]{:S(2)}) %collective-permute-start.10) | collective-permute-done | bytes 262176 | tf_op jit(solution)/shard_map/ppermute | solution.py:39
  60.9 2.7 %collective-permute-done.11.refs_2_ = bf16[32,4096]{1,0:T(8,128)(2,1)S(1)} collective-permute-done((bf16[32,4096]{1,0:T(8,128)(2,1)S(1)}, bf16[32,4096]{1,0:T(8,128)(2,1)S(1)}, u32[]{:S(2)}, u32[]{:S(2)}) %collective-permute-start.11) | collective-permute-done | bytes 262176 | tf_op jit(solution)/shard_map/ppermute | solution.py:35
  63.6 1.4 %collective-permute-done.12.refs_3_ = bf16[32,4096]{1,0:T(8,128)(2,1)S(1)} collective-permute-done((bf16[32,4096]{1,0:T(8,128)(2,1)S(1)}, bf16[32,4096]{1,0:T(8,128)(2,1)S(1)}, u32[]{:S(2)}, u32[]{:S(2)}) %collective-permute-start.12) | collective-permute-done | bytes 262176 | tf_op jit(solution)/shard_map/ppermute | solution.py:43
  65.0 1.0 %shard_map.100 = bf16[8,2,4,4096]{3,2,1,0:T(4,128)(2,1)} custom-call(bf16[8,4,4096]{2,1,0:T(4,128)(2,1)S(1)} %shard_map.98.out_total, f32[32,4096]{1,0:T(8,128)S(1)} %get-tuple-element.63.refs_0_, bf16[32,4096]{1,0:T(8,128)(2,1)S(1)} %collective-permute-done.10.refs_1_, bf16[32,4096]{1,0:T(8,128)(2,1)S(1)} %collective-permute-done.11.refs_2_, ...), custom_call_target="tpu_custom_call" | custom-call | tf_op jit(solution)/shard_map/pallas_call | solution.py:64
  66.0 4.1 %all-to-all-start.1 = ((bf16[8,2,4,4096]{3,2,1,0:T(4,128)(2,1)}), bf16[8,2,4,4096]{3,2,1,0:T(4,128)(2,1)S(1)}, u32[]{:S(2)}, u32[]{:S(2)}) async-start(bf16[8,2,4,4096]{3,2,1,0:T(4,128)(2,1)} %shard_map.100), calls=%async_computation.1 | async-start | bytes 1048576 | tf_op jit(solution)/shard_map/all_to_all | solution.py:47
  71.2 3.3 %collective-permute-done.17.refs_11_ = bf16[3,128,256]{2,1,0:T(8,128)(2,1)S(1)} collective-permute-done((bf16[3,128,256]{2,1,0:T(8,128)(2,1)S(1)}, bf16[3,128,256]{2,1,0:T(8,128)(2,1)S(1)}, u32[]{:S(2)}, u32[]{:S(2)}) %collective-permute-start.17) | collective-permute-done | bytes 196640 | tf_op jit(solution)/shard_map/ppermute | solution.py:31
  74.5 4.2 %shard_map.101 = (bf16[1,4096,256]{2,1,0:T(8,128)(2,1)}, bf16[1,4096,256]{2,1,0:T(8,128)(2,1)}, bf16[1,256,4096]{2,1,0:T(8,128)(2,1)}) custom-call(bf16[2,32,4096]{2,1,0:T(8,128)(2,1)S(1)} %shard_map.94.refs_0_, bf16[2,32,4096]{2,1,0:T(8,128)(2,1)S(1)} %collective-permute-done.4.refs_1_, bf16[2,32,4096]{2,1,0:T(8,128)(2,1)S(1)} %collective-permute-done.5.refs_2_, ...), custom_call_target="tpu_custom_call" | custom-call | tf_op jit(solution)/shard_map/pallas_call | solution.py:207
  78.7 4.6 %all-to-all-done.1.arrived = bf16[8,2,4,4096]{3,2,1,0:T(4,128)(2,1)S(1)} async-done(((bf16[8,2,4,4096]{3,2,1,0:T(4,128)(2,1)}), bf16[8,2,4,4096]{3,2,1,0:T(4,128)(2,1)S(1)}, u32[]{:S(2)}, u32[]{:S(2)}) %all-to-all-start.1) | async-done | bytes 524320 | tf_op jit(solution)/shard_map/all_to_all | solution.py:47
  85.0 3.6 %collective-permute-done.18 = bf16[1,4,4096]{2,1,0:T(4,128)(2,1)S(1)} collective-permute-done((bf16[1,4,4096]{2,1,0:T(4,128)(2,1)S(1)}, bf16[1,4,4096]{2,1,0:T(4,128)(2,1)S(1)}, u32[]{:S(2)}, u32[]{:S(2)}) %collective-permute-start.18) | collective-permute-done | bytes 32800 | tf_op jit(solution)/shard_map/ppermute | solution.py:52
  (38 shorter events, 9.1 us)
Async XLA Ops:
  0.6 35.4 %copy-start = (bf16[1,4096,256]{2,1,0:T(8,128)(2,1)S(1)}, bf16[1,4096,256]{2,1,0:T(8,128)(2,1)}, u32[]{:S(2)}) copy-start(bf16[1,4096,256]{2,1,0:T(8,128)(2,1)} %refs_0_) | copy-start | bytes 6291460
  0.6 32.3 %collective-permute-start.1 = (bf16[1,4096,256]{2,1,0:T(8,128)(2,1)}, bf16[1,4096,256]{2,1,0:T(8,128)(2,1)S(1)}, u32[]{:S(2)}, u32[]{:S(2)}) collective-permute-start(bf16[1,4096,256]{2,1,0:T(8,128)(2,1)} %refs_0_), channel_id=1, source_target_pairs={{0,1},{1,0},{8,9},{9,8},{2,3},{3,2},{10,11},{11,10},{4,5},{5,4},{1... | collective-permute-start | bytes 6291464 | tf_op jit(solution)/shard_map/ppermute | solution.py:31
  0.7 32.2 %collective-permute-start.2 = (bf16[1,4096,256]{2,1,0:T(8,128)(2,1)}, bf16[1,4096,256]{2,1,0:T(8,128)(2,1)S(1)}, u32[]{:S(2)}, u32[]{:S(2)}) collective-permute-start(bf16[1,4096,256]{2,1,0:T(8,128)(2,1)} %refs_1_.1), channel_id=1, source_target_pairs={{0,1},{1,0},{8,9},{9,8},{2,3},{3,2},{10,11},{11,10},{4,5},{5,4},{1... | collective-permute-start | bytes 6291464 | tf_op jit(solution)/shard_map/ppermute | solution.py:31
  1.2 31.7 %collective-permute-start.3 = (bf16[1,256,4096]{2,1,0:T(8,128)(2,1)}, bf16[1,256,4096]{2,1,0:T(8,128)(2,1)S(1)}, u32[]{:S(2)}, u32[]{:S(2)}) collective-permute-start(bf16[1,256,4096]{2,1,0:T(8,128)(2,1)} %refs_2_.1), channel_id=1, source_target_pairs={{0,1},{1,0},{8,9},{9,8},{2,3},{3,2},{10,11},{11,10},{4,5},{5,4},{1... | collective-permute-start | bytes 6291464 | tf_op jit(solution)/shard_map/ppermute | solution.py:31
  1.3 4.1 %collective-permute-start = (bf16[4,4096]{1,0:T(4,128)(2,1)}, bf16[4,4096]{1,0:T(4,128)(2,1)S(1)}, u32[]{:S(2)}, u32[]{:S(2)}) collective-permute-start(bf16[4,4096]{1,0:T(4,128)(2,1)} %bitcast.1), channel_id=1, source_target_pairs={{0,64},{64,128},{128,192},{192,0},{1,65},{65,129},{129,193},{193,1... | collective-permute-start | bytes 98312 | tf_op jit(solution)/shard_map/ppermute | solution.py:52
  3.6 0.8 copy-start.3
  33.0 11.8 %collective-permute-start.5 = (bf16[2,32,4096]{2,1,0:T(8,128)(2,1)S(1)}, bf16[2,32,4096]{2,1,0:T(8,128)(2,1)S(1)}, u32[]{:S(2)}, u32[]{:S(2)}) collective-permute-start(bf16[2,32,4096]{2,1,0:T(8,128)(2,1)S(1)} %shard_map.94.refs_0_), channel_id=1, source_target_pairs={{0,48},{1,49},{8,56},{9,57},{2,50},{3,51},{10,58},{11,59},{4,52},{... | collective-permute-start | bytes 1572872 | tf_op jit(solution)/shard_map/ppermute | solution.py:39
  33.5 13.0 %collective-permute-start.4 = (bf16[2,32,4096]{2,1,0:T(8,128)(2,1)S(1)}, bf16[2,32,4096]{2,1,0:T(8,128)(2,1)S(1)}, u32[]{:S(2)}, u32[]{:S(2)}) collective-permute-start(bf16[2,32,4096]{2,1,0:T(8,128)(2,1)S(1)} %shard_map.94.refs_0_), channel_id=1, source_target_pairs={{0,16},{1,17},{8,24},{9,25},{2,18},{3,19},{10,26},{11,27},{4,20},{... | collective-permute-start | bytes 1572872 | tf_op jit(solution)/shard_map/ppermute | solution.py:35
  35.1 11.4 %collective-permute-start.6 = (bf16[2,32,4096]{2,1,0:T(8,128)(2,1)S(1)}, bf16[2,32,4096]{2,1,0:T(8,128)(2,1)S(1)}, u32[]{:S(2)}, u32[]{:S(2)}) collective-permute-start(bf16[2,32,4096]{2,1,0:T(8,128)(2,1)S(1)} %shard_map.94.refs_0_), channel_id=1, source_target_pairs={{0,8},{1,15},{8,2},{9,1},{2,10},{3,9},{10,4},{11,3},{4,12},{5,11},... | collective-permute-start | bytes 1572872 | tf_op jit(solution)/shard_map/ppermute | solution.py:43
  36.1 1.6 %copy-start.1 = (bf16[1,4096,256]{2,1,0:T(8,128)(2,1)S(1)}, bf16[1,4096,256]{2,1,0:T(8,128)(2,1)}, u32[]{:S(2)}) copy-start(bf16[1,4096,256]{2,1,0:T(8,128)(2,1)} %refs_1_.1) | copy-start | bytes 6291460
  37.7 1.6 %copy-start.2 = (bf16[1,256,4096]{2,1,0:T(8,128)(2,1)S(1)}, bf16[1,256,4096]{2,1,0:T(8,128)(2,1)}, u32[]{:S(2)}) copy-start(bf16[1,256,4096]{2,1,0:T(8,128)(2,1)} %refs_2_.1) | copy-start | bytes 6291460
  48.5 9.0 %collective-permute-start.7 = (bf16[32,4096]{1,0:T(8,128)(2,1)S(1)}, bf16[32,4096]{1,0:T(8,128)(2,1)S(1)}, u32[]{:S(2)}, u32[]{:S(2)}) collective-permute-start(bf16[32,4096]{1,0:T(8,128)(2,1)S(1)} %get-tuple-element.57), channel_id=1, source_target_pairs={{0,48},{1,49},{8,56},{9,57},{2,50},{3,51},{10,58},{11,59},{4,52},{... | collective-permute-start | bytes 786440 | tf_op jit(solution)/shard_map/ppermute | solution.py:39
  49.2 9.8 %collective-permute-start.8 = (bf16[32,4096]{1,0:T(8,128)(2,1)S(1)}, bf16[32,4096]{1,0:T(8,128)(2,1)S(1)}, u32[]{:S(2)}, u32[]{:S(2)}) collective-permute-start(bf16[32,4096]{1,0:T(8,128)(2,1)S(1)} %get-tuple-element.58), channel_id=1, source_target_pairs={{0,16},{1,17},{8,24},{9,25},{2,18},{3,19},{10,26},{11,27},{4,20},{... | collective-permute-start | bytes 786440 | tf_op jit(solution)/shard_map/ppermute | solution.py:35
  50.6 8.4 %collective-permute-start.9 = (bf16[32,4096]{1,0:T(8,128)(2,1)S(1)}, bf16[32,4096]{1,0:T(8,128)(2,1)S(1)}, u32[]{:S(2)}, u32[]{:S(2)}) collective-permute-start(bf16[32,4096]{1,0:T(8,128)(2,1)S(1)} %get-tuple-element.59), channel_id=1, source_target_pairs={{0,8},{1,15},{8,2},{9,1},{2,10},{3,9},{10,4},{11,3},{4,12},{5,11},... | collective-permute-start | bytes 786440 | tf_op jit(solution)/shard_map/ppermute | solution.py:43
  54.4 6.4 %collective-permute-start.10 = (bf16[32,4096]{1,0:T(8,128)(2,1)S(1)}, bf16[32,4096]{1,0:T(8,128)(2,1)S(1)}, u32[]{:S(2)}, u32[]{:S(2)}) collective-permute-start(bf16[32,4096]{1,0:T(8,128)(2,1)S(1)} %get-tuple-element.64), channel_id=1, source_target_pairs={{0,48},{1,49},{8,56},{9,57},{2,50},{3,51},{10,58},{11,59},{4,52},{... | collective-permute-start | bytes 786440 | tf_op jit(solution)/shard_map/ppermute | solution.py:39
  56.0 7.6 %collective-permute-start.11 = (bf16[32,4096]{1,0:T(8,128)(2,1)S(1)}, bf16[32,4096]{1,0:T(8,128)(2,1)S(1)}, u32[]{:S(2)}, u32[]{:S(2)}) collective-permute-start(bf16[32,4096]{1,0:T(8,128)(2,1)S(1)} %get-tuple-element.65), channel_id=1, source_target_pairs={{0,16},{1,17},{8,24},{9,25},{2,18},{3,19},{10,26},{11,27},{4,20},{... | collective-permute-start | bytes 786440 | tf_op jit(solution)/shard_map/ppermute | solution.py:35
  57.4 7.6 %collective-permute-start.12 = (bf16[32,4096]{1,0:T(8,128)(2,1)S(1)}, bf16[32,4096]{1,0:T(8,128)(2,1)S(1)}, u32[]{:S(2)}, u32[]{:S(2)}) collective-permute-start(bf16[32,4096]{1,0:T(8,128)(2,1)S(1)} %get-tuple-element.66), channel_id=1, source_target_pairs={{0,8},{1,15},{8,2},{9,1},{2,10},{3,9},{10,4},{11,3},{4,12},{5,11},... | collective-permute-start | bytes 786440 | tf_op jit(solution)/shard_map/ppermute | solution.py:43
  66.0 17.4 %all-to-all-start.1 = ((bf16[8,2,4,4096]{3,2,1,0:T(4,128)(2,1)}), bf16[8,2,4,4096]{3,2,1,0:T(4,128)(2,1)S(1)}, u32[]{:S(2)}, u32[]{:S(2)}) async-start(bf16[8,2,4,4096]{3,2,1,0:T(4,128)(2,1)} %shard_map.100), calls=%async_computation.1 | async-start | bytes 1048576 | tf_op jit(solution)/shard_map/all_to_all | solution.py:47
  70.1 4.4 %collective-permute-start.13 = (bf16[2,32,4096]{2,1,0:T(8,128)(2,1)S(1)}, bf16[2,32,4096]{2,1,0:T(8,128)(2,1)S(1)}, u32[]{:S(2)}, u32[]{:S(2)}) collective-permute-start(bf16[2,32,4096]{2,1,0:T(8,128)(2,1)S(1)} %shard_map.94.refs_0_), channel_id=1, source_target_pairs={{0,1},{1,0},{8,9},{9,8},{2,3},{3,2},{10,11},{11,10},{4,5},{5,4},{1... | collective-permute-start | bytes 1572872 | tf_op jit(solution)/shard_map/ppermute | solution.py:31
  70.1 4.4 %collective-permute-start.14 = (bf16[2,32,4096]{2,1,0:T(8,128)(2,1)S(1)}, bf16[2,32,4096]{2,1,0:T(8,128)(2,1)S(1)}, u32[]{:S(2)}, u32[]{:S(2)}) collective-permute-start(bf16[2,32,4096]{2,1,0:T(8,128)(2,1)S(1)} %collective-permute-done.4.refs_1_), channel_id=1, source_target_pairs={{0,1},{1,0},{8,9},{9,8},{2,3},{3,2},{10,11},{11,10},{4,5},{5,4},{1... | collective-permute-start | bytes 1572872 | tf_op jit(solution)/shard_map/ppermute | solution.py:31
  70.6 3.9 %collective-permute-start.15 = (bf16[2,32,4096]{2,1,0:T(8,128)(2,1)S(1)}, bf16[2,32,4096]{2,1,0:T(8,128)(2,1)S(1)}, u32[]{:S(2)}, u32[]{:S(2)}) collective-permute-start(bf16[2,32,4096]{2,1,0:T(8,128)(2,1)S(1)} %collective-permute-done.5.refs_2_), channel_id=1, source_target_pairs={{0,1},{1,0},{8,9},{9,8},{2,3},{3,2},{10,11},{11,10},{4,5},{5,4},{1... | collective-permute-start | bytes 1572872 | tf_op jit(solution)/shard_map/ppermute | solution.py:31
  70.7 3.9 %collective-permute-start.16 = (bf16[2,32,4096]{2,1,0:T(8,128)(2,1)S(1)}, bf16[2,32,4096]{2,1,0:T(8,128)(2,1)S(1)}, u32[]{:S(2)}, u32[]{:S(2)}) collective-permute-start(bf16[2,32,4096]{2,1,0:T(8,128)(2,1)S(1)} %collective-permute-done.6.refs_3_), channel_id=1, source_target_pairs={{0,1},{1,0},{8,9},{9,8},{2,3},{3,2},{10,11},{11,10},{4,5},{5,4},{1... | collective-permute-start | bytes 1572872 | tf_op jit(solution)/shard_map/ppermute | solution.py:31
  71.1 3.4 %collective-permute-start.17 = (bf16[3,128,256]{2,1,0:T(8,128)(2,1)S(1)}, bf16[3,128,256]{2,1,0:T(8,128)(2,1)S(1)}, u32[]{:S(2)}, u32[]{:S(2)}) collective-permute-start(bf16[3,128,256]{2,1,0:T(8,128)(2,1)S(1)} %get-tuple-element.75), channel_id=1, source_target_pairs={{0,1},{1,0},{8,9},{9,8},{2,3},{3,2},{10,11},{11,10},{4,5},{5,4},{1... | collective-permute-start | bytes 589832 | tf_op jit(solution)/shard_map/ppermute | solution.py:31
  83.4 5.2 %collective-permute-start.18 = (bf16[1,4,4096]{2,1,0:T(4,128)(2,1)S(1)}, bf16[1,4,4096]{2,1,0:T(4,128)(2,1)S(1)}, u32[]{:S(2)}, u32[]{:S(2)}) collective-permute-start(bf16[1,4,4096]{2,1,0:T(4,128)(2,1)S(1)} %shard_map.103), channel_id=1, source_target_pairs={{0,192},{64,0},{128,64},{192,128},{1,193},{65,1},{129,65},{193,129... | collective-permute-start | bytes 98312 | tf_op jit(solution)/shard_map/ppermute | solution.py:52

commit v7 on v6

--- a/solution.py
+++ b/solution.py
@@ -110,9 +110,9 @@
 
 def split_body(got_ref, own_ref):
     for kind in (0, 1):
-        for pair in range(NZ // 2):
-            two = [got_ref[2 * pair + i, kind].astype(F32) for i in (0, 1)]
-            own_ref[kind, 8 * pair : 8 * pair + 8, :] = jnp.concatenate(two, 0).astype(BF16)
+        for half in (0, 1):
+            four = [got_ref[4 * half + i, kind].astype(F32) for i in range(4)]
+            own_ref[kind, 16 * half : 16 * half + 16, :] = jnp.concatenate(four, 0).astype(BF16)
 
 
 def put_sums(sums, columns, own, last, next_, step):
@@ -217,13 +217,13 @@
 
 def add_terms(terms, joined, at):
     own, *received = terms
-    for pair in range(NZ // 2):
-        rows = slice(8 * pair, 8 * pair + 8)
+    for half in (0, 1):
+        rows = slice(16 * half, 16 * half + 16)
         sums = own[rows, :]
         for term in received:
             sums = sums + term[rows, :].astype(F32)
-        for i in (0, 1):
-            joined[(2 * pair + i, *at)] = sums[4 * i : 4 * i + 4].astype(BF16)
+        for i in range(4):
+            joined[(4 * half + i, *at)] = sums[4 * i : 4 * i + 4].astype(BF16)
 
 
 def out_total_body(*refs):

time: 89.6 us -> 89.6 us (level)
  no operation moved by 1% of the time
where the time goes in v7:
time: 89.6 us; the launch traced here: 89.2 us
  blocking collectives  27.4 us (31%)
  waiting for transfers between devices  22.8 us (25%)
  starting transfers between devices  19.7 us (22%)
  Pallas kernels  14 us (16%)
  local copies, waits for them, and re-layouts  4.56 us (5%)
    all_to_all x1, blocking collectives, colour_all_to_all(): return lax.all_to_all(x, PLANE, 0, 0, axis_index_groups=COLOURS)  27.4 us
    pallas_call x10, Pallas kernels, local_kernel(): pl.pallas_call(body, out_shape=[jax.ShapeDtypeStruct(shape, dtype) for sh...  9.31 us
    ppermute x2, waiting for transfers between devices, from_behind(): lax.ppermute(x, axis, [(i, (i + by) % length) for i in range(length)])  4.8 us
    all_to_all x1, waiting for transfers between devices, colour_all_to_all(): return lax.all_to_all(x, PLANE, 0, 0, axis_index_groups=COLOURS)  4.63 us
    unnamed x9, local copies, waits for them, and re-layouts  4.56 us
    ppermute x3, starting transfers between devices, z_step(): return lax.ppermute(x, PLANE, Z_STEP)  4.41 us
    ppermute x3, waiting for transfers between devices, y_next(): return lax.ppermute(x, PLANE, Y_NEXT)  4.38 us
    ppermute x3, waiting for transfers between devices, y_last(): return lax.ppermute(x, PLANE, Y_LAST)  4.26 us
  transfers between devices with their start and end apart: 20, of which 10 were waited for; matrix products, arithmetic and copies ran while one was open for 0% of the time, Pallas kernels for 12%

profile of v7, /device:TPU:6, one launch (start us, length us, event | category | flops | bytes accessed | tf_op | source)
XLA Modules:
  0.0 89.2 jit_solution(8853713051261347926)
XLA Ops:
  1.3 2.2 %collective-permute-start = (bf16[4,4096]{1,0:T(4,128)(2,1)}, bf16[4,4096]{1,0:T(4,128)(2,1)S(1)}, u32[]{:S(2)}, u32[]{:S(2)}) collective-permute-start(bf16[4,4096]{1,0:T(4,128)(2,1)} %bitcast.1), channel_id=1, source_target_pairs={{0,64},{64,128},{128,192},{192,0},{1,65},{65,129},{129,193},{193,1... | collective-permute-start | bytes 98312 | tf_op jit(solution)/shard_map/ppermute | solution.py:52
  4.3 1.2 %collective-permute-done.layer = bf16[4,4096]{1,0:T(4,128)(2,1)S(1)} collective-permute-done((bf16[4,4096]{1,0:T(4,128)(2,1)}, bf16[4,4096]{1,0:T(4,128)(2,1)S(1)}, u32[]{:S(2)}, u32[]{:S(2)}) %collective-permute-start) | collective-permute-done | bytes 32800 | tf_op jit(solution)/shard_map/ppermute | solution.py:52
  5.5 27.4 %all_to_all.10.got_ref = bf16[8,2,4,4096]{3,2,1,0:T(4,128)(2,1)S(1)} all-to-all(bf16[8,2,4,4096]{3,2,1,0:T(4,128)(2,1)S(1)} %shard_map.93), channel_id=1, replica_groups={{0,40,2,42,4,44,6,46},{1,41,3,43,5,45,7,47},{16,56,18,58,20,60,22,62},{..., dimensions={0} | all-to-all | bytes 1048576 | tf_op jit(solution)/shard_map/all_to_all | solution.py:47
  33.5 1.6 %collective-permute-start.4 = (bf16[2,32,4096]{2,1,0:T(8,128)(2,1)S(1)}, bf16[2,32,4096]{2,1,0:T(8,128)(2,1)S(1)}, u32[]{:S(2)}, u32[]{:S(2)}) collective-permute-start(bf16[2,32,4096]{2,1,0:T(8,128)(2,1)S(1)} %shard_map.94.refs_0_), channel_id=1, source_target_pairs={{0,16},{1,17},{8,24},{9,25},{2,18},{3,19},{10,26},{11,27},{4,20},{... | collective-permute-start | bytes 1572872 | tf_op jit(solution)/shard_map/ppermute | solution.py:35
  36.1 1.6 %copy-done.1 = bf16[1,4096,256]{2,1,0:T(8,128)(2,1)S(1)} copy-done((bf16[1,4096,256]{2,1,0:T(8,128)(2,1)S(1)}, bf16[1,4096,256]{2,1,0:T(8,128)(2,1)}, u32[]{:S(2)}) %copy-start.1) | copy-done | bytes 2097176
  37.7 1.6 %copy-done.2 = bf16[1,256,4096]{2,1,0:T(8,128)(2,1)S(1)} copy-done((bf16[1,256,4096]{2,1,0:T(8,128)(2,1)S(1)}, bf16[1,256,4096]{2,1,0:T(8,128)(2,1)}, u32[]{:S(2)}) %copy-start.2) | copy-done | bytes 2097176
  39.7 3.5 %shard_map.96 = (bf16[1024,4096]{1,0:T(8,128)(2,1)S(1)}, bf16[4096,512]{1,0:T(8,128)(2,1)S(1)}) custom-call(bf16[1,4096,256]{2,1,0:T(8,128)(2,1)S(1)} %get-tuple-element.46.gate_w.refs_4_, bf16[1,4096,256]{2,1,0:T(8,128)(2,1)S(1)} %get-tuple-element.47.up_w.refs_6_, bf16[1,4096,256]{2,1,0:T(8,128)(2,1)S(1)} %collective-permute-done.1.gate_x.refs_5_, ...), custom_call_target="tpu_custom_call" | custom-call | tf_op jit(solution)/shard_map/pallas_call | solution.py:64
  43.2 1.6 %collective-permute-done.5.refs_2_ = bf16[2,32,4096]{2,1,0:T(8,128)(2,1)S(1)} collective-permute-done((bf16[2,32,4096]{2,1,0:T(8,128)(2,1)S(1)}, bf16[2,32,4096]{2,1,0:T(8,128)(2,1)S(1)}, u32[]{:S(2)}, u32[]{:S(2)}) %collective-permute-start.5) | collective-permute-done | bytes 524320 | tf_op jit(solution)/shard_map/ppermute | solution.py:39
  44.8 1.7 %collective-permute-done.4.refs_1_ = bf16[2,32,4096]{2,1,0:T(8,128)(2,1)S(1)} collective-permute-done((bf16[2,32,4096]{2,1,0:T(8,128)(2,1)S(1)}, bf16[2,32,4096]{2,1,0:T(8,128)(2,1)S(1)}, u32[]{:S(2)}, u32[]{:S(2)}) %collective-permute-start.4) | collective-permute-done | bytes 524320 | tf_op jit(solution)/shard_map/ppermute | solution.py:35
  46.5 2.0 %shard_map.97 = (bf16[128,256]{1,0:T(8,128)(2,1)S(1)}, bf16[128,256]{1,0:T(8,128)(2,1)S(1)}, f32[2,128,256]{2,1,0:T(8,128)S(1)}, f32[2,128,256]{2,1,0:T(8,128)S(...) custom-call(bf16[2,32,4096]{2,1,0:T(8,128)(2,1)S(1)} %shard_map.94.r, ...), custom_call_target="tpu_custom_call" | custom-call | tf_op jit(solution)/shard_map/pallas_call | solution.py:64
  49.2 1.4 %collective-permute-start.8 = (bf16[32,4096]{1,0:T(8,128)(2,1)S(1)}, bf16[32,4096]{1,0:T(8,128)(2,1)S(1)}, u32[]{:S(2)}, u32[]{:S(2)}) collective-permute-start(bf16[32,4096]{1,0:T(8,128)(2,1)S(1)} %get-tuple-element.58), channel_id=1, source_target_pairs={{0,16},{1,17},{8,24},{9,25},{2,18},{3,19},{10,26},{11,27},{4,20},{... | collective-permute-start | bytes 786440 | tf_op jit(solution)/shard_map/ppermute | solution.py:35
  50.6 1.9 %collective-permute-start.9 = (bf16[32,4096]{1,0:T(8,128)(2,1)S(1)}, bf16[32,4096]{1,0:T(8,128)(2,1)S(1)}, u32[]{:S(2)}, u32[]{:S(2)}) collective-permute-start(bf16[32,4096]{1,0:T(8,128)(2,1)S(1)} %get-tuple-element.59), channel_id=1, source_target_pairs={{0,8},{1,15},{8,2},{9,1},{2,10},{3,9},{10,4},{11,3},{4,12},{5,11},... | collective-permute-start | bytes 786440 | tf_op jit(solution)/shard_map/ppermute | solution.py:43
  52.5 2.0 %shard_map.99 = (bf16[128,256]{1,0:T(8,128)(2,1)S(1)}, bf16[128,256]{1,0:T(8,128)(2,1)S(1)}, bf16[3,128,256]{2,1,0:T(8,128)(2,1)S(1)}, f32[32,4096]{1,0:T(8,128)...) custom-call(bf16[2,32,4096]{2,1,0:T(8,128)(2,1)S(1)} %shard_map.94.refs_0_, ...), custom_call_target="tpu_custom_call" | custom-call | tf_op jit(solution)/shard_map/pallas_call | solution.py:64
  54.4 1.6 %collective-permute-start.10 = (bf16[32,4096]{1,0:T(8,128)(2,1)S(1)}, bf16[32,4096]{1,0:T(8,128)(2,1)S(1)}, u32[]{:S(2)}, u32[]{:S(2)}) collective-permute-start(bf16[32,4096]{1,0:T(8,128)(2,1)S(1)} %get-tuple-element.64), channel_id=1, source_target_pairs={{0,48},{1,49},{8,56},{9,57},{2,50},{3,51},{10,58},{11,59},{4,52},{... | collective-permute-start | bytes 786440 | tf_op jit(solution)/shard_map/ppermute | solution.py:39
  57.4 1.6 %collective-permute-start.12 = (bf16[32,4096]{1,0:T(8,128)(2,1)S(1)}, bf16[32,4096]{1,0:T(8,128)(2,1)S(1)}, u32[]{:S(2)}, u32[]{:S(2)}) collective-permute-start(bf16[32,4096]{1,0:T(8,128)(2,1)S(1)} %get-tuple-element.66), channel_id=1, source_target_pairs={{0,8},{1,15},{8,2},{9,1},{2,10},{3,9},{10,4},{11,3},{4,12},{5,11},... | collective-permute-start | bytes 786440 | tf_op jit(solution)/shard_map/ppermute | solution.py:43
  59.1 1.7 %collective-permute-done.10.refs_1_ = bf16[32,4096]{1,0:T(8,128)(2,1)S(1)} collective-permute-done((bf16[32,4096]{1,0:T(8,128)(2,1)S(1)}, bf16[32,4096]{1,0:T(8,128)(2,1)S(1)}, u32[]{:S(2)}, u32[]{:S(2)}) %collective-permute-start.10) | collective-permute-done | bytes 262176 | tf_op jit(solution)/shard_map/ppermute | solution.py:39
  60.9 2.7 %collective-permute-done.11.refs_2_ = bf16[32,4096]{1,0:T(8,128)(2,1)S(1)} collective-permute-done((bf16[32,4096]{1,0:T(8,128)(2,1)S(1)}, bf16[32,4096]{1,0:T(8,128)(2,1)S(1)}, u32[]{:S(2)}, u32[]{:S(2)}) %collective-permute-start.11) | collective-permute-done | bytes 262176 | tf_op jit(solution)/shard_map/ppermute | solution.py:35
  63.6 1.4 %collective-permute-done.12.refs_3_ = bf16[32,4096]{1,0:T(8,128)(2,1)S(1)} collective-permute-done((bf16[32,4096]{1,0:T(8,128)(2,1)S(1)}, bf16[32,4096]{1,0:T(8,128)(2,1)S(1)}, u32[]{:S(2)}, u32[]{:S(2)}) %collective-permute-start.12) | collective-permute-done | bytes 262176 | tf_op jit(solution)/shard_map/ppermute | solution.py:43
  65.0 1.0 %shard_map.100 = bf16[8,2,4,4096]{3,2,1,0:T(4,128)(2,1)} custom-call(bf16[8,4,4096]{2,1,0:T(4,128)(2,1)S(1)} %shard_map.98.out_total, f32[32,4096]{1,0:T(8,128)S(1)} %get-tuple-element.63.refs_0_, bf16[32,4096]{1,0:T(8,128)(2,1)S(1)} %collective-permute-done.10.refs_1_, bf16[32,4096]{1,0:T(8,128)(2,1)S(1)} %collective-permute-done.11.refs_2_, ...), custom_call_target="tpu_custom_call" | custom-call | tf_op jit(solution)/shard_map/pallas_call | solution.py:64
  66.0 4.1 %all-to-all-start.1 = ((bf16[8,2,4,4096]{3,2,1,0:T(4,128)(2,1)}), bf16[8,2,4,4096]{3,2,1,0:T(4,128)(2,1)S(1)}, u32[]{:S(2)}, u32[]{:S(2)}) async-start(bf16[8,2,4,4096]{3,2,1,0:T(4,128)(2,1)} %shard_map.100), calls=%async_computation.1 | async-start | bytes 1048576 | tf_op jit(solution)/shard_map/all_to_all | solution.py:47
  71.2 3.3 %collective-permute-done.17.refs_11_ = bf16[3,128,256]{2,1,0:T(8,128)(2,1)S(1)} collective-permute-done((bf16[3,128,256]{2,1,0:T(8,128)(2,1)S(1)}, bf16[3,128,256]{2,1,0:T(8,128)(2,1)S(1)}, u32[]{:S(2)}, u32[]{:S(2)}) %collective-permute-start.17) | collective-permute-done | bytes 196640 | tf_op jit(solution)/shard_map/ppermute | solution.py:31
  74.5 4.2 %shard_map.101 = (bf16[1,4096,256]{2,1,0:T(8,128)(2,1)}, bf16[1,4096,256]{2,1,0:T(8,128)(2,1)}, bf16[1,256,4096]{2,1,0:T(8,128)(2,1)}) custom-call(bf16[2,32,4096]{2,1,0:T(8,128)(2,1)S(1)} %shard_map.94.refs_0_, bf16[2,32,4096]{2,1,0:T(8,128)(2,1)S(1)} %collective-permute-done.4.refs_1_, bf16[2,32,4096]{2,1,0:T(8,128)(2,1)S(1)} %collective-permute-done.5.refs_2_, ...), custom_call_target="tpu_custom_call" | custom-call | tf_op jit(solution)/shard_map/pallas_call | solution.py:207
  78.7 4.6 %all-to-all-done.1.arrived = bf16[8,2,4,4096]{3,2,1,0:T(4,128)(2,1)S(1)} async-done(((bf16[8,2,4,4096]{3,2,1,0:T(4,128)(2,1)}), bf16[8,2,4,4096]{3,2,1,0:T(4,128)(2,1)S(1)}, u32[]{:S(2)}, u32[]{:S(2)}) %all-to-all-start.1) | async-done | bytes 524320 | tf_op jit(solution)/shard_map/all_to_all | solution.py:47
  85.0 3.6 %collective-permute-done.18 = bf16[1,4,4096]{2,1,0:T(4,128)(2,1)S(1)} collective-permute-done((bf16[1,4,4096]{2,1,0:T(4,128)(2,1)S(1)}, bf16[1,4,4096]{2,1,0:T(4,128)(2,1)S(1)}, u32[]{:S(2)}, u32[]{:S(2)}) %collective-permute-start.18) | collective-permute-done | bytes 32800 | tf_op jit(solution)/shard_map/ppermute | solution.py:52
  (38 shorter events, 9.1 us)
Async XLA Ops:
  0.6 35.4 %copy-start = (bf16[1,4096,256]{2,1,0:T(8,128)(2,1)S(1)}, bf16[1,4096,256]{2,1,0:T(8,128)(2,1)}, u32[]{:S(2)}) copy-start(bf16[1,4096,256]{2,1,0:T(8,128)(2,1)} %refs_0_) | copy-start | bytes 6291460
  0.6 32.3 %collective-permute-start.1 = (bf16[1,4096,256]{2,1,0:T(8,128)(2,1)}, bf16[1,4096,256]{2,1,0:T(8,128)(2,1)S(1)}, u32[]{:S(2)}, u32[]{:S(2)}) collective-permute-start(bf16[1,4096,256]{2,1,0:T(8,128)(2,1)} %refs_0_), channel_id=1, source_target_pairs={{0,1},{1,0},{8,9},{9,8},{2,3},{3,2},{10,11},{11,10},{4,5},{5,4},{1... | collective-permute-start | bytes 6291464 | tf_op jit(solution)/shard_map/ppermute | solution.py:31
  0.7 32.2 %collective-permute-start.2 = (bf16[1,4096,256]{2,1,0:T(8,128)(2,1)}, bf16[1,4096,256]{2,1,0:T(8,128)(2,1)S(1)}, u32[]{:S(2)}, u32[]{:S(2)}) collective-permute-start(bf16[1,4096,256]{2,1,0:T(8,128)(2,1)} %refs_1_.1), channel_id=1, source_target_pairs={{0,1},{1,0},{8,9},{9,8},{2,3},{3,2},{10,11},{11,10},{4,5},{5,4},{1... | collective-permute-start | bytes 6291464 | tf_op jit(solution)/shard_map/ppermute | solution.py:31
  1.2 31.7 %collective-permute-start.3 = (bf16[1,256,4096]{2,1,0:T(8,128)(2,1)}, bf16[1,256,4096]{2,1,0:T(8,128)(2,1)S(1)}, u32[]{:S(2)}, u32[]{:S(2)}) collective-permute-start(bf16[1,256,4096]{2,1,0:T(8,128)(2,1)} %refs_2_.1), channel_id=1, source_target_pairs={{0,1},{1,0},{8,9},{9,8},{2,3},{3,2},{10,11},{11,10},{4,5},{5,4},{1... | collective-permute-start | bytes 6291464 | tf_op jit(solution)/shard_map/ppermute | solution.py:31
  1.3 4.1 %collective-permute-start = (bf16[4,4096]{1,0:T(4,128)(2,1)}, bf16[4,4096]{1,0:T(4,128)(2,1)S(1)}, u32[]{:S(2)}, u32[]{:S(2)}) collective-permute-start(bf16[4,4096]{1,0:T(4,128)(2,1)} %bitcast.1), channel_id=1, source_target_pairs={{0,64},{64,128},{128,192},{192,0},{1,65},{65,129},{129,193},{193,1... | collective-permute-start | bytes 98312 | tf_op jit(solution)/shard_map/ppermute | solution.py:52
  3.6 0.8 copy-start.3
  33.0 11.8 %collective-permute-start.5 = (bf16[2,32,4096]{2,1,0:T(8,128)(2,1)S(1)}, bf16[2,32,4096]{2,1,0:T(8,128)(2,1)S(1)}, u32[]{:S(2)}, u32[]{:S(2)}) collective-permute-start(bf16[2,32,4096]{2,1,0:T(8,128)(2,1)S(1)} %shard_map.94.refs_0_), channel_id=1, source_target_pairs={{0,48},{1,49},{8,56},{9,57},{2,50},{3,51},{10,58},{11,59},{4,52},{... | collective-permute-start | bytes 1572872 | tf_op jit(solution)/shard_map/ppermute | solution.py:39
  33.5 13.0 %collective-permute-start.4 = (bf16[2,32,4096]{2,1,0:T(8,128)(2,1)S(1)}, bf16[2,32,4096]{2,1,0:T(8,128)(2,1)S(1)}, u32[]{:S(2)}, u32[]{:S(2)}) collective-permute-start(bf16[2,32,4096]{2,1,0:T(8,128)(2,1)S(1)} %shard_map.94.refs_0_), channel_id=1, source_target_pairs={{0,16},{1,17},{8,24},{9,25},{2,18},{3,19},{10,26},{11,27},{4,20},{... | collective-permute-start | bytes 1572872 | tf_op jit(solution)/shard_map/ppermute | solution.py:35
  35.1 11.4 %collective-permute-start.6 = (bf16[2,32,4096]{2,1,0:T(8,128)(2,1)S(1)}, bf16[2,32,4096]{2,1,0:T(8,128)(2,1)S(1)}, u32[]{:S(2)}, u32[]{:S(2)}) collective-permute-start(bf16[2,32,4096]{2,1,0:T(8,128)(2,1)S(1)} %shard_map.94.refs_0_), channel_id=1, source_target_pairs={{0,8},{1,15},{8,2},{9,1},{2,10},{3,9},{10,4},{11,3},{4,12},{5,11},... | collective-permute-start | bytes 1572872 | tf_op jit(solution)/shard_map/ppermute | solution.py:43
  36.1 1.6 %copy-start.1 = (bf16[1,4096,256]{2,1,0:T(8,128)(2,1)S(1)}, bf16[1,4096,256]{2,1,0:T(8,128)(2,1)}, u32[]{:S(2)}) copy-start(bf16[1,4096,256]{2,1,0:T(8,128)(2,1)} %refs_1_.1) | copy-start | bytes 6291460
  37.7 1.6 %copy-start.2 = (bf16[1,256,4096]{2,1,0:T(8,128)(2,1)S(1)}, bf16[1,256,4096]{2,1,0:T(8,128)(2,1)}, u32[]{:S(2)}) copy-start(bf16[1,256,4096]{2,1,0:T(8,128)(2,1)} %refs_2_.1) | copy-start | bytes 6291460
  48.5 9.0 %collective-permute-start.7 = (bf16[32,4096]{1,0:T(8,128)(2,1)S(1)}, bf16[32,4096]{1,0:T(8,128)(2,1)S(1)}, u32[]{:S(2)}, u32[]{:S(2)}) collective-permute-start(bf16[32,4096]{1,0:T(8,128)(2,1)S(1)} %get-tuple-element.57), channel_id=1, source_target_pairs={{0,48},{1,49},{8,56},{9,57},{2,50},{3,51},{10,58},{11,59},{4,52},{... | collective-permute-start | bytes 786440 | tf_op jit(solution)/shard_map/ppermute | solution.py:39
  49.2 9.8 %collective-permute-start.8 = (bf16[32,4096]{1,0:T(8,128)(2,1)S(1)}, bf16[32,4096]{1,0:T(8,128)(2,1)S(1)}, u32[]{:S(2)}, u32[]{:S(2)}) collective-permute-start(bf16[32,4096]{1,0:T(8,128)(2,1)S(1)} %get-tuple-element.58), channel_id=1, source_target_pairs={{0,16},{1,17},{8,24},{9,25},{2,18},{3,19},{10,26},{11,27},{4,20},{... | collective-permute-start | bytes 786440 | tf_op jit(solution)/shard_map/ppermute | solution.py:35
  50.6 8.4 %collective-permute-start.9 = (bf16[32,4096]{1,0:T(8,128)(2,1)S(1)}, bf16[32,4096]{1,0:T(8,128)(2,1)S(1)}, u32[]{:S(2)}, u32[]{:S(2)}) collective-permute-start(bf16[32,4096]{1,0:T(8,128)(2,1)S(1)} %get-tuple-element.59), channel_id=1, source_target_pairs={{0,8},{1,15},{8,2},{9,1},{2,10},{3,9},{10,4},{11,3},{4,12},{5,11},... | collective-permute-start | bytes 786440 | tf_op jit(solution)/shard_map/ppermute | solution.py:43
  54.4 6.4 %collective-permute-start.10 = (bf16[32,4096]{1,0:T(8,128)(2,1)S(1)}, bf16[32,4096]{1,0:T(8,128)(2,1)S(1)}, u32[]{:S(2)}, u32[]{:S(2)}) collective-permute-start(bf16[32,4096]{1,0:T(8,128)(2,1)S(1)} %get-tuple-element.64), channel_id=1, source_target_pairs={{0,48},{1,49},{8,56},{9,57},{2,50},{3,51},{10,58},{11,59},{4,52},{... | collective-permute-start | bytes 786440 | tf_op jit(solution)/shard_map/ppermute | solution.py:39
  56.0 7.6 %collective-permute-start.11 = (bf16[32,4096]{1,0:T(8,128)(2,1)S(1)}, bf16[32,4096]{1,0:T(8,128)(2,1)S(1)}, u32[]{:S(2)}, u32[]{:S(2)}) collective-permute-start(bf16[32,4096]{1,0:T(8,128)(2,1)S(1)} %get-tuple-element.65), channel_id=1, source_target_pairs={{0,16},{1,17},{8,24},{9,25},{2,18},{3,19},{10,26},{11,27},{4,20},{... | collective-permute-start | bytes 786440 | tf_op jit(solution)/shard_map/ppermute | solution.py:35
  57.4 7.6 %collective-permute-start.12 = (bf16[32,4096]{1,0:T(8,128)(2,1)S(1)}, bf16[32,4096]{1,0:T(8,128)(2,1)S(1)}, u32[]{:S(2)}, u32[]{:S(2)}) collective-permute-start(bf16[32,4096]{1,0:T(8,128)(2,1)S(1)} %get-tuple-element.66), channel_id=1, source_target_pairs={{0,8},{1,15},{8,2},{9,1},{2,10},{3,9},{10,4},{11,3},{4,12},{5,11},... | collective-permute-start | bytes 786440 | tf_op jit(solution)/shard_map/ppermute | solution.py:43
  66.0 17.4 %all-to-all-start.1 = ((bf16[8,2,4,4096]{3,2,1,0:T(4,128)(2,1)}), bf16[8,2,4,4096]{3,2,1,0:T(4,128)(2,1)S(1)}, u32[]{:S(2)}, u32[]{:S(2)}) async-start(bf16[8,2,4,4096]{3,2,1,0:T(4,128)(2,1)} %shard_map.100), calls=%async_computation.1 | async-start | bytes 1048576 | tf_op jit(solution)/shard_map/all_to_all | solution.py:47
  70.1 4.4 %collective-permute-start.13 = (bf16[2,32,4096]{2,1,0:T(8,128)(2,1)S(1)}, bf16[2,32,4096]{2,1,0:T(8,128)(2,1)S(1)}, u32[]{:S(2)}, u32[]{:S(2)}) collective-permute-start(bf16[2,32,4096]{2,1,0:T(8,128)(2,1)S(1)} %shard_map.94.refs_0_), channel_id=1, source_target_pairs={{0,1},{1,0},{8,9},{9,8},{2,3},{3,2},{10,11},{11,10},{4,5},{5,4},{1... | collective-permute-start | bytes 1572872 | tf_op jit(solution)/shard_map/ppermute | solution.py:31
  70.1 4.4 %collective-permute-start.14 = (bf16[2,32,4096]{2,1,0:T(8,128)(2,1)S(1)}, bf16[2,32,4096]{2,1,0:T(8,128)(2,1)S(1)}, u32[]{:S(2)}, u32[]{:S(2)}) collective-permute-start(bf16[2,32,4096]{2,1,0:T(8,128)(2,1)S(1)} %collective-permute-done.4.refs_1_), channel_id=1, source_target_pairs={{0,1},{1,0},{8,9},{9,8},{2,3},{3,2},{10,11},{11,10},{4,5},{5,4},{1... | collective-permute-start | bytes 1572872 | tf_op jit(solution)/shard_map/ppermute | solution.py:31
  70.6 3.9 %collective-permute-start.15 = (bf16[2,32,4096]{2,1,0:T(8,128)(2,1)S(1)}, bf16[2,32,4096]{2,1,0:T(8,128)(2,1)S(1)}, u32[]{:S(2)}, u32[]{:S(2)}) collective-permute-start(bf16[2,32,4096]{2,1,0:T(8,128)(2,1)S(1)} %collective-permute-done.5.refs_2_), channel_id=1, source_target_pairs={{0,1},{1,0},{8,9},{9,8},{2,3},{3,2},{10,11},{11,10},{4,5},{5,4},{1... | collective-permute-start | bytes 1572872 | tf_op jit(solution)/shard_map/ppermute | solution.py:31
  70.7 3.9 %collective-permute-start.16 = (bf16[2,32,4096]{2,1,0:T(8,128)(2,1)S(1)}, bf16[2,32,4096]{2,1,0:T(8,128)(2,1)S(1)}, u32[]{:S(2)}, u32[]{:S(2)}) collective-permute-start(bf16[2,32,4096]{2,1,0:T(8,128)(2,1)S(1)} %collective-permute-done.6.refs_3_), channel_id=1, source_target_pairs={{0,1},{1,0},{8,9},{9,8},{2,3},{3,2},{10,11},{11,10},{4,5},{5,4},{1... | collective-permute-start | bytes 1572872 | tf_op jit(solution)/shard_map/ppermute | solution.py:31
  71.1 3.4 %collective-permute-start.17 = (bf16[3,128,256]{2,1,0:T(8,128)(2,1)S(1)}, bf16[3,128,256]{2,1,0:T(8,128)(2,1)S(1)}, u32[]{:S(2)}, u32[]{:S(2)}) collective-permute-start(bf16[3,128,256]{2,1,0:T(8,128)(2,1)S(1)} %get-tuple-element.75), channel_id=1, source_target_pairs={{0,1},{1,0},{8,9},{9,8},{2,3},{3,2},{10,11},{11,10},{4,5},{5,4},{1... | collective-permute-start | bytes 589832 | tf_op jit(solution)/shard_map/ppermute | solution.py:31
  83.4 5.2 %collective-permute-start.18 = (bf16[1,4,4096]{2,1,0:T(4,128)(2,1)S(1)}, bf16[1,4,4096]{2,1,0:T(4,128)(2,1)S(1)}, u32[]{:S(2)}, u32[]{:S(2)}) collective-permute-start(bf16[1,4,4096]{2,1,0:T(4,128)(2,1)S(1)} %shard_map.103), channel_id=1, source_target_pairs={{0,192},{64,0},{128,64},{192,128},{1,193},{65,1},{129,65},{193,129... | collective-permute-start | bytes 98312 | tf_op jit(solution)/shard_map/ppermute | solution.py:52

commit v8 on v7

--- a/solution.py
+++ b/solution.py
@@ -11,7 +11,6 @@
 NY, NZ = 4, 8
 BF16 = jnp.bfloat16
 F32 = jnp.float32
-CHUNK = 4096
 
 
 def place(y, z, core):
@@ -135,30 +134,24 @@
         rise[core] = upper * (sigma * (1.0 + gate * (1.0 - sigma)))
         hiddens[core][...] = (swish[core] * upper).astype(BF16)
 
-    @pl.loop(0, down_ws[0].shape[2], step=CHUNK)
-    def _(start):
-        columns = pl.ds(pl.multiple_of(start, CHUNK), CHUNK)
-        sums = sum(
-            jnp.dot(hiddens[core][...], down_ws[core][0, :, columns], preferred_element_type=F32) for core in (0, 1)
-        )
-        put_sums(sums, columns, *sends)
+    columns = slice(None)
+    sums = sum(
+        jnp.dot(hiddens[core][...], down_ws[core][0, :, columns], preferred_element_type=F32) for core in (0, 1)
+    )
+    put_sums(sums, columns, *sends)
 
 
 def turn_body(gate_w, up_w, gate_x, up_x, down_w, down_x, across, down):
     units = gate_w.shape[2]
     for i, source in enumerate((gate_w, up_w, gate_x, up_x)):
 
-        @pl.loop(0, source.shape[1], step=CHUNK)
-        def _(start):
-            columns = pl.ds(pl.multiple_of(start, CHUNK), CHUNK)
-            across[i * units : (i + 1) * units, columns] = source[0, columns, :].T
+        columns = slice(None)
+        across[i * units : (i + 1) * units, columns] = source[0, columns, :].T
 
     for i, source in enumerate((down_w, down_x)):
 
-        @pl.loop(0, source.shape[2], step=CHUNK)
-        def _(start):
-            columns = pl.ds(pl.multiple_of(start, CHUNK), CHUNK)
-            down[columns, i * units : (i + 1) * units] = source[0, :, columns].T
+        columns = slice(None)
+        down[columns, i * units : (i + 1) * units] = source[0, :, columns].T
 
 
 def backward_body(*refs):
@@ -176,10 +169,8 @@
         grads[:, 2 * core * units : (2 * core + 1) * units] = to_gate[...]
         grads[:, (2 * core + 1) * units : 2 * (core + 1) * units] = to_up[...]
 
-    @pl.loop(0, across.shape[1], step=CHUNK)
-    def _(start):
-        columns = pl.ds(pl.multiple_of(start, CHUNK), CHUNK)
-        put_sums(jnp.dot(grads[...], across[:, columns], preferred_element_type=F32), columns, *sends)
+    columns = slice(None)
+    put_sums(jnp.dot(grads[...], across[:, columns], preferred_element_type=F32), columns, *sends)
 
 
 def weight_grads_body(*refs):
@@ -292,6 +283,7 @@
     (back,) = local_kernel(functools.partial(total_body, 1), [total], arrived)
     returned = from_behind(back, "section", -1)
     (output,) = local_kernel(functools.partial(total_body, 0), [total], arrived)
+    (returned,) = local_kernel(copy_body, [total], returned)
     return (output, returned, grad_gate, grad_up, grad_down)
 
 

time: 89.6 us -> 89.6 us (level)
    pallas_call x10 -> x11, Pallas kernels: 9.31 us -> 9.93 us  [local_kernel(): pl.pallas_call(body, out_shape=[jax.ShapeDtypeStruct(shape, dtype) for sh...]
    unnamed x9 -> x8, local copies, waits for them, and re-layouts: 4.56 us -> 3.94 us
where the time goes in v8:
time: 89.6 us; the launch traced here: 89.2 us
  blocking collectives  27.4 us (31%)
  waiting for transfers between devices  22.8 us (25%)
  starting transfers between devices  19.7 us (22%)
  Pallas kernels  14.6 us (16%)
  local copies, waits for them, and re-layouts  3.94 us (4%)
    all_to_all x1, blocking collectives, colour_all_to_all(): return lax.all_to_all(x, PLANE, 0, 0, axis_index_groups=COLOURS)  27.4 us
    pallas_call x11, Pallas kernels, local_kernel(): pl.pallas_call(body, out_shape=[jax.ShapeDtypeStruct(shape, dtype) for sh...  9.93 us
    ppermute x2, waiting for transfers between devices, from_behind(): lax.ppermute(x, axis, [(i, (i + by) % length) for i in range(length)])  4.8 us
    all_to_all x1, waiting for transfers between devices, colour_all_to_all(): return lax.all_to_all(x, PLANE, 0, 0, axis_index_groups=COLOURS)  4.63 us
    ppermute x3, starting transfers between devices, z_step(): return lax.ppermute(x, PLANE, Z_STEP)  4.41 us
    ppermute x3, waiting for transfers between devices, y_next(): return lax.ppermute(x, PLANE, Y_NEXT)  4.38 us
    ppermute x3, waiting for transfers between devices, y_last(): return lax.ppermute(x, PLANE, Y_LAST)  4.26 us
    pallas_call x1, Pallas kernels, weight_grads(): pl.pallas_call(weight_grads_body, grid=(width // part,), out_shape=[jax.S...  4.2 us
  transfers between devices with their start and end apart: 20, of which 10 were waited for; matrix products, arithmetic and copies ran while one was open for 0% of the time, Pallas kernels for 12%

profile of v8, /device:TPU:6, one launch (start us, length us, event | category | flops | bytes accessed | tf_op | source)
XLA Modules:
  0.0 89.2 jit_solution(13840573622122601058)
XLA Ops:
  1.3 2.2 %collective-permute-start = (bf16[4,4096]{1,0:T(4,128)(2,1)}, bf16[4,4096]{1,0:T(4,128)(2,1)S(1)}, u32[]{:S(2)}, u32[]{:S(2)}) collective-permute-start(bf16[4,4096]{1,0:T(4,128)(2,1)} %bitcast.1), channel_id=1, source_target_pairs={{0,64},{64,128},{128,192},{192,0},{1,65},{65,129},{129,193},{193,1... | collective-permute-start | bytes 98312 | tf_op jit(solution)/shard_map/ppermute | solution.py:51
  4.3 1.2 %collective-permute-done.layer = bf16[4,4096]{1,0:T(4,128)(2,1)S(1)} collective-permute-done((bf16[4,4096]{1,0:T(4,128)(2,1)}, bf16[4,4096]{1,0:T(4,128)(2,1)S(1)}, u32[]{:S(2)}, u32[]{:S(2)}) %collective-permute-start) | collective-permute-done | bytes 32800 | tf_op jit(solution)/shard_map/ppermute | solution.py:51
  5.5 27.4 %all_to_all.10.got_ref = bf16[8,2,4,4096]{3,2,1,0:T(4,128)(2,1)S(1)} all-to-all(bf16[8,2,4,4096]{3,2,1,0:T(4,128)(2,1)S(1)} %shard_map.93), channel_id=1, replica_groups={{0,40,2,42,4,44,6,46},{1,41,3,43,5,45,7,47},{16,56,18,58,20,60,22,62},{..., dimensions={0} | all-to-all | bytes 1048576 | tf_op jit(solution)/shard_map/all_to_all | solution.py:46
  33.5 1.6 %collective-permute-start.4 = (bf16[2,32,4096]{2,1,0:T(8,128)(2,1)S(1)}, bf16[2,32,4096]{2,1,0:T(8,128)(2,1)S(1)}, u32[]{:S(2)}, u32[]{:S(2)}) collective-permute-start(bf16[2,32,4096]{2,1,0:T(8,128)(2,1)S(1)} %shard_map.94.refs_0_), channel_id=1, source_target_pairs={{0,16},{1,17},{8,24},{9,25},{2,18},{3,19},{10,26},{11,27},{4,20},{... | collective-permute-start | bytes 1572872 | tf_op jit(solution)/shard_map/ppermute | solution.py:34
  36.1 1.6 %copy-done.1 = bf16[1,4096,256]{2,1,0:T(8,128)(2,1)S(1)} copy-done((bf16[1,4096,256]{2,1,0:T(8,128)(2,1)S(1)}, bf16[1,4096,256]{2,1,0:T(8,128)(2,1)}, u32[]{:S(2)}) %copy-start.1) | copy-done | bytes 2097176
  37.7 1.6 %copy-done.2 = bf16[1,256,4096]{2,1,0:T(8,128)(2,1)S(1)} copy-done((bf16[1,256,4096]{2,1,0:T(8,128)(2,1)S(1)}, bf16[1,256,4096]{2,1,0:T(8,128)(2,1)}, u32[]{:S(2)}) %copy-start.2) | copy-done | bytes 2097176
  39.7 3.5 %shard_map.96 = (bf16[1024,4096]{1,0:T(8,128)(2,1)S(1)}, bf16[4096,512]{1,0:T(8,128)(2,1)S(1)}) custom-call(bf16[1,4096,256]{2,1,0:T(8,128)(2,1)S(1)} %get-tuple-element.46.gate_w.refs_4_, bf16[1,4096,256]{2,1,0:T(8,128)(2,1)S(1)} %get-tuple-element.47.up_w.refs_6_, bf16[1,4096,256]{2,1,0:T(8,128)(2,1)S(1)} %collective-permute-done.1.gate_x.refs_5_, ...), custom_call_target="tpu_custom_call" | custom-call | tf_op jit(solution)/shard_map/pallas_call | solution.py:63
  43.2 1.6 %collective-permute-done.5.refs_2_ = bf16[2,32,4096]{2,1,0:T(8,128)(2,1)S(1)} collective-permute-done((bf16[2,32,4096]{2,1,0:T(8,128)(2,1)S(1)}, bf16[2,32,4096]{2,1,0:T(8,128)(2,1)S(1)}, u32[]{:S(2)}, u32[]{:S(2)}) %collective-permute-start.5) | collective-permute-done | bytes 524320 | tf_op jit(solution)/shard_map/ppermute | solution.py:38
  44.8 1.7 %collective-permute-done.4.refs_1_ = bf16[2,32,4096]{2,1,0:T(8,128)(2,1)S(1)} collective-permute-done((bf16[2,32,4096]{2,1,0:T(8,128)(2,1)S(1)}, bf16[2,32,4096]{2,1,0:T(8,128)(2,1)S(1)}, u32[]{:S(2)}, u32[]{:S(2)}) %collective-permute-start.4) | collective-permute-done | bytes 524320 | tf_op jit(solution)/shard_map/ppermute | solution.py:34
  46.5 2.0 %shard_map.97 = (bf16[128,256]{1,0:T(8,128)(2,1)S(1)}, bf16[128,256]{1,0:T(8,128)(2,1)S(1)}, f32[2,128,256]{2,1,0:T(8,128)S(1)}, f32[2,128,256]{2,1,0:T(8,128)S(...) custom-call(bf16[2,32,4096]{2,1,0:T(8,128)(2,1)S(1)} %shard_map.94.r, ...), custom_call_target="tpu_custom_call" | custom-call | tf_op jit(solution)/shard_map/pallas_call | solution.py:63
  49.2 1.4 %collective-permute-start.8 = (bf16[32,4096]{1,0:T(8,128)(2,1)S(1)}, bf16[32,4096]{1,0:T(8,128)(2,1)S(1)}, u32[]{:S(2)}, u32[]{:S(2)}) collective-permute-start(bf16[32,4096]{1,0:T(8,128)(2,1)S(1)} %get-tuple-element.58), channel_id=1, source_target_pairs={{0,16},{1,17},{8,24},{9,25},{2,18},{3,19},{10,26},{11,27},{4,20},{... | collective-permute-start | bytes 786440 | tf_op jit(solution)/shard_map/ppermute | solution.py:34
  50.6 1.9 %collective-permute-start.9 = (bf16[32,4096]{1,0:T(8,128)(2,1)S(1)}, bf16[32,4096]{1,0:T(8,128)(2,1)S(1)}, u32[]{:S(2)}, u32[]{:S(2)}) collective-permute-start(bf16[32,4096]{1,0:T(8,128)(2,1)S(1)} %get-tuple-element.59), channel_id=1, source_target_pairs={{0,8},{1,15},{8,2},{9,1},{2,10},{3,9},{10,4},{11,3},{4,12},{5,11},... | collective-permute-start | bytes 786440 | tf_op jit(solution)/shard_map/ppermute | solution.py:42
  52.5 2.0 %shard_map.99 = (bf16[128,256]{1,0:T(8,128)(2,1)S(1)}, bf16[128,256]{1,0:T(8,128)(2,1)S(1)}, bf16[3,128,256]{2,1,0:T(8,128)(2,1)S(1)}, f32[32,4096]{1,0:T(8,128)...) custom-call(bf16[2,32,4096]{2,1,0:T(8,128)(2,1)S(1)} %shard_map.94.refs_0_, ...), custom_call_target="tpu_custom_call" | custom-call | tf_op jit(solution)/shard_map/pallas_call | solution.py:63
  54.4 1.6 %collective-permute-start.10 = (bf16[32,4096]{1,0:T(8,128)(2,1)S(1)}, bf16[32,4096]{1,0:T(8,128)(2,1)S(1)}, u32[]{:S(2)}, u32[]{:S(2)}) collective-permute-start(bf16[32,4096]{1,0:T(8,128)(2,1)S(1)} %get-tuple-element.64), channel_id=1, source_target_pairs={{0,48},{1,49},{8,56},{9,57},{2,50},{3,51},{10,58},{11,59},{4,52},{... | collective-permute-start | bytes 786440 | tf_op jit(solution)/shard_map/ppermute | solution.py:38
  57.4 1.6 %collective-permute-start.12 = (bf16[32,4096]{1,0:T(8,128)(2,1)S(1)}, bf16[32,4096]{1,0:T(8,128)(2,1)S(1)}, u32[]{:S(2)}, u32[]{:S(2)}) collective-permute-start(bf16[32,4096]{1,0:T(8,128)(2,1)S(1)} %get-tuple-element.66), channel_id=1, source_target_pairs={{0,8},{1,15},{8,2},{9,1},{2,10},{3,9},{10,4},{11,3},{4,12},{5,11},... | collective-permute-start | bytes 786440 | tf_op jit(solution)/shard_map/ppermute | solution.py:42
  59.1 1.7 %collective-permute-done.10.refs_1_ = bf16[32,4096]{1,0:T(8,128)(2,1)S(1)} collective-permute-done((bf16[32,4096]{1,0:T(8,128)(2,1)S(1)}, bf16[32,4096]{1,0:T(8,128)(2,1)S(1)}, u32[]{:S(2)}, u32[]{:S(2)}) %collective-permute-start.10) | collective-permute-done | bytes 262176 | tf_op jit(solution)/shard_map/ppermute | solution.py:38
  60.9 2.7 %collective-permute-done.11.refs_2_ = bf16[32,4096]{1,0:T(8,128)(2,1)S(1)} collective-permute-done((bf16[32,4096]{1,0:T(8,128)(2,1)S(1)}, bf16[32,4096]{1,0:T(8,128)(2,1)S(1)}, u32[]{:S(2)}, u32[]{:S(2)}) %collective-permute-start.11) | collective-permute-done | bytes 262176 | tf_op jit(solution)/shard_map/ppermute | solution.py:34
  63.6 1.4 %collective-permute-done.12.refs_3_ = bf16[32,4096]{1,0:T(8,128)(2,1)S(1)} collective-permute-done((bf16[32,4096]{1,0:T(8,128)(2,1)S(1)}, bf16[32,4096]{1,0:T(8,128)(2,1)S(1)}, u32[]{:S(2)}, u32[]{:S(2)}) %collective-permute-start.12) | collective-permute-done | bytes 262176 | tf_op jit(solution)/shard_map/ppermute | solution.py:42
  65.0 1.0 %shard_map.100 = bf16[8,2,4,4096]{3,2,1,0:T(4,128)(2,1)} custom-call(bf16[8,4,4096]{2,1,0:T(4,128)(2,1)S(1)} %shard_map.98.out_total, f32[32,4096]{1,0:T(8,128)S(1)} %get-tuple-element.63.refs_0_, bf16[32,4096]{1,0:T(8,128)(2,1)S(1)} %collective-permute-done.10.refs_1_, bf16[32,4096]{1,0:T(8,128)(2,1)S(1)} %collective-permute-done.11.refs_2_, ...), custom_call_target="tpu_custom_call" | custom-call | tf_op jit(solution)/shard_map/pallas_call | solution.py:63
  66.0 4.1 %all-to-all-start.1 = ((bf16[8,2,4,4096]{3,2,1,0:T(4,128)(2,1)}), bf16[8,2,4,4096]{3,2,1,0:T(4,128)(2,1)S(1)}, u32[]{:S(2)}, u32[]{:S(2)}) async-start(bf16[8,2,4,4096]{3,2,1,0:T(4,128)(2,1)} %shard_map.100), calls=%async_computation.1 | async-start | bytes 1048576 | tf_op jit(solution)/shard_map/all_to_all | solution.py:46
  71.2 3.3 %collective-permute-done.17.refs_11_ = bf16[3,128,256]{2,1,0:T(8,128)(2,1)S(1)} collective-permute-done((bf16[3,128,256]{2,1,0:T(8,128)(2,1)S(1)}, bf16[3,128,256]{2,1,0:T(8,128)(2,1)S(1)}, u32[]{:S(2)}, u32[]{:S(2)}) %collective-permute-start.17) | collective-permute-done | bytes 196640 | tf_op jit(solution)/shard_map/ppermute | solution.py:30
  74.5 4.2 %shard_map.101 = (bf16[1,4096,256]{2,1,0:T(8,128)(2,1)}, bf16[1,4096,256]{2,1,0:T(8,128)(2,1)}, bf16[1,256,4096]{2,1,0:T(8,128)(2,1)}) custom-call(bf16[2,32,4096]{2,1,0:T(8,128)(2,1)S(1)} %shard_map.94.refs_0_, bf16[2,32,4096]{2,1,0:T(8,128)(2,1)S(1)} %collective-permute-done.4.refs_1_, bf16[2,32,4096]{2,1,0:T(8,128)(2,1)S(1)} %collective-permute-done.5.refs_2_, ...), custom_call_target="tpu_custom_call" | custom-call | tf_op jit(solution)/shard_map/pallas_call | solution.py:198
  78.7 4.6 %all-to-all-done.1.arrived = bf16[8,2,4,4096]{3,2,1,0:T(4,128)(2,1)S(1)} async-done(((bf16[8,2,4,4096]{3,2,1,0:T(4,128)(2,1)}), bf16[8,2,4,4096]{3,2,1,0:T(4,128)(2,1)S(1)}, u32[]{:S(2)}, u32[]{:S(2)}) %all-to-all-start.1) | async-done | bytes 524320 | tf_op jit(solution)/shard_map/all_to_all | solution.py:46
  85.0 3.6 %collective-permute-done.18.source = bf16[1,4,4096]{2,1,0:T(4,128)(2,1)S(1)} collective-permute-done((bf16[1,4,4096]{2,1,0:T(4,128)(2,1)S(1)}, bf16[1,4,4096]{2,1,0:T(4,128)(2,1)S(1)}, u32[]{:S(2)}, u32[]{:S(2)}) %collective-permute-start.18) | collective-permute-done | bytes 32800 | tf_op jit(solution)/shard_map/ppermute | solution.py:51
  (38 shorter events, 9.1 us)
Async XLA Ops:
  0.6 35.4 %copy-start = (bf16[1,4096,256]{2,1,0:T(8,128)(2,1)S(1)}, bf16[1,4096,256]{2,1,0:T(8,128)(2,1)}, u32[]{:S(2)}) copy-start(bf16[1,4096,256]{2,1,0:T(8,128)(2,1)} %refs_0_) | copy-start | bytes 6291460
  0.6 32.3 %collective-permute-start.1 = (bf16[1,4096,256]{2,1,0:T(8,128)(2,1)}, bf16[1,4096,256]{2,1,0:T(8,128)(2,1)S(1)}, u32[]{:S(2)}, u32[]{:S(2)}) collective-permute-start(bf16[1,4096,256]{2,1,0:T(8,128)(2,1)} %refs_0_), channel_id=1, source_target_pairs={{0,1},{1,0},{8,9},{9,8},{2,3},{3,2},{10,11},{11,10},{4,5},{5,4},{1... | collective-permute-start | bytes 6291464 | tf_op jit(solution)/shard_map/ppermute | solution.py:30
  0.7 32.2 %collective-permute-start.2 = (bf16[1,4096,256]{2,1,0:T(8,128)(2,1)}, bf16[1,4096,256]{2,1,0:T(8,128)(2,1)S(1)}, u32[]{:S(2)}, u32[]{:S(2)}) collective-permute-start(bf16[1,4096,256]{2,1,0:T(8,128)(2,1)} %refs_1_.1), channel_id=1, source_target_pairs={{0,1},{1,0},{8,9},{9,8},{2,3},{3,2},{10,11},{11,10},{4,5},{5,4},{1... | collective-permute-start | bytes 6291464 | tf_op jit(solution)/shard_map/ppermute | solution.py:30
  1.2 31.7 %collective-permute-start.3 = (bf16[1,256,4096]{2,1,0:T(8,128)(2,1)}, bf16[1,256,4096]{2,1,0:T(8,128)(2,1)S(1)}, u32[]{:S(2)}, u32[]{:S(2)}) collective-permute-start(bf16[1,256,4096]{2,1,0:T(8,128)(2,1)} %refs_2_.1), channel_id=1, source_target_pairs={{0,1},{1,0},{8,9},{9,8},{2,3},{3,2},{10,11},{11,10},{4,5},{5,4},{1... | collective-permute-start | bytes 6291464 | tf_op jit(solution)/shard_map/ppermute | solution.py:30
  1.3 4.1 %collective-permute-start = (bf16[4,4096]{1,0:T(4,128)(2,1)}, bf16[4,4096]{1,0:T(4,128)(2,1)S(1)}, u32[]{:S(2)}, u32[]{:S(2)}) collective-permute-start(bf16[4,4096]{1,0:T(4,128)(2,1)} %bitcast.1), channel_id=1, source_target_pairs={{0,64},{64,128},{128,192},{192,0},{1,65},{65,129},{129,193},{193,1... | collective-permute-start | bytes 98312 | tf_op jit(solution)/shard_map/ppermute | solution.py:51
  3.6 0.8 copy-start.3
  33.0 11.8 %collective-permute-start.5 = (bf16[2,32,4096]{2,1,0:T(8,128)(2,1)S(1)}, bf16[2,32,4096]{2,1,0:T(8,128)(2,1)S(1)}, u32[]{:S(2)}, u32[]{:S(2)}) collective-permute-start(bf16[2,32,4096]{2,1,0:T(8,128)(2,1)S(1)} %shard_map.94.refs_0_), channel_id=1, source_target_pairs={{0,48},{1,49},{8,56},{9,57},{2,50},{3,51},{10,58},{11,59},{4,52},{... | collective-permute-start | bytes 1572872 | tf_op jit(solution)/shard_map/ppermute | solution.py:38
  33.5 13.0 %collective-permute-start.4 = (bf16[2,32,4096]{2,1,0:T(8,128)(2,1)S(1)}, bf16[2,32,4096]{2,1,0:T(8,128)(2,1)S(1)}, u32[]{:S(2)}, u32[]{:S(2)}) collective-permute-start(bf16[2,32,4096]{2,1,0:T(8,128)(2,1)S(1)} %shard_map.94.refs_0_), channel_id=1, source_target_pairs={{0,16},{1,17},{8,24},{9,25},{2,18},{3,19},{10,26},{11,27},{4,20},{... | collective-permute-start | bytes 1572872 | tf_op jit(solution)/shard_map/ppermute | solution.py:34
  35.1 11.4 %collective-permute-start.6 = (bf16[2,32,4096]{2,1,0:T(8,128)(2,1)S(1)}, bf16[2,32,4096]{2,1,0:T(8,128)(2,1)S(1)}, u32[]{:S(2)}, u32[]{:S(2)}) collective-permute-start(bf16[2,32,4096]{2,1,0:T(8,128)(2,1)S(1)} %shard_map.94.refs_0_), channel_id=1, source_target_pairs={{0,8},{1,15},{8,2},{9,1},{2,10},{3,9},{10,4},{11,3},{4,12},{5,11},... | collective-permute-start | bytes 1572872 | tf_op jit(solution)/shard_map/ppermute | solution.py:42
  36.1 1.6 %copy-start.1 = (bf16[1,4096,256]{2,1,0:T(8,128)(2,1)S(1)}, bf16[1,4096,256]{2,1,0:T(8,128)(2,1)}, u32[]{:S(2)}) copy-start(bf16[1,4096,256]{2,1,0:T(8,128)(2,1)} %refs_1_.1) | copy-start | bytes 6291460
  37.7 1.6 %copy-start.2 = (bf16[1,256,4096]{2,1,0:T(8,128)(2,1)S(1)}, bf16[1,256,4096]{2,1,0:T(8,128)(2,1)}, u32[]{:S(2)}) copy-start(bf16[1,256,4096]{2,1,0:T(8,128)(2,1)} %refs_2_.1) | copy-start | bytes 6291460
  48.5 9.0 %collective-permute-start.7 = (bf16[32,4096]{1,0:T(8,128)(2,1)S(1)}, bf16[32,4096]{1,0:T(8,128)(2,1)S(1)}, u32[]{:S(2)}, u32[]{:S(2)}) collective-permute-start(bf16[32,4096]{1,0:T(8,128)(2,1)S(1)} %get-tuple-element.57), channel_id=1, source_target_pairs={{0,48},{1,49},{8,56},{9,57},{2,50},{3,51},{10,58},{11,59},{4,52},{... | collective-permute-start | bytes 786440 | tf_op jit(solution)/shard_map/ppermute | solution.py:38
  49.2 9.8 %collective-permute-start.8 = (bf16[32,4096]{1,0:T(8,128)(2,1)S(1)}, bf16[32,4096]{1,0:T(8,128)(2,1)S(1)}, u32[]{:S(2)}, u32[]{:S(2)}) collective-permute-start(bf16[32,4096]{1,0:T(8,128)(2,1)S(1)} %get-tuple-element.58), channel_id=1, source_target_pairs={{0,16},{1,17},{8,24},{9,25},{2,18},{3,19},{10,26},{11,27},{4,20},{... | collective-permute-start | bytes 786440 | tf_op jit(solution)/shard_map/ppermute | solution.py:34
  50.6 8.4 %collective-permute-start.9 = (bf16[32,4096]{1,0:T(8,128)(2,1)S(1)}, bf16[32,4096]{1,0:T(8,128)(2,1)S(1)}, u32[]{:S(2)}, u32[]{:S(2)}) collective-permute-start(bf16[32,4096]{1,0:T(8,128)(2,1)S(1)} %get-tuple-element.59), channel_id=1, source_target_pairs={{0,8},{1,15},{8,2},{9,1},{2,10},{3,9},{10,4},{11,3},{4,12},{5,11},... | collective-permute-start | bytes 786440 | tf_op jit(solution)/shard_map/ppermute | solution.py:42
  54.4 6.4 %collective-permute-start.10 = (bf16[32,4096]{1,0:T(8,128)(2,1)S(1)}, bf16[32,4096]{1,0:T(8,128)(2,1)S(1)}, u32[]{:S(2)}, u32[]{:S(2)}) collective-permute-start(bf16[32,4096]{1,0:T(8,128)(2,1)S(1)} %get-tuple-element.64), channel_id=1, source_target_pairs={{0,48},{1,49},{8,56},{9,57},{2,50},{3,51},{10,58},{11,59},{4,52},{... | collective-permute-start | bytes 786440 | tf_op jit(solution)/shard_map/ppermute | solution.py:38
  56.0 7.6 %collective-permute-start.11 = (bf16[32,4096]{1,0:T(8,128)(2,1)S(1)}, bf16[32,4096]{1,0:T(8,128)(2,1)S(1)}, u32[]{:S(2)}, u32[]{:S(2)}) collective-permute-start(bf16[32,4096]{1,0:T(8,128)(2,1)S(1)} %get-tuple-element.65), channel_id=1, source_target_pairs={{0,16},{1,17},{8,24},{9,25},{2,18},{3,19},{10,26},{11,27},{4,20},{... | collective-permute-start | bytes 786440 | tf_op jit(solution)/shard_map/ppermute | solution.py:34
  57.4 7.6 %collective-permute-start.12 = (bf16[32,4096]{1,0:T(8,128)(2,1)S(1)}, bf16[32,4096]{1,0:T(8,128)(2,1)S(1)}, u32[]{:S(2)}, u32[]{:S(2)}) collective-permute-start(bf16[32,4096]{1,0:T(8,128)(2,1)S(1)} %get-tuple-element.66), channel_id=1, source_target_pairs={{0,8},{1,15},{8,2},{9,1},{2,10},{3,9},{10,4},{11,3},{4,12},{5,11},... | collective-permute-start | bytes 786440 | tf_op jit(solution)/shard_map/ppermute | solution.py:42
  66.0 17.4 %all-to-all-start.1 = ((bf16[8,2,4,4096]{3,2,1,0:T(4,128)(2,1)}), bf16[8,2,4,4096]{3,2,1,0:T(4,128)(2,1)S(1)}, u32[]{:S(2)}, u32[]{:S(2)}) async-start(bf16[8,2,4,4096]{3,2,1,0:T(4,128)(2,1)} %shard_map.100), calls=%async_computation.1 | async-start | bytes 1048576 | tf_op jit(solution)/shard_map/all_to_all | solution.py:46
  70.1 4.4 %collective-permute-start.13 = (bf16[2,32,4096]{2,1,0:T(8,128)(2,1)S(1)}, bf16[2,32,4096]{2,1,0:T(8,128)(2,1)S(1)}, u32[]{:S(2)}, u32[]{:S(2)}) collective-permute-start(bf16[2,32,4096]{2,1,0:T(8,128)(2,1)S(1)} %shard_map.94.refs_0_), channel_id=1, source_target_pairs={{0,1},{1,0},{8,9},{9,8},{2,3},{3,2},{10,11},{11,10},{4,5},{5,4},{1... | collective-permute-start | bytes 1572872 | tf_op jit(solution)/shard_map/ppermute | solution.py:30
  70.1 4.4 %collective-permute-start.14 = (bf16[2,32,4096]{2,1,0:T(8,128)(2,1)S(1)}, bf16[2,32,4096]{2,1,0:T(8,128)(2,1)S(1)}, u32[]{:S(2)}, u32[]{:S(2)}) collective-permute-start(bf16[2,32,4096]{2,1,0:T(8,128)(2,1)S(1)} %collective-permute-done.4.refs_1_), channel_id=1, source_target_pairs={{0,1},{1,0},{8,9},{9,8},{2,3},{3,2},{10,11},{11,10},{4,5},{5,4},{1... | collective-permute-start | bytes 1572872 | tf_op jit(solution)/shard_map/ppermute | solution.py:30
  70.6 3.9 %collective-permute-start.15 = (bf16[2,32,4096]{2,1,0:T(8,128)(2,1)S(1)}, bf16[2,32,4096]{2,1,0:T(8,128)(2,1)S(1)}, u32[]{:S(2)}, u32[]{:S(2)}) collective-permute-start(bf16[2,32,4096]{2,1,0:T(8,128)(2,1)S(1)} %collective-permute-done.5.refs_2_), channel_id=1, source_target_pairs={{0,1},{1,0},{8,9},{9,8},{2,3},{3,2},{10,11},{11,10},{4,5},{5,4},{1... | collective-permute-start | bytes 1572872 | tf_op jit(solution)/shard_map/ppermute | solution.py:30
  70.7 3.9 %collective-permute-start.16 = (bf16[2,32,4096]{2,1,0:T(8,128)(2,1)S(1)}, bf16[2,32,4096]{2,1,0:T(8,128)(2,1)S(1)}, u32[]{:S(2)}, u32[]{:S(2)}) collective-permute-start(bf16[2,32,4096]{2,1,0:T(8,128)(2,1)S(1)} %collective-permute-done.6.refs_3_), channel_id=1, source_target_pairs={{0,1},{1,0},{8,9},{9,8},{2,3},{3,2},{10,11},{11,10},{4,5},{5,4},{1... | collective-permute-start | bytes 1572872 | tf_op jit(solution)/shard_map/ppermute | solution.py:30
  71.1 3.4 %collective-permute-start.17 = (bf16[3,128,256]{2,1,0:T(8,128)(2,1)S(1)}, bf16[3,128,256]{2,1,0:T(8,128)(2,1)S(1)}, u32[]{:S(2)}, u32[]{:S(2)}) collective-permute-start(bf16[3,128,256]{2,1,0:T(8,128)(2,1)S(1)} %get-tuple-element.75), channel_id=1, source_target_pairs={{0,1},{1,0},{8,9},{9,8},{2,3},{3,2},{10,11},{11,10},{4,5},{5,4},{1... | collective-permute-start | bytes 589832 | tf_op jit(solution)/shard_map/ppermute | solution.py:30
  83.4 5.2 %collective-permute-start.18 = (bf16[1,4,4096]{2,1,0:T(4,128)(2,1)S(1)}, bf16[1,4,4096]{2,1,0:T(4,128)(2,1)S(1)}, u32[]{:S(2)}, u32[]{:S(2)}) collective-permute-start(bf16[1,4,4096]{2,1,0:T(4,128)(2,1)S(1)} %shard_map.103), channel_id=1, source_target_pairs={{0,192},{64,0},{128,64},{192,128},{1,193},{65,1},{129,65},{193,129... | collective-permute-start | bytes 98312 | tf_op jit(solution)/shard_map/ppermute | solution.py:51
